TPU v7x, 32 devices: a whole 2x2x4 slice. The times are simulated.
32 devices in a mesh: dp: 16 (over z, y, x), mp: 2 (over core).
Axes of the slice: x: 2, y: 2, z: 4, core: 2. Of those that a mesh axis runs over, the one named last changes fastest.
Arguments:
- tokens: bfloat16 [65536, 128], P(('dp', 'mp')), may hold values from -6 to 6
- stem_norm: bfloat16 [128], replicated, may hold values from 0.5 to 1.5
- stem_latent: bfloat16 [16, 128], replicated, may hold values from -6 to 6
- stem_wq: bfloat16 [128, 128], P(None, 'mp'), may hold values from -0.5 to 0.5
- stem_wkv: bfloat16 [2, 128, 128], P(None, None, 'mp'), may hold values from -0.5 to 0.5
- stem_wo: bfloat16 [128, 128], P('mp'), may hold values from -2 to 2
- norm_attn: bfloat16 [2, 128], replicated, may hold values from 0.5 to 1.5
- w_qkv: bfloat16 [2, 3, 128, 128], P(None, None, None, 'mp'), may hold values from -0.5 to 0.5
- w_out: bfloat16 [2, 128, 128], P(None, 'mp'), may hold values from -1 to 1
- norm_mlp: bfloat16 [2, 128], replicated, may hold values from 0.5 to 1.5
- w_up: bfloat16 [2, 128, 512], P(None, None, 'mp'), may hold values from -0.5 to 0.5
- b_up: bfloat16 [2, 512], P(None, 'mp'), may hold values from -3 to 3
- w_down: bfloat16 [2, 512, 128], P(None, 'mp'), may hold values from -0.25 to 0.25
- b_down: bfloat16 [2, 128], replicated, may hold values from -2 to 2
- w_act: bfloat16 [128, 128], replicated, may hold values from -0.125 to 0.125
- b_act: bfloat16 [128], replicated, may hold values from -3 to 3
- span_len: int32 [256], P(('dp', 'mp')), may hold values from 4 to 16
- joint_mask: int32 [256, 8], P(('dp', 'mp')), may hold values 0 or 1
- targets: float32 [256, 128], P(('dp', 'mp')), may hold values from -6 to 6
Outputs:
- actions: float32 [256, 128], P(('dp', 'mp'))
- masked_loss: float32 [], replicated
- grad_tokens: float32 [65536, 128], P(('dp', 'mp'))
- grad_stem_norm: float32 [128], replicated
- grad_stem_latent: float32 [16, 128], replicated
- grad_stem_wq: float32 [128, 128], P(None, 'mp')
- grad_stem_wkv: float32 [2, 128, 128], P(None, None, 'mp')
- grad_stem_wo: float32 [128, 128], P('mp')
- grad_norm_attn: float32 [2, 128], replicated
- grad_w_qkv: float32 [2, 3, 128, 128], P(None, None, None, 'mp')
- grad_w_out: float32 [2, 128, 128], P(None, 'mp')
- grad_norm_mlp: float32 [2, 128], replicated
- grad_w_up: float32 [2, 128, 512], P(None, None, 'mp')
- grad_b_up: float32 [2, 512], P(None, 'mp')
- grad_w_down: float32 [2, 512, 128], P(None, 'mp')
- grad_b_down: float32 [2, 128], replicated
- grad_w_act: float32 [128, 128], replicated
- grad_b_act: float32 [128], replicated
All inputs are finite; a program needn't handle non-finite values. No bound on the sum of `joint_mask` on one device may be relied on, other than what follows from the above.
Results may differ from a plain program's by a relative error of at most 0.019.
Values may be sent and summed in bfloat16 or wider, within the bound.
A program may use at most 64 MiB of HBM per device.

v0:
```python
import jax
import jax.numpy as jnp
from jax import lax
from jax.sharding import PartitionSpec as P

HD = 16
LAT = 16
SEQ_LEN = 256
SPAN = 16
JOINTS = 8
AC = 128


epsilon = 1e-05
highest = lax.Precision.HIGHEST


def spread_rows(values_in):
    return lax.all_gather(values_in, "mp", axis=0, tiled=True)


def fold_rows(values_in):
    return lax.psum_scatter(
        values_in.astype(jnp.bfloat16), "mp", scatter_dimension=0, tiled=True
    ).astype(jnp.float32)


def spread_grads(values_in):
    return lax.all_gather(values_in, "mp", axis=0, tiled=True)


def fold_grads(values_in):
    return lax.psum_scatter(
        values_in.astype(jnp.bfloat16), "mp", scatter_dimension=0, tiled=True
    ).astype(jnp.float32)


def low_dot(left, right):
    return jnp.dot(left, right, preferred_element_type=jnp.float32)


def normalize(values_in, gain_vec):
    mean_rows = jnp.mean(values_in, axis=-1, keepdims=True)
    centred = values_in - mean_rows
    variance = jnp.mean(centred * centred, axis=-1, keepdims=True)
    inv_rows = lax.rsqrt(variance + epsilon)
    unit_rows = centred * inv_rows
    return (unit_rows * gain_vec, unit_rows, inv_rows)


def normalize_back(upstream, unit_rows, inv_rows, gain_vec):
    scaled = upstream * gain_vec
    d_gain = jnp.sum(upstream * unit_rows, axis=0)
    inner_term = (
        scaled
        - jnp.mean(scaled, axis=-1, keepdims=True)
        - unit_rows * jnp.mean(scaled * unit_rows, axis=-1, keepdims=True)
    )
    return (inv_rows * inner_term, d_gain)


def attend(queries, key_rows, value_rows):
    scaling = HD ** (-0.5)
    scores = (
        jnp.einsum("bqhe,bkhe->bhqk", queries, key_rows, preferred_element_type=jnp.float32)
        * scaling
    )
    row_max = jnp.max(scores, axis=-1, keepdims=True)
    exp_scores = jnp.exp(scores - row_max)
    row_total = jnp.sum(exp_scores, axis=-1, keepdims=True)
    attn_probs = exp_scores / row_total
    mixed_heads = jnp.einsum(
        "bhqk,bkhe->bqhe",
        attn_probs.astype(jnp.bfloat16),
        value_rows,
        preferred_element_type=jnp.float32,
    )
    return (mixed_heads.astype(jnp.bfloat16), row_max + jnp.log(row_total))


def attend_back(queries, key_rows, value_rows, log_total, d_mixed):
    scaling = HD ** (-0.5)
    scores = (
        jnp.einsum("bqhe,bkhe->bhqk", queries, key_rows, preferred_element_type=jnp.float32)
        * scaling
    )
    attn_probs = jnp.exp(scores - log_total)
    d_probs = jnp.einsum("bqhe,bkhe->bhqk", d_mixed, value_rows, preferred_element_type=jnp.float32)
    d_values = jnp.einsum(
        "bhqk,bqhe->bkhe",
        attn_probs.astype(jnp.bfloat16),
        d_mixed,
        preferred_element_type=jnp.float32,
    )
    inner_term = jnp.sum(attn_probs * d_probs, axis=-1, keepdims=True)
    d_scores = (attn_probs * (d_probs - inner_term)).astype(jnp.bfloat16)
    d_queries = (
        jnp.einsum("bhqk,bkhe->bqhe", d_scores, key_rows, preferred_element_type=jnp.float32)
        * scaling
    )
    d_keys = (
        jnp.einsum("bhqk,bqhe->bkhe", d_scores, queries, preferred_element_type=jnp.float32)
        * scaling
    )
    return (d_queries, d_keys, d_values)


def trunk_forward(residual, weights):
    gain_attn, qkv_mat, out_mat, gain_mlp, up_mat, up_bias, down_mat, down_bias = weights
    normed, unit_a, inv_a = normalize(residual, gain_attn)
    rows_a = spread_rows(normed.astype(jnp.bfloat16))
    local_cols = qkv_mat.shape[2]
    head_shape = (rows_a.shape[0] // LAT, LAT, local_cols // HD, HD)
    queries = low_dot(rows_a, qkv_mat[0]).astype(jnp.bfloat16).reshape(head_shape)
    key_rows = low_dot(rows_a, qkv_mat[1]).astype(jnp.bfloat16).reshape(head_shape)
    value_rows = low_dot(rows_a, qkv_mat[2]).astype(jnp.bfloat16).reshape(head_shape)
    mixed_heads, log_total = attend(queries, key_rows, value_rows)
    mixed_flat = mixed_heads.reshape(rows_a.shape[0], local_cols)
    middle = residual + fold_rows(low_dot(mixed_flat, out_mat))
    normed_m, unit_m, inv_m = normalize(middle, gain_mlp)
    rows_m = spread_rows(normed_m.astype(jnp.bfloat16))
    up_rows = low_dot(rows_m, up_mat) + up_bias
    hidden_act = jax.nn.gelu(up_rows, approximate=False).astype(jnp.bfloat16)
    output = middle + fold_rows(low_dot(hidden_act, down_mat)) + down_bias
    saved_rows = (
        unit_a,
        inv_a,
        rows_a,
        queries,
        key_rows,
        value_rows,
        mixed_flat,
        log_total,
        unit_m,
        inv_m,
        rows_m,
        up_rows,
        hidden_act,
    )
    return (output, saved_rows)


def trunk_back(upstream, saved_rows, weights):
    gain_attn, qkv_mat, out_mat, gain_mlp, up_mat, up_bias, down_mat, down_bias = weights
    (
        unit_a,
        inv_a,
        rows_a,
        queries,
        key_rows,
        value_rows,
        mixed_flat,
        log_total,
        unit_m,
        inv_m,
        rows_m,
        up_rows,
        hidden_act,
    ) = saved_rows
    grad_top = upstream.astype(jnp.bfloat16)
    d_down_bias = jnp.sum(grad_top.astype(jnp.float32), axis=0)
    rows_top = spread_grads(grad_top)
    d_down = low_dot(hidden_act.T, rows_top)
    d_hidden = low_dot(rows_top, down_mat.T)
    d_act = jax.vjp(lambda arg_val: jax.nn.gelu(arg_val, approximate=False), up_rows)[1](d_hidden)[
        0
    ]
    d_upper = d_act.astype(jnp.bfloat16)
    d_up_bias = jnp.sum(d_upper.astype(jnp.float32), axis=0)
    d_up = low_dot(rows_m.T, d_upper)
    d_rows_m = fold_grads(low_dot(d_upper, up_mat.T))
    d_middle, d_gain_mlp = normalize_back(d_rows_m, unit_m, inv_m, gain_mlp)
    d_middle = upstream + d_middle
    grad_attn = d_middle.astype(jnp.bfloat16)
    rows_attn = spread_grads(grad_attn)
    d_out = low_dot(mixed_flat.T, rows_attn)
    d_mixed = low_dot(rows_attn, out_mat.T).astype(jnp.bfloat16).reshape(queries.shape)
    d_queries, d_keys, d_values = attend_back(queries, key_rows, value_rows, log_total, d_mixed)
    flat_shape = mixed_flat.shape
    grad_parts = [
        grad_part.astype(jnp.bfloat16).reshape(flat_shape)
        for grad_part in (d_queries, d_keys, d_values)
    ]
    d_qkv = jnp.stack([low_dot(rows_a.T, grad_part) for grad_part in grad_parts])
    d_rows_term = (
        low_dot(grad_parts[0], qkv_mat[0].T)
        + low_dot(grad_parts[1], qkv_mat[1].T)
        + low_dot(grad_parts[2], qkv_mat[2].T)
    )
    d_rows_a = fold_grads(d_rows_term)
    d_input, d_gain_attn = normalize_back(d_rows_a, unit_a, inv_a, gain_attn)
    return (
        d_middle + d_input,
        (d_qkv, d_out, d_up, d_up_bias, d_down),
        (d_gain_attn, d_gain_mlp, d_down_bias),
    )


def on_device(
    tokens,
    stem_norm,
    stem_latent,
    stem_wq,
    stem_wkv,
    stem_wo,
    norm_attn,
    w_qkv,
    w_out,
    norm_mlp,
    w_up,
    b_up,
    w_down,
    b_down,
    w_act,
    b_act,
    span_len,
    joint_mask,
    targets,
):
    own_seqs = span_len.shape[0]
    model_width = tokens.shape[1]
    layer_count = norm_attn.shape[0]
    total_seqs = own_seqs * lax.axis_size("dp") * lax.axis_size("mp")
    steps_grid = lax.broadcasted_iota(jnp.int32, (SPAN, JOINTS), 0)
    valid_mask = (
        ((steps_grid[None] < span_len[:, None, None]) & (joint_mask[:, None, :] > 0))
        .astype(jnp.float32)
        .reshape(own_seqs, AC)
    )
    entries = lax.psum(jnp.sum(valid_mask), ("dp", "mp"))

    def layer_weights(layer_idx):
        return (
            norm_attn[layer_idx].astype(jnp.float32),
            w_qkv[layer_idx],
            w_out[layer_idx],
            norm_mlp[layer_idx].astype(jnp.float32),
            w_up[layer_idx],
            b_up[layer_idx].astype(jnp.float32),
            w_down[layer_idx],
            b_down[layer_idx].astype(jnp.float32),
        )

    stem_gain = stem_norm.astype(jnp.float32)
    normed_x, unit_x, inv_x = normalize(tokens.astype(jnp.float32), stem_gain)
    rows_x = spread_rows(normed_x.astype(jnp.bfloat16))
    local_cols = stem_wq.shape[1]
    group_seqs = rows_x.shape[0] // SEQ_LEN
    query_small = low_dot(stem_latent, stem_wq).astype(jnp.bfloat16)
    stem_queries = jnp.broadcast_to(
        query_small.reshape(1, LAT, local_cols // HD, HD), (group_seqs, LAT, local_cols // HD, HD)
    )
    key_shape = (group_seqs, SEQ_LEN, local_cols // HD, HD)
    stem_keys = low_dot(rows_x, stem_wkv[0]).astype(jnp.bfloat16).reshape(key_shape)
    stem_values = low_dot(rows_x, stem_wkv[1]).astype(jnp.bfloat16).reshape(key_shape)
    stem_mixed, stem_log = attend(stem_queries, stem_keys, stem_values)
    stem_flat = stem_mixed.reshape(group_seqs * LAT, local_cols)
    latent_full = stem_latent.astype(jnp.float32)
    residual = jnp.tile(latent_full, (own_seqs, 1)) + fold_rows(low_dot(stem_flat, stem_wo))
    layer_inputs = []
    kept_saved = []
    for layer_idx in range(layer_count):
        layer_inputs.append(residual)
        residual, saved_rows = trunk_forward(residual, layer_weights(layer_idx))
        kept_saved.append(None)
    pooled = jnp.sum(residual.reshape(own_seqs, LAT, model_width), axis=1)
    act_mat = w_act.astype(jnp.float32)
    pred = jnp.dot(pooled, act_mat, precision=highest) + b_act.astype(jnp.float32)
    errors = pred - targets
    squares = jnp.sum(valid_mask * errors * errors)
    d_pred = total_seqs * AC / entries * valid_mask * errors
    d_act_mat = jnp.dot(pooled.T, d_pred, precision=highest)
    d_act_bias = jnp.sum(d_pred, axis=0)
    d_pooled = jnp.dot(d_pred, act_mat.T, precision=highest)
    upstream = jnp.broadcast_to(d_pooled[:, None, :], (own_seqs, LAT, model_width)).reshape(
        own_seqs * LAT, model_width
    )
    layer_sums = []
    shared_rows = []
    for layer_idx in reversed(range(layer_count)):
        weights = layer_weights(layer_idx)
        saved_rows = trunk_forward(layer_inputs[layer_idx], weights)[1]
        upstream, layer_part, shared_part = trunk_back(upstream, saved_rows, weights)
        layer_sums.insert(0, layer_part)
        shared_rows.insert(0, shared_part)
    d_latent = jnp.sum(upstream.reshape(own_seqs, LAT, model_width), axis=0)
    grad_stem = upstream.astype(jnp.bfloat16)
    rows_stem = spread_grads(grad_stem)
    d_stem_wo = low_dot(stem_flat.T, rows_stem)
    d_stem_mixed = low_dot(rows_stem, stem_wo.T).astype(jnp.bfloat16).reshape(stem_queries.shape)
    d_queries, d_keys, d_values = attend_back(
        stem_queries, stem_keys, stem_values, stem_log, d_stem_mixed
    )
    d_query_sum = jnp.sum(d_queries, axis=0).reshape(LAT, local_cols)
    d_stem_wq = jnp.dot(latent_full.T, d_query_sum, precision=highest)
    d_latent = d_latent + jnp.dot(d_query_sum, stem_wq.astype(jnp.float32).T, precision=highest)
    key_grads = d_keys.astype(jnp.bfloat16).reshape(rows_x.shape[0], local_cols)
    value_grads = d_values.astype(jnp.bfloat16).reshape(rows_x.shape[0], local_cols)
    d_stem_wkv = jnp.stack([low_dot(rows_x.T, key_grads), low_dot(rows_x.T, value_grads)])
    d_rows_x = fold_grads(low_dot(key_grads, stem_wkv[0].T) + low_dot(value_grads, stem_wkv[1].T))
    grad_tokens, d_stem_gain = normalize_back(d_rows_x, unit_x, inv_x, stem_gain)
    stacked = tuple(
        (jnp.stack([part_row[column] for part_row in layer_sums]) for column in range(5))
    )
    shared_stack = tuple(
        (jnp.stack([part_row[column] for part_row in shared_rows]) for column in range(3))
    )
    shared_items = (
        squares,
        d_stem_gain,
        d_latent,
        shared_stack[0],
        shared_stack[1],
        shared_stack[2],
        d_act_mat,
        d_act_bias,
    )
    pending = (d_stem_wq, d_stem_wkv, d_stem_wo) + stacked
    summed = lax.psum(pending, "dp")
    layer_grads = summed[3:]
    stem_sums = summed[:3]
    shared = lax.psum(
        (
            shared_items[0],
            shared_items[1],
            shared_items[2],
            shared_items[3],
            shared_items[4],
            shared_items[5],
            shared_items[6],
            shared_items[7],
        ),
        ("dp", "mp"),
    )
    return (
        valid_mask * pred,
        shared[0] / entries,
        grad_tokens,
        shared[1],
        shared[2],
        stem_sums[0],
        stem_sums[1],
        stem_sums[2],
        shared[3],
        layer_grads[0],
        layer_grads[1],
        shared[4],
        layer_grads[2],
        layer_grads[3],
        layer_grads[4],
        shared[5],
        shared[6],
        shared[7],
    )


def solution(mesh):
    in_specs = (
        P(("dp", "mp"), None),
        P(),
        P(),
        P(None, "mp"),
        P(None, None, "mp"),
        P("mp", None),
        P(),
        P(None, None, None, "mp"),
        P(None, "mp", None),
        P(),
        P(None, None, "mp"),
        P(None, "mp"),
        P(None, "mp", None),
        P(),
        P(),
        P(),
        P(("dp", "mp")),
        P(("dp", "mp"), None),
        P(("dp", "mp"), None),
    )
    out_specs = (
        P(("dp", "mp"), None),
        P(),
        P(("dp", "mp"), None),
        P(),
        P(),
        P(None, "mp"),
        P(None, None, "mp"),
        P("mp", None),
        P(),
        P(None, None, None, "mp"),
        P(None, "mp", None),
        P(),
        P(None, None, "mp"),
        P(None, "mp"),
        P(None, "mp", None),
        P(),
        P(),
        P(),
    )
    return jax.shard_map(
        on_device, mesh=mesh, in_specs=in_specs, out_specs=out_specs, check_vma=False
    )
```

profile of v0, /device:TPU:0, one launch (start us, length us, event | category | flops | bytes accessed | tf_op | source)
XLA Modules:
  0.0 638.8 jit_solution(5279137691413765930)
XLA Ops:
  10.9 2.4 fusion.27
  14.3 11.0 %all-gather.2.cloned.1.call-done = bf16[4096,128]{1,0:T(8,128)(2,1)} async-done(((bf16[2048,128]{1,0:T(8,128)(2,1)}), bf16[4096,128]{1,0:T(8,128)(2,1)}) %all-gather.2.cloned.1.call-update) | async-done | bytes 1048592 | tf_op jit(solution)/shard_map/all_gather | solution.py:19
  31.3 8.2 %reduce-scatter.11.cloned.1.call-done = bf16[128,128]{1,0:T(8,128)(2,1)} async-done(((bf16[256,128]{1,0:T(8,128)(2,1)}), bf16[128,128]{1,0:T(8,128)(2,1)}) %reduce-scatter.11.cloned.1.call-update) | async-done | bytes 32784 | tf_op jit(solution)/shard_map/reduce_scatter | solution.py:23
  42.7 1.9 all_gather.35
  52.1 8.2 %reduce-scatter.13.cloned.1.call-done = bf16[128,128]{1,0:T(8,128)(2,1)} async-done(((bf16[256,128]{1,0:T(8,128)(2,1)}), bf16[128,128]{1,0:T(8,128)(2,1)}) %reduce-scatter.13.cloned.1.call-update) | async-done | bytes 32784 | tf_op jit(solution)/shard_map/reduce_scatter | solution.py:23
  63.0 1.9 all_gather.36
  64.9 2.4 multiply_convert_fusion.4
  68.7 8.2 %reduce-scatter.15.cloned.1.call-done = bf16[128,128]{1,0:T(8,128)(2,1)} async-done(((bf16[256,128]{1,0:T(8,128)(2,1)}), bf16[128,128]{1,0:T(8,128)(2,1)}) %reduce-scatter.15.cloned.1.call-update) | async-done | bytes 32784 | tf_op jit(solution)/shard_map/reduce_scatter | solution.py:23
  78.1 1.9 all_gather.37
  89.4 8.7 %reduce-scatter.17.cloned.1.call-done = bf16[128,128]{1,0:T(8,128)(2,1)} async-done(((bf16[256,128]{1,0:T(8,128)(2,1)}), bf16[128,128]{1,0:T(8,128)(2,1)}) %reduce-scatter.17.cloned.1.call-update) | async-done | bytes 32784 | tf_op jit(solution)/shard_map/reduce_scatter | solution.py:23
  100.0 1.9 all_gather.38
  101.9 2.4 multiply_convert_fusion.3
  106.6 40.9 %psum.120 = f32[]{:T(128)} all-reduce(f32[]{:T(128)} %convert_reduce_fusion.4), channel_id=1, replica_groups=mesh['dp'=16,'mp'=2] {'dp','mp'}, use_global_device_ids=true, to_apply=%region_25.0 | all-reduce | flops 1 | bytes 8 | tf_op jit(solution)/shard_map/psum | solution.py:230
  149.7 2.1 fusion.179
  152.6 1.9 all_gather.39
  155.1 1.9 convert_reduce_fusion.1
  160.2 6.8 %reduce-scatter.21.cloned.1.call-done = bf16[128,128]{1,0:T(8,128)(2,1)} async-done(((bf16[256,128]{1,0:T(8,128)(2,1)}), bf16[128,128]{1,0:T(8,128)(2,1)}) %reduce-scatter.21.cloned.1.call-update) | async-done | bytes 32784 | tf_op jit(solution)/shard_map/reduce_scatter | solution.py:33
  169.9 1.9 all_gather.40
  189.2 8.7 %reduce-scatter.23.cloned.1.call-done = bf16[128,128]{1,0:T(8,128)(2,1)} async-done(((bf16[256,128]{1,0:T(8,128)(2,1)}), bf16[128,128]{1,0:T(8,128)(2,1)}) %reduce-scatter.23.cloned.1.call-update) | async-done | bytes 32784 | tf_op jit(solution)/shard_map/reduce_scatter | solution.py:33
  201.0 1.8 all_gather.41
  202.8 1.9 convert_reduce_fusion.2
  207.3 7.9 %reduce-scatter.25.cloned.1.call-done = bf16[128,128]{1,0:T(8,128)(2,1)} async-done(((bf16[256,128]{1,0:T(8,128)(2,1)}), bf16[128,128]{1,0:T(8,128)(2,1)}) %reduce-scatter.25.cloned.1.call-update) | async-done | bytes 32784 | tf_op jit(solution)/shard_map/reduce_scatter | solution.py:33
  218.2 1.8 all_gather.42
  228.7 8.7 %reduce-scatter.27.cloned.1.call-done = bf16[128,128]{1,0:T(8,128)(2,1)} async-done(((bf16[256,128]{1,0:T(8,128)(2,1)}), bf16[128,128]{1,0:T(8,128)(2,1)}) %reduce-scatter.27.cloned.1.call-update) | async-done | bytes 32784 | tf_op jit(solution)/shard_map/reduce_scatter | solution.py:33
  240.5 2.1 all_gather.43
  250.0 1.8 convolution_bitcast_fusion.2
  273.5 2.2 fusion.32
  275.7 40.7 %all-reduce = (f32[]{:T(128)}, f32[128]{0:T(128)}, f32[16,128]{1,0:T(8,128)}, f32[2,128]{1,0:T(2,128)}, f32[2,128]{1,0:T(2,128)}, /*index=5*/f32[2,128]{1,0:T(2,128)}, f32[128]{0:T(128)}) all-reduce(f32[]{:T(128)} %get-tuple-element.34, f32[128]{0:T(128)S(1)} %get-tuple-element.18, ...), channel_id=1, replica_groups=mesh['dp'=16,'mp'=2] {'dp','mp'}, use_global_device_ids=true, to_apply=%region_23.0 | all-reduce | flops 3073 | bytes 24584 | tf_op jit(solution)/shard_map/psum | solution.py:322
  317.8 3.8 fusion.29
  321.6 61.8 %all-reduce.7.cloned.1.call-done = f32[128,128]{1,0:T(8,128)} async-done(((f32[128,128]{1,0:T(8,128)}), f32[128,128]{1,0:T(8,128)}) %all-reduce.7.cloned.1.call-update) | async-done | bytes 65552 | tf_op jit(solution)/shard_map/psum | solution.py:322
  383.4 113.8 %all-reduce.9.cloned.1.call-done = (f32[128,64]{0,1:T(8,128)}, f32[64,128]{1,0:T(8,128)}, f32[2,256]{1,0:T(2,128)}) async-done(((f32[128,64]{0,1:T(8,128)}, f32[64,128]{1,0:T(8,128)}, f32[2,256]{1,0:T(2,128)}), (f32[128,64]{0,1:T(8,128)}, f32[64,128]{1,0:T(8,128)}, f32[2,256]{1,0:T(2,128)})) %all-reduce.9.cloned.1.call-update) | async-done | bytes 67600 | tf_op jit(solution)/shard_map/psum | solution.py:319
  497.2 120.6 %all-reduce.11.cloned.1.call-done = (f32[2,128,64]{1,2,0:T(8,128)}, f32[2,3,128,64]{2,3,1,0:T(8,128)}, f32[2,64,128]{2,1,0:T(8,128)}, f32[2,128,256]{2,1,0:T(8,128)}, f32[2,256,128]{2,1,0:T(8,128)}) async-done(((f32[2,128,64]{1,2,0:T(8,128)}, f32[2,3,128,64]{2,3,1,0:T(8,128)}, f32[2,64,128]{2,1,0:T(8,128)}, f32[2,128,256]{2,1,0:T(8,128)}, f32[2,256,128]{2,1,0:T(8,128)}), (f32[2,128,64]{1,2,0:T(8,128)}, ...) | async-done | bytes 851984 | tf_op jit(solution)/shard_map/psum | solution.py:319
  (417 shorter events, 128.1 us)
Async XLA Ops:
  7.2 142.5 %copy-start = (bf16[128,128]{1,0:T(8,128)(2,1)S(1)}, bf16[128,128]{1,0:T(8,128)(2,1)}, u32[]{:S(2)}) copy-start(bf16[128,128]{1,0:T(8,128)(2,1)} %param.33) | copy-start | bytes 98308
  7.2 18.1 %copy-start.48 = (bf16[2,128,64]{1,2,0:T(8,128)(2,1)S(1)}, bf16[2,128,64]{1,2,0:T(8,128)(2,1)}, u32[]{:S(2)}) copy-start(bf16[2,128,64]{1,2,0:T(8,128)(2,1)} %param.23) | copy-start | bytes 98308
  7.3 18.0 %all-gather.2.cloned.1.call-start = ((), (), s32[]{:S(2)}) async-start(), calls=%async_computation.10 | async-start | bytes 1572864 | tf_op jit(solution)/shard_map/all_gather | solution.py:19
  8.0 19.1 %copy-start.80 = (f32[128]{0:T(128)}, f32[128]{0:T(128)S(1)}, u32[]{:S(2)}) copy-start(f32[128]{0:T(128)S(1)} %convert_element_type.312) | copy-start | bytes 1540
  10.9 16.3 %copy-start.50 = (f32[2048]{0:T(1024)}, f32[2048]{0:T(1024)S(1)}, u32[]{:S(2)}) copy-start(f32[2048]{0:T(1024)S(1)} %add_rsqrt_fusion) | copy-start | bytes 24580
  13.4 26.1 %reduce-scatter.11.cloned.1.call-start = ((), (), s32[]{:S(2)}) async-start(), calls=%async_computation.11 | async-start | bytes 98304 | tf_op jit(solution)/shard_map/reduce_scatter | solution.py:23
  28.8 15.8 %copy-start.23 = (bf16[2,3,128,64]{2,3,1,0:T(8,128)(2,1)S(1)}, bf16[2,3,128,64]{2,3,1,0:T(8,128)(2,1)}, u32[]{:S(2)}) copy-start(bf16[2,3,128,64]{2,3,1,0:T(8,128)(2,1)} %param.26) | copy-start | bytes 294916
  30.7 29.6 %reduce-scatter.13.cloned.1.call-start = ((), (), s32[]{:S(2)}) async-start(), calls=%async_computation.12 | async-start | bytes 98304 | tf_op jit(solution)/shard_map/reduce_scatter | solution.py:23
  47.0 17.8 %copy-start.26 = (f32[16,4,16]{2,1,0:T(4,128)}, f32[16,4,16]{2,1,0:T(4,128)S(1)}, u32[]{:S(2)}) copy-start(f32[16,4,16]{2,1,0:T(4,128)S(1)} %get-tuple-element.77) | copy-start | bytes 12292
  47.1 17.8 %copy-start.95 = (f32[1,256]{1,0:T(1,128)S(1)}, f32[1,256]{1,0:T(1,128)}, u32[]{:S(2)}) copy-start(f32[1,256]{1,0:T(1,128)} %get-tuple-element.68) | copy-start | bytes 3076
  51.5 25.4 %reduce-scatter.15.cloned.1.call-start = ((), (), s32[]{:S(2)}) async-start(), calls=%async_computation.13 | async-start | bytes 98304 | tf_op jit(solution)/shard_map/reduce_scatter | solution.py:23
  68.1 30.0 %reduce-scatter.17.cloned.1.call-start = ((), (), s32[]{:S(2)}) async-start(), calls=%async_computation.14 | async-start | bytes 98304 | tf_op jit(solution)/shard_map/reduce_scatter | solution.py:23
  89.4 59.5 %reduce-scatter.19.cloned.1.call-start = ((), (), s32[]{:S(2)}) async-start(), calls=%async_computation.15 | async-start | bytes 98304 | tf_op jit(solution)/shard_map/reduce_scatter | solution.py:23
  101.9 45.6 %copy-start.98 = (bf16[128]{0:T(256)(128)(2,1)S(1)}, bf16[128]{0:T(256)(128)(2,1)}, u32[]{:S(2)}) copy-start(bf16[128]{0:T(256)(128)(2,1)} %param.34) | copy-start | bytes 772
  101.9 47.0 %copy-start.91 = (f32[128]{0:T(128)S(1)}, f32[128]{0:T(128)}, u32[]{:S(2)}) copy-start(f32[128]{0:T(128)} %get-tuple-element.69) | copy-start | bytes 1540
  105.8 61.1 %reduce-scatter.21.cloned.1.call-start = ((), (), s32[]{:S(2)}) async-start(), calls=%async_computation.16 | async-start | bytes 98304 | tf_op jit(solution)/shard_map/reduce_scatter | solution.py:33
  159.3 38.6 %reduce-scatter.23.cloned.1.call-start = ((), (), s32[]{:S(2)}) async-start(), calls=%async_computation.17 | async-start | bytes 98304 | tf_op jit(solution)/shard_map/reduce_scatter | solution.py:33
  181.7 24.8 %copy-start.27 = (f32[16,4,16]{2,1,0:T(4,128)S(1)}, f32[16,4,16]{2,1,0:T(4,128)}, u32[]{:S(2)}) copy-start(f32[16,4,16]{2,1,0:T(4,128)} %copy-done.26) | copy-start | bytes 12292
  189.1 30.9 %copy-start.54 = (bf16[2,64,128]{2,1,0:T(8,128)(2,1)S(1)}, bf16[2,64,128]{2,1,0:T(8,128)(2,1)}, u32[]{:S(2)}) copy-start(bf16[2,64,128]{2,1,0:T(8,128)(2,1)} %param.27) | copy-start | bytes 98308
  189.1 31.6 %copy-start.15 = (bf16[16,16,4,16]{3,1,2,0:T(8,128)(2,1)S(1)}, bf16[16,16,4,16]{3,1,2,0:T(8,128)(2,1)}, u32[]{:S(2)}) copy-start(bf16[16,16,4,16]{3,1,2,0:T(8,128)(2,1)} %copy.248) | copy-start | bytes 98308
  189.2 26.0 %reduce-scatter.25.cloned.1.call-start = ((), (), s32[]{:S(2)}) async-start(), calls=%async_computation.18 | async-start | bytes 98304 | tf_op jit(solution)/shard_map/reduce_scatter | solution.py:33
  202.8 17.2 %copy-start.44 = (bf16[256,128]{1,0:T(8,128)(2,1)}, bf16[256,128]{1,0:T(8,128)(2,1)S(1)}, u32[]{:S(2)}) copy-start(bf16[256,128]{1,0:T(8,128)(2,1)S(1)} %all_gather.41) | copy-start | bytes 196612
  206.5 30.9 %reduce-scatter.27.cloned.1.call-start = ((), (), s32[]{:S(2)}) async-start(), calls=%async_computation.19 | async-start | bytes 98304 | tf_op jit(solution)/shard_map/reduce_scatter | solution.py:33
  223.0 17.5 %copy-start.38 = (bf16[256,64]{0,1:T(8,128)(2,1)}, bf16[256,64]{0,1:T(8,128)(2,1)S(1)}, u32[]{:S(2)}) copy-start(bf16[256,64]{0,1:T(8,128)(2,1)S(1)} %reshape.309) | copy-start | bytes 98308
  223.0 21.1 %copy-start.13 = (bf16[8,8,16,256]{3,2,1,0:T(8,128)(2,1)S(1)}, bf16[8,8,16,256]{3,2,1,0:T(8,128)(2,1)}, u32[]{:S(2)}) copy-start(bf16[8,8,16,256]{3,2,1,0:T(8,128)(2,1)} %copy-done.12) | copy-start | bytes 1572868
  225.2 15.4 %copy-start.36 = (bf16[256,64]{0,1:T(8,128)(2,1)}, bf16[256,64]{0,1:T(8,128)(2,1)S(1)}, u32[]{:S(2)}) copy-start(bf16[256,64]{0,1:T(8,128)(2,1)S(1)} %reshape.310) | copy-start | bytes 98308
  228.6 44.8 %reduce-scatter.29.cloned.1.call-start = ((), (), s32[]{:S(2)}) async-start(), calls=%async_computation.20 | async-start | bytes 1572864 | tf_op jit(solution)/shard_map/reduce_scatter | solution.py:33
  248.5 134.9 %all-reduce.7.cloned.1.call-start = ((), (), s32[]{:S(2)}) async-start(), calls=%async_computation.21 | async-start | bytes 131072 | tf_op jit(solution)/shard_map/psum | solution.py:322
  250.0 18.6 %copy-start.30 = (bf16[256,64]{0,1:T(8,128)(2,1)S(1)}, bf16[256,64]{0,1:T(8,128)(2,1)}, u32[]{:S(2)}) copy-start(bf16[256,64]{0,1:T(8,128)(2,1)} %copy-done.29) | copy-start | bytes 98308
  250.0 19.4 %copy-start.11 = (bf16[8,8,16,256]{3,2,1,0:T(8,128)(2,1)S(1)}, bf16[8,8,16,256]{3,2,1,0:T(8,128)(2,1)}, u32[]{:S(2)}) copy-start(bf16[8,8,16,256]{3,2,1,0:T(8,128)(2,1)} %copy-done.10) | copy-start | bytes 1572868
  254.7 242.4 %all-reduce.9.cloned.1.call-start = ((), (), s32[]{:S(2)}) async-start(), calls=%async_computation.22 | async-start | bytes 135168 | tf_op jit(solution)/shard_map/psum | solution.py:319
  272.8 345.0 %all-reduce.11.cloned.1.call-start = ((), (), s32[]{:S(2)}) async-start(), calls=%async_computation.23 | async-start | bytes 1703936 | tf_op jit(solution)/shard_map/psum | solution.py:319
  (81 other events, 366.3 us)
Sparse Core Ops, SparseCore 0:
  13.5 11.7 all-gather.1
  30.8 8.6 reduce-scatter.10
  51.6 8.5 reduce-scatter.12
  68.3 8.6 reduce-scatter.14
  89.5 8.5 reduce-scatter.16
  105.9 8.6 reduce-scatter.18
  159.5 7.4 reduce-scatter.20
  189.3 8.5 reduce-scatter.22
  206.6 8.5 reduce-scatter.24
  228.7 8.6 reduce-scatter.26
  248.6 9.6 reduce-scatter.28
  264.7 118.6 all-reduce.6
  391.4 105.6 all-reduce.8
  505.3 112.4 all-reduce.10
where the time goes:
time: 643 us; the launch traced here: 639 us
  waiting for transfers between devices  373 us (58%)
  blocking collectives  98.5 us (15%)
  matrix products  58.3 us (9%)
  other arithmetic  48.8 us (8%)
  local copies, waits for them, and re-layouts  40.7 us (6%)
  between operations  18.7 us (3%)
    psum x2, waiting for transfers between devices, on_device(): summed = lax.psum(pending, 'dp')  234 us
    psum x1, waiting for transfers between devices, on_device(): lax.psum((shared_items[0], shared_items[1], shared_items[2], shared_items...  61.8 us
    dot_general x46, matrix products, low_dot(): return jnp.dot(left, right, preferred_element_type=jnp.float32)  41 us
    psum x1, blocking collectives, on_device(): entries = lax.psum(jnp.sum(valid_mask), ('dp', 'mp'))  40.9 us
    psum x1, blocking collectives, on_device(): lax.psum((shared_items[0], shared_items[1], shared_items[2], shared_items...  40.7 us
    reduce_scatter x5, waiting for transfers between devices, fold_rows(): lax.psum_scatter(values_in.astype(jnp.bfloat16), 'mp', scatter_dimension=...  33.3 us
    reduce_scatter x5, waiting for transfers between devices, fold_grads(): lax.psum_scatter(values_in.astype(jnp.bfloat16), 'mp', scatter_dimension=...  32.1 us
    unnamed x211, local copies, waits for them, and re-layouts  18.4 us
  transfers between devices with their start and end apart: 14, of which 12 were waited for; matrix products, arithmetic and copies ran while one was open for 6% of the time, Pallas kernels for 0%

commit v1 on v0

v1 whole, which is shorter than its diff:
```python
import functools

import jax
import jax.numpy as jnp
from jax import lax
from jax.experimental import pallas as pl
from jax.experimental.pallas import tpu as pltpu
from jax.sharding import PartitionSpec as P

HD = 16
LAT = 16
SEQ_LEN = 256
SPAN = 16
JOINTS = 8
HEADS = 8
D = 128
FF = 512
AC = 128
LAYERS = 2

F32 = jnp.float32
BF = jnp.bfloat16
MESH = pl.DeviceIdType.MESH
epsilon = 1e-05
highest = lax.Precision.HIGHEST

CHUNKS = (640, 256, 512, 384)
TAIL = 112


def nn(left, right):
    return jnp.dot(left, right, preferred_element_type=F32)


def nt(left, right):
    return lax.dot_general(left, right, (((1,), (1,)), ((), ())), preferred_element_type=F32)


def tn(left, right):
    return lax.dot_general(left, right, (((0,), (0,)), ((), ())), preferred_element_type=F32)


def iota(shape, axis):
    return lax.broadcasted_iota(jnp.int32, shape, axis)


def radices_of(count):
    found = []
    while count > 1:
        radix = 4 if count % 4 == 0 else 2
        found.append(radix)
        count //= radix
    return found


def flip(digit, offset):
    if offset == 1:
        return digit + 1 - 2 * (digit % 2)
    if offset == 2:
        return (digit + 2) % 4
    return 3 - digit


def norm_rows(values_in, gain_vec):
    mean_rows = jnp.mean(values_in, axis=-1, keepdims=True)
    centred = values_in - mean_rows
    variance = jnp.mean(centred * centred, axis=-1, keepdims=True)
    inv_rows = lax.rsqrt(variance + epsilon)
    unit_rows = centred * inv_rows
    return unit_rows * gain_vec, unit_rows, inv_rows


def norm_back(upstream, unit_rows, inv_rows, gain_vec):
    scaled = upstream * gain_vec
    inner = (
        scaled
        - jnp.mean(scaled, axis=-1, keepdims=True)
        - unit_rows * jnp.mean(scaled * unit_rows, axis=-1, keepdims=True)
    )
    return inv_rows * inner


def split_rows(values_in):
    first = values_in.astype(BF).astype(F32)
    rest = values_in - first
    second = rest.astype(BF).astype(F32)
    return jnp.concatenate([first, second, rest - second], axis=0).astype(BF)


def main_kernel(
    radices,
    tokens_h,
    stem_norm_h,
    stem_latent_h,
    stem_wq_h,
    stem_wkv_h,
    stem_wo_h,
    norm_attn_h,
    w_qkv_h,
    w_out_h,
    norm_mlp_h,
    w_up_h,
    b_up_h,
    w_down_h,
    b_down_h,
    w_act_h,
    b_act_h,
    span_len_h,
    joint_mask_h,
    targets_h,
    grad_tokens,
    fin_a,
    fin_b,
    fin_c,
    fin_d,
    tail_out,
    wq_out,
    head_out,
    x_v,
    stem_norm_v,
    stem_latent_v,
    wq_v,
    wkv_v,
    wo_v,
    norm_attn_v,
    wqkv_v,
    wout_v,
    norm_mlp_v,
    wup_v,
    bup_v,
    wdn_v,
    b_down_v,
    w_act_v,
    b_act_v,
    span_s,
    joint_v,
    targets_v,
    next_v,
    unit_v,
    inv_v,
    e_v,
    ds_v,
    small_v,
    ent_v,
    ent_r,
    own,
    oth,
    rcv,
    snd,
    rs_r,
    part,
    full_r,
    tail_s,
    tail_r,
    in_sem,
    send_sem,
    recv_sem,
):
    dp, mp = lax.axis_index("dp"), lax.axis_index("mp")
    own_seqs = targets_h.shape[0]
    rows = own_seqs * LAT
    fins = (fin_a, fin_b, fin_c, fin_d)
    core = (dp, 1 - mp)
    strides, digits = [], []
    stride = 1
    for radix in radices:
        strides.append(stride)
        digits.append((dp // stride) % radix)
        stride *= radix

    def partner(level, offset):
        digit = digits[level]
        return (dp + (flip(digit, offset) - digit) * strides[level], mp)

    barrier = pltpu.get_barrier_semaphore()
    greeted = [core]
    for level, radix in enumerate(radices):
        greeted += [partner(level, offset) for offset in range(1, radix)]
    for device in greeted:
        pl.semaphore_signal(barrier, inc=1, device_id=device, device_id_type=MESH)

    slots = [0]
    sends = []

    def remote(src, dst, device):
        slot = slots[0]
        slots[0] += 1
        copy = pltpu.make_async_remote_copy(
            src_ref=src,
            dst_ref=dst,
            send_sem=send_sem.at[slot],
            recv_sem=recv_sem.at[slot],
            device_id=device,
            device_id_type=MESH,
        )
        copy.start()
        sends.append(copy)
        return copy

    local = {}
    pairs = (
        ("tokens", tokens_h, x_v),
        ("stem_norm", stem_norm_h, stem_norm_v),
        ("stem_latent", stem_latent_h, stem_latent_v),
        ("wq", stem_wq_h, wq_v.at[0]),
        ("wkv", stem_wkv_h, wkv_v.at[0]),
        ("wo", stem_wo_h, wo_v.at[0]),
        ("wqkv", w_qkv_h, wqkv_v.at[0]),
        ("wout", w_out_h, wout_v.at[0]),
        ("wup", w_up_h, wup_v.at[0]),
        ("wdn", w_down_h, wdn_v.at[0]),
        ("norm_attn", norm_attn_h, norm_attn_v),
        ("norm_mlp", norm_mlp_h, norm_mlp_v),
        ("bup", b_up_h, bup_v.at[0]),
        ("b_down", b_down_h, b_down_v),
        ("w_act", w_act_h, w_act_v),
        ("b_act", b_act_h, b_act_v),
        ("span", span_len_h, span_s),
        ("joint", joint_mask_h, joint_v),
        ("targets", targets_h, targets_v),
    )
    for place, (name, src, dst) in enumerate(pairs):
        local[name] = pltpu.make_async_copy(src, dst, in_sem.at[place])
        local[name].start()

    head_mask = (
        (iota((HEADS, D, D), 2) // HD == iota((HEADS, D, D), 0)).astype(F32).astype(BF)
    )
    row_mask = (iota((HEADS, D, D), 1) // HD == iota((HEADS, D, D), 0)).astype(F32).astype(BF)
    diag_heads = (iota((D, D), 0) // LAT == iota((D, D), 1) // HD).astype(F32)
    block_add = jnp.where(iota((rows, rows), 0) // LAT == iota((rows, rows), 1) // LAT, 0.0, -1e30)
    mean_mat = jnp.full((D, D), 1.0 / D, BF)
    mean_twice = jnp.full((2 * D, D), 1.0 / D, BF)

    pl.semaphore_wait(barrier, len(greeted))
    gathered = {}
    for name, src, dst in (
        ("wq", stem_wq_h, wq_v.at[1]),
        ("wkv", stem_wkv_h, wkv_v.at[1]),
        ("wo", stem_wo_h, wo_v.at[1]),
        ("wqkv", w_qkv_h, wqkv_v.at[1]),
        ("wout", w_out_h, wout_v.at[1]),
        ("wup", w_up_h, wup_v.at[1]),
        ("wdn", w_down_h, wdn_v.at[1]),
        ("bup", b_up_h, bup_v.at[1]),
    ):
        gathered[name] = remote(src, dst, core)

    local["span"].wait()
    local["joint"].wait()
    spans = jnp.zeros((own_seqs, AC), jnp.int32)
    for seq in range(own_seqs):
        spans = jnp.where(iota((own_seqs, AC), 0) == seq, span_s[seq], spans)
    joints = (joint_v[...] > 0).astype(F32).astype(BF)
    spread = (iota((JOINTS, AC), 1) % JOINTS == iota((JOINTS, AC), 0)).astype(F32).astype(BF)
    valid = jnp.where(iota((own_seqs, AC), 1) // JOINTS < spans, nn(joints, spread), 0.0)
    ent_v[0] = jnp.broadcast_to(jnp.sum(valid, axis=0, keepdims=True), (8, AC))
    pending = [remote(ent_v.at[0], ent_r.at[0], core)]

    def entries_step(level):
        for copy in pending:
            copy.wait_recv()
        if level == 0:
            total = ent_v[0] + ent_r[0]
        else:
            total = tree(ent_v[level], [ent_r[at] for at in ent_slots[-1]])
        if level == len(radices):
            return total
        ent_v[level + 1] = total
        pending.clear()
        places = []
        for offset in range(1, radices[level]):
            place = 1 + sum(radices[:level]) - level + offset - 1
            places.append(place)
            pending.append(remote(ent_v.at[level + 1], ent_r.at[place], partner(level, offset)))
        ent_slots.append(places)
        return None

    ent_slots = []

    def tree(mine, others):
        if len(others) == 1:
            return mine + others[0]
        return (mine + others[0]) + (others[1] + others[2])

    local["tokens"].wait()
    local["stem_norm"].wait()
    stem_gain = stem_norm_v[...].astype(F32).reshape(1, D)
    half = own_seqs * SEQ_LEN // 2
    for start in (0, half):
        at = pl.ds(start, half)
        raw = x_v[at, :]
        centred = raw.astype(F32) - nn(raw, mean_mat)
        square = centred * centred
        upper = square.astype(BF)
        lower = (square - upper.astype(F32)).astype(BF)
        inv = lax.rsqrt(nn(jnp.concatenate([upper, lower], axis=1), mean_twice) + epsilon)
        unit = centred * inv
        inv_v[at, :] = inv
        unit_v[at, :] = unit
        next_v[at, 0:D] = (unit * stem_gain).astype(BF)
        next_v[at, D : 2 * D] = jnp.ones((half, D), BF)

    def both(ref, *index):
        return jnp.concatenate([ref[(0,) + index], ref[(1,) + index]], axis=0)

    entries_step(0)
    local["stem_latent"].wait()
    for name in ("wq", "wkv"):
        local[name].wait()
        gathered[name].wait_recv()
    latent = stem_latent_v[...]
    wq_t = both(wq_v)
    wk_t, wv_t = both(wkv_v, 0), both(wkv_v, 1)
    stem_q = (nt(latent, wq_t).astype(BF).astype(F32) * HD ** (-0.5)).astype(BF)
    q_diag = (jnp.concatenate([stem_q] * HEADS, axis=0).astype(F32) * diag_heads).astype(BF)
    fold = nn(q_diag, wk_t)
    fold_b = fold.astype(BF)
    mixed, shares, tops = [], [], []
    for seq in range(own_seqs):
        at = pl.ds(seq * SEQ_LEN, SEQ_LEN)
        scores = nt(fold_b, next_v[at, 0:D])
        probs = jnp.exp(scores - jnp.max(scores, axis=1, keepdims=True)).astype(BF)
        e_v[:, seq * SEQ_LEN : (seq + 1) * SEQ_LEN] = probs
        both_sums = nn(probs, next_v[at, :])
        share = 1.0 / both_sums[:, D:]
        shares.append(share)
        mixed.append((both_sums[:, :D] * share).astype(BF))
    mixed_all = jnp.concatenate(mixed, axis=0)
    heads_out = nt(mixed_all, wv_t).reshape(own_seqs, D, D) * diag_heads[None]
    stem_out = jnp.sum(heads_out.reshape(own_seqs, HEADS, LAT, D), axis=1).reshape(rows, D)
    stem_out = stem_out.astype(BF)
    local["wo"].wait()
    gathered["wo"].wait_recv()
    stem_wo = both(wo_v)
    latent_f = latent.astype(F32)
    hidden = jnp.concatenate([latent_f] * own_seqs, axis=0) + nn(stem_out, stem_wo)
    entries_step(1)

    for name in ("norm_attn", "norm_mlp", "b_down", "w_act", "b_act", "targets"):
        local[name].wait()
    for name in ("wqkv", "wout", "wup", "wdn", "bup"):
        local[name].wait()
        gathered[name].wait_recv()
    gain_attn = norm_attn_v[...].astype(F32)
    gain_mlp = norm_mlp_v[...].astype(F32)
    down_bias = b_down_v[...].astype(F32)
    up_bias = jnp.concatenate([bup_v[0], bup_v[1]], axis=1).astype(F32)

    def heads_below(matrix):
        return (matrix[None] * head_mask).reshape(HEADS * rows, D)

    def heads_beside(matrix):
        return jnp.concatenate([matrix * row_mask[head] for head in range(HEADS)], axis=1)

    def lanes_beside(cube):
        return jnp.concatenate([cube[head] for head in range(HEADS)], axis=1)

    def trunk_forward(residual, layer):
        gain_a, gain_m = gain_attn[layer : layer + 1], gain_mlp[layer : layer + 1]
        qkv = jnp.concatenate([both(wqkv_v, layer, part_at) for part_at in range(3)], axis=0)
        out_mat = both(wout_v, layer)
        up_mat = jnp.concatenate([wup_v[0, layer], wup_v[1, layer]], axis=1)
        down_mat = both(wdn_v, layer)
        normed, unit_a, inv_a = norm_rows(residual, gain_a)
        rows_a = normed.astype(BF)
        flat = nt(rows_a, qkv).astype(BF)
        queries = flat[:, :D] * jnp.asarray(HD ** (-0.5), BF)
        keys, values = flat[:, D : 2 * D], flat[:, 2 * D :]
        keys_t = nt(qkv[D : 2 * D], rows_a).astype(BF) * jnp.asarray(HD ** (-0.5), BF)
        values_t = nt(qkv[2 * D :], rows_a).astype(BF)
        scores = nt(heads_below(keys), queries).reshape(HEADS, rows, rows) + block_add[None]
        exped = jnp.exp(scores - jnp.max(scores, axis=1, keepdims=True))
        probs = exped / jnp.sum(exped, axis=1, keepdims=True)
        probs_b = probs.astype(BF)
        out_t = nn(heads_beside(values_t), probs_b.reshape(HEADS * rows, rows))
        attended = out_t.T.astype(BF)
        middle = residual + nn(attended, out_mat)
        normed_m, unit_m, inv_m = norm_rows(middle, gain_m)
        rows_m = normed_m.astype(BF)
        up_rows = nn(rows_m, up_mat) + up_bias[layer : layer + 1]
        cdf = 0.5 + 0.5 * lax.erf(up_rows * (0.5**0.5))
        slope = cdf + up_rows * (jnp.exp(-0.5 * up_rows * up_rows) * 0.3989422804014327)
        hidden_act = (up_rows * cdf).astype(BF)
        output = middle + nn(hidden_act, down_mat) + down_bias[layer : layer + 1]
        saved = dict(
            gain_a=gain_a, gain_m=gain_m, qkv=qkv, out_mat=out_mat, up_mat=up_mat,
            down_mat=down_mat, unit_a=unit_a, inv_a=inv_a, rows_a=rows_a, queries=queries,
            keys_t=keys_t, values=values, probs=probs, probs_b=probs_b, attended=attended,
            unit_m=unit_m, inv_m=inv_m, rows_m=rows_m, slope=slope, hidden_act=hidden_act,
        )
        return output, saved

    kept = []
    for layer in range(LAYERS):
        hidden, saved = trunk_forward(hidden, layer)
        kept.append(saved)
        if layer + 2 < len(radices):
            entries_step(layer + 2)

    entries = jnp.sum(entries_step(len(radices))[0:1], axis=1, keepdims=True)
    total_seqs = own_seqs * lax.axis_size("dp") * lax.axis_size("mp")
    pooled = jnp.sum(hidden.reshape(own_seqs, LAT, D), axis=1)
    act_mat = w_act_v[...]

    def summed3(stacked):
        return stacked[0:own_seqs] + stacked[own_seqs : 2 * own_seqs] + stacked[2 * own_seqs :]

    pred = summed3(nn(split_rows(pooled), act_mat)) + b_act_v[...].astype(F32).reshape(1, AC)
    errors = pred - targets_v[...]
    squares = jnp.sum(valid * errors * errors, axis=0, keepdims=True)
    d_pred = (total_seqs * AC / entries) * (valid * errors)
    head_out[0:own_seqs] = valid * pred
    head_out[own_seqs : own_seqs + 8] = jnp.broadcast_to(entries, (8, AC))
    d_act = lax.dot_general(
        pooled, d_pred, (((0,), (0,)), ((), ())), precision=highest, preferred_element_type=F32
    ).astype(BF)
    d_pooled = summed3(nt(split_rows(d_pred), act_mat))
    upstream = jnp.broadcast_to(d_pooled[:, None, :], (own_seqs, LAT, D)).reshape(rows, D)

    first_row = [sum(CHUNKS[:chunk]) for chunk in range(len(CHUNKS))]
    first_piece = [begin // radices[0] for begin in first_row]
    live = [[] for _ in CHUNKS]

    def put(chunk, offset, mine, others):
        at = pl.ds(first_row[chunk] + offset, mine.shape[0])
        own[at, :] = mine.astype(BF)
        oth[at, :] = others.astype(BF)

    def core_send(chunk):
        at = pl.ds(first_row[chunk], CHUNKS[chunk])
        live[chunk] = [remote(oth.at[at], rcv.at[at], core)]

    def received(chunk):
        for copy in live[chunk]:
            copy.wait_recv()
        live[chunk] = []

    def scatter(chunk):
        received(chunk)
        at = pl.ds(first_row[chunk], CHUNKS[chunk])
        snd[at, :] = (own[at, :].astype(F32) + rcv[at, :].astype(F32)).astype(BF)
        size = CHUNKS[chunk] // radices[0]
        here = pl.ds(first_piece[chunk], size)
        for offset in range(1, radices[0]):
            begin = first_row[chunk] + flip(digits[0], offset) * size
            src = snd.at[pl.ds(pl.multiple_of(begin, 16), size)]
            live[chunk].append(remote(src, rs_r.at[offset - 1, here], partner(0, offset)))

    def share_on(chunk, level):
        received(chunk)
        size = CHUNKS[chunk] // radices[0]
        here = pl.ds(first_piece[chunk], size)
        if level == 1:
            begin = pl.multiple_of(first_row[chunk] + digits[0] * size, 16)
            mine = snd[pl.ds(begin, size), :].astype(F32)
            got = [rs_r[at, here, :].astype(F32) for at in range(radices[0] - 1)]
        else:
            mine = part[level - 2, here, :].astype(F32)
            got = [full_r[level - 2, at, here, :].astype(F32) for at in range(radices[level - 1] - 1)]
        total = tree(mine, got).astype(BF)
        if level < len(radices):
            part[level - 1, here, :] = total
            for offset in range(1, radices[level]):
                dst = full_r.at[level - 1, offset - 1, here]
                live[chunk].append(remote(part.at[level - 1, here], dst, partner(level, offset)))
            return
        mine_at = pl.ds(pl.multiple_of(digits[0] * size, 16), size)
        fins[chunk][mine_at, :] = total
        for offset in range(1, radices[0]):
            piece = fins[chunk].at[mine_at]
            live[chunk].append(remote(piece, piece, partner(0, offset)))

    last = len(radices)

    def back_mlp(upstream, layer, chunk):
        kv = kept[layer]
        grad_top = upstream.astype(BF)
        small_v[16 + 5 + layer : 16 + 6 + layer, :] = jnp.sum(
            grad_top.astype(F32), axis=0, keepdims=True
        )
        d_hidden = nt(grad_top, kv["down_mat"])
        d_upper = (kv["slope"] * d_hidden).astype(BF)
        d_rows = nt(d_upper, kv["up_mat"])
        d_middle = upstream + norm_back(d_rows, kv["unit_m"], kv["inv_m"], kv["gain_m"])
        small_v[16 + 3 + layer : 16 + 4 + layer, :] = jnp.sum(
            d_rows * kv["unit_m"], axis=0, keepdims=True
        )
        d_bias = jnp.sum(d_upper.astype(F32), axis=0, keepdims=True)
        for block in range(4):
            row = 32 + 4 * layer + block
            small_v[row : row + 1, :] = d_bias[:, block * D : (block + 1) * D]
        d_down = tn(kv["hidden_act"], grad_top)
        d_up = tn(kv["rows_m"], d_upper)
        put(chunk, 0, d_up[:, 0:128], d_up[:, 256:384])
        put(chunk, 128, d_up[:, 128:256], d_up[:, 384:512])
        put(chunk, 256, d_down[0:256], d_down[256:512])
        return d_middle

    def back_attn(d_middle, layer, chunk):
        kv = kept[layer]
        grad_attn = d_middle.astype(BF)
        d_mixed = nt(grad_attn, kv["out_mat"]).astype(BF)
        d_probs = nt(heads_below(kv["values"]), d_mixed).reshape(HEADS, rows, rows)
        probs = kv["probs"]
        weighted = probs * d_probs
        inner = jnp.sum(weighted, axis=1, keepdims=True)
        d_scores = (weighted - probs * inner).astype(BF)
        d_q_t = nn(heads_beside(kv["keys_t"]), d_scores.reshape(HEADS * rows, rows))
        d_keys = nn(lanes_beside(d_scores), heads_below(kv["queries"])).astype(BF)
        d_values = nn(lanes_beside(kv["probs_b"]), heads_below(d_mixed)).astype(BF)
        grads = jnp.concatenate([d_q_t.T.astype(BF), d_keys, d_values], axis=1)
        d_rows = nn(grads, kv["qkv"])
        small_v[16 + 1 + layer : 16 + 2 + layer, :] = jnp.sum(
            d_rows * kv["unit_a"], axis=0, keepdims=True
        )
        d_input = d_middle + norm_back(d_rows, kv["unit_a"], kv["inv_a"], kv["gain_a"])
        d_out = tn(kv["attended"], grad_attn)
        d_qkv = tn(grads, kv["rows_a"])
        for place in range(3):
            begin = place * D
            put(chunk, place * 64, d_qkv[begin : begin + 64], d_qkv[begin + 64 : begin + 128])
        put(chunk, 192, d_out[0:64], d_out[64:128])
        return d_input

    put(0, 512, d_act, d_act)
    upstream = back_mlp(upstream, 1, 0)
    core_send(0)
    upstream = back_attn(upstream, 1, 1)
    core_send(1)
    scatter(0)
    upstream = back_mlp(upstream, 0, 2)
    core_send(2)
    scatter(1)
    upstream = back_attn(upstream, 0, 3)
    share_on(0, 1)
    scatter(2)

    grad_stem = upstream.astype(BF)
    d_out_t = nt(stem_wo, grad_stem).astype(BF)
    d_out = nt(grad_stem, stem_wo).astype(BF)
    d_stem_wo = tn(stem_out, grad_stem)
    put(3, 256, d_stem_wo[0:64], d_stem_wo[64:128])
    mixed_heads = jnp.transpose(
        mixed_all.reshape(own_seqs, HEADS, LAT, D), (1, 0, 2, 3)
    ).reshape(HEADS * rows, D)
    d_wv = nn(heads_beside(d_out_t), mixed_heads)
    put(3, 320, d_wv[0:64], d_wv[64:128])
    core_send(3)
    diag_b = diag_heads.astype(BF).reshape(1, HEADS, LAT, D)
    d_diag = (d_out.reshape(own_seqs, 1, LAT, D) * diag_b).reshape(own_seqs, D, D)
    back_v = nn(d_diag.reshape(own_seqs * D, D), wv_t).reshape(own_seqs, D, D)
    d_fold = jnp.zeros((D, D), F32)
    gain_sum = jnp.zeros((D, D), F32)
    folds_v = []
    for seq in range(own_seqs):
        at = pl.ds(seq * SEQ_LEN, SEQ_LEN)
        lanes = slice(seq * SEQ_LEN, (seq + 1) * SEQ_LEN)
        gain_sum += back_v[seq] * mixed[seq].astype(F32)
        scaled_v = back_v[seq] * shares[seq]
        scaled_b = scaled_v.astype(BF)
        folds_v.append(scaled_b)
        d_probs = nt(scaled_b, next_v[at, 0:D])
        probs = e_v[:, lanes].astype(F32)
        weighted = probs * d_probs
        inner = jnp.sum(weighted, axis=1, keepdims=True) * shares[seq][:, 0:1]
        d_scores = (weighted - probs * inner).astype(BF)
        ds_v[:, lanes] = d_scores
        d_fold += nn(d_scores, next_v[at, 0:D])

    d_fold_b = d_fold.astype(BF)
    d_wk = nn(q_diag.astype(F32).T.astype(BF), d_fold_b)
    d_q = nt(d_fold_b, wk_t) * diag_heads
    d_q = jnp.sum(d_q.reshape(HEADS, LAT, D), axis=0) * HD ** (-0.5)
    d_latent = jnp.sum(upstream.reshape(own_seqs, LAT, D), axis=0) + nn(d_q.astype(BF), wq_t)
    small_v[0:16, :] = d_latent
    gain_rows = jnp.sum(gain_sum + d_fold * fold, axis=0, keepdims=True)
    small_v[16:17, :] = gain_rows / stem_gain
    small_v[23:24, :] = jnp.sum(d_pred, axis=0, keepdims=True)
    square_top = squares.astype(BF).astype(F32)
    small_v[24:25, :] = square_top
    small_v[25:26, :] = squares - square_top
    tail_s[0, 0:64, :] = d_wk[0:64].astype(BF)
    tail_s[0, 64:80, :] = d_q.astype(BF)
    tail_s[1, 0:64, :] = d_wk[64:128].astype(BF)
    tail_s[1, 64:80, :] = jnp.concatenate([d_q[:, 64:], d_q[:, :64]], axis=1).astype(BF)
    for place, begin in ((0, 0), (1, 2)):
        for layer in range(LAYERS):
            row = 26 + 2 * layer
            src = 32 + 4 * layer + begin
            small_v[row : row + 2, :] = small_v[src : src + 2, :]
        small_v[30:32, :] = jnp.zeros((2, D), F32)
        tail_s[place, 80:112, :] = small_v[0:32, :].astype(BF)
    tail_live = [remote(tail_s.at[1], tail_r.at[0], core)]

    def tail_step(level):
        for copy in tail_live:
            copy.wait_recv()
        tail_live.clear()
        first = 1 + sum(radices[: level - 1]) - (level - 1)
        count = 1 if level == 0 else radices[level - 1] - 1
        begin = 0 if level == 0 else first
        mine = tail_s[0 if level == 0 else level + 1].astype(F32)
        total = tree(mine, [tail_r[begin + at].astype(F32) for at in range(count)])
        if level == last:
            return total
        tail_s[level + 2] = total.astype(BF)
        nxt = 1 + sum(radices[:level]) - level
        for offset in range(1, radices[level]):
            dst = tail_r.at[nxt + offset - 1]
            tail_live.append(remote(tail_s.at[level + 2], dst, partner(level, offset)))
        return None

    fold_g = (fold * stem_gain).astype(BF)
    fold_side = jnp.concatenate([fold_g, nn(fold_g, mean_mat).astype(BF)], axis=1)

    def token_grads(seq):
        at = pl.ds(seq * SEQ_LEN, SEQ_LEN)
        lanes = slice(seq * SEQ_LEN, (seq + 1) * SEQ_LEN)
        left = jnp.concatenate([ds_v[:, lanes], e_v[:, lanes]], axis=0)
        value_g = (folds_v[seq].astype(F32) * stem_gain).astype(BF)
        value_side = jnp.concatenate([value_g, nn(value_g, mean_mat).astype(BF)], axis=1)
        both_grads = tn(left, jnp.concatenate([fold_side, value_side], axis=0))
        scaled = both_grads[:, :D]
        unit = unit_v[at, :]
        slope_mean = nn((scaled * unit).astype(BF), mean_mat)
        grad_tokens[at, :] = inv_v[at, :] * (scaled - both_grads[:, D:] - unit * slope_mean)

    steps = [
        lambda: share_on(1, 1),
        lambda: scatter(3),
        lambda: tail_step(0),
        lambda: share_on(2, 1),
        lambda: share_on(0, 2),
        lambda: share_on(3, 1),
        lambda: tail_step(1),
        lambda: share_on(1, 2),
    ]
    for seq in range(own_seqs):
        token_grads(seq)
        if seq < len(steps):
            steps[seq]()
    for step in steps[own_seqs:]:
        step()
    share_on(2, 2)
    share_on(3, 2)
    for level in range(3, last + 1):
        for chunk in range(len(CHUNKS)):
            share_on(chunk, level)
    for level in range(2, last):
        tail_step(level)
    total = tail_step(last)
    tail_out[...] = total
    wq_out[...] = tn(total[64:80, 0:64].astype(BF), latent)
    for chunk in range(len(CHUNKS)):
        received(chunk)
    for copy in sends:
        copy.wait_send()


def split_kernel(
    grad_tokens,
    fin_a,
    fin_b,
    fin_c,
    fin_d,
    tail,
    wq_in,
    head,
    actions,
    masked_loss,
    d_tokens,
    d_stem_norm,
    d_latent,
    d_stem_wq,
    d_stem_wkv,
    d_stem_wo,
    d_norm_attn,
    d_qkv,
    d_out,
    d_norm_mlp,
    d_up,
    d_b_up,
    d_down,
    d_b_down,
    d_act,
    d_b_act,
    sem,
):
    copy = pltpu.make_async_copy(grad_tokens, d_tokens, sem)
    copy.start()
    own_seqs = actions.shape[0]
    for layer, mlp, attn in ((1, fin_a, fin_b), (0, fin_c, fin_d)):
        d_up[layer, :, 0:128] = mlp[0:128, :].astype(F32)
        d_up[layer, :, 128:256] = mlp[128:256, :].astype(F32)
        d_down[layer] = mlp[256:512, :].astype(F32)
        for place in range(3):
            d_qkv[layer, place] = attn[64 * place : 64 * place + 64, :].astype(F32)
        d_out[layer] = attn[192:256, :].astype(F32)
        d_b_up[layer : layer + 1, 0:128] = tail[106 + 2 * layer : 107 + 2 * layer, :]
        d_b_up[layer : layer + 1, 128:256] = tail[107 + 2 * layer : 108 + 2 * layer, :]
    d_act[...] = fin_a[512:640, :].astype(F32)
    d_stem_wo[...] = fin_d[256:320, :].astype(F32)
    d_stem_wkv[1] = fin_d[320:384, :].astype(F32)
    d_stem_wkv[0] = tail[0:64, :]
    d_stem_wq[...] = wq_in[...]
    d_latent[...] = tail[80:96, :]
    d_stem_norm[...] = tail[96:97, :].reshape(D)
    d_norm_attn[...] = tail[97:99, :]
    d_norm_mlp[...] = tail[99:101, :]
    d_b_down[...] = tail[101:103, :]
    d_b_act[...] = tail[103:104, :].reshape(D)
    actions[...] = head[0:own_seqs, :]
    squares = jnp.sum(tail[104:105, :] + tail[105:106, :], axis=1, keepdims=True)
    loss = squares / head[own_seqs : own_seqs + 1, :]
    masked_loss[...] = loss.reshape(D)
    copy.wait()


def on_device(radices, *args):
    (
        tokens,
        stem_norm,
        stem_latent,
        stem_wq,
        stem_wkv,
        stem_wo,
        norm_attn,
        w_qkv,
        w_out,
        norm_mlp,
        w_up,
        b_up,
        w_down,
        b_down,
        w_act,
        b_act,
        span_len,
        joint_mask,
        targets,
    ) = args
    own_seqs = targets.shape[0]
    count = own_seqs * SEQ_LEN
    rows = own_seqs * LAT
    last = len(radices)
    spread = sum(radices) - last
    vmem = pl.BlockSpec(memory_space=pltpu.VMEM)
    hbm = pl.BlockSpec(memory_space=pltpu.HBM)
    total_rows = sum(CHUNKS)
    pieces = total_rows // radices[0]
    wide = max(radices) - 1
    n_remote = 8 + 1 + spread + len(CHUNKS) * (1 + spread + radices[0] - 1) + 1 + spread
    shape = jax.ShapeDtypeStruct
    main = pl.pallas_call(
        functools.partial(main_kernel, radices),
        out_shape=[
            shape((count, D), F32),
            *[shape((size, D), BF) for size in CHUNKS],
            shape((TAIL, D), F32),
            shape((64, D), F32),
            shape((own_seqs + 8, AC), F32),
        ],
        in_specs=[hbm] * len(args),
        out_specs=[vmem] * 8,
        scratch_shapes=[
            pltpu.VMEM((count, D), BF),
            pltpu.VMEM((D,), BF),
            pltpu.VMEM((LAT, D), BF),
            pltpu.VMEM((2, 64, D), BF),
            pltpu.VMEM((2, 2, 64, D), BF),
            pltpu.VMEM((2, 64, D), BF),
            pltpu.VMEM((LAYERS, D), BF),
            pltpu.VMEM((2, LAYERS, 3, 64, D), BF),
            pltpu.VMEM((2, LAYERS, 64, D), BF),
            pltpu.VMEM((LAYERS, D), BF),
            pltpu.VMEM((2, LAYERS, D, FF // 2), BF),
            pltpu.VMEM((2, LAYERS, FF // 2), BF),
            pltpu.VMEM((2, LAYERS, FF // 2, D), BF),
            pltpu.VMEM((LAYERS, D), BF),
            pltpu.VMEM((D, AC), BF),
            pltpu.VMEM((AC,), BF),
            pltpu.SMEM((own_seqs,), jnp.int32),
            pltpu.VMEM((own_seqs, JOINTS), jnp.int32),
            pltpu.VMEM((own_seqs, AC), F32),
            pltpu.VMEM((count, 2 * D), BF),
            pltpu.VMEM((count, D), F32),
            pltpu.VMEM((count, D), F32),
            pltpu.VMEM((D, count), BF),
            pltpu.VMEM((D, count), BF),
            pltpu.VMEM((40, D), F32),
            pltpu.VMEM((1 + last, 8, AC), F32),
            pltpu.VMEM((1 + spread, 8, AC), F32),
            pltpu.VMEM((total_rows, D), BF),
            pltpu.VMEM((total_rows, D), BF),
            pltpu.VMEM((total_rows, D), BF),
            pltpu.VMEM((total_rows, D), BF),
            pltpu.VMEM((wide, pieces, D), BF),
            pltpu.VMEM((last - 1, pieces, D), BF),
            pltpu.VMEM((last - 1, wide, pieces, D), BF),
            pltpu.VMEM((2 + last, TAIL, D), BF),
            pltpu.VMEM((1 + spread, TAIL, D), BF),
            pltpu.SemaphoreType.DMA((len(args),)),
            pltpu.SemaphoreType.DMA((n_remote,)),
            pltpu.SemaphoreType.DMA((n_remote,)),
        ],
        compiler_params=pltpu.CompilerParams(
            collective_id=0, has_side_effects=True, vmem_limit_bytes=40 * 2**20
        ),
        name="stem_trunk_head",
    )(
        tokens,
        stem_norm,
        stem_latent,
        jnp.transpose(stem_wq),
        jnp.transpose(stem_wkv, (0, 2, 1)),
        stem_wo,
        norm_attn,
        jnp.transpose(w_qkv, (0, 1, 3, 2)),
        w_out,
        norm_mlp,
        w_up,
        b_up,
        w_down,
        b_down,
        w_act,
        b_act,
        span_len,
        joint_mask,
        targets,
    )
    outs = [
        shape((own_seqs, AC), F32),
        shape((D,), F32),
        shape((count, D), F32),
        shape((D,), F32),
        shape((LAT, D), F32),
        shape((64, D), F32),
        shape((2, 64, D), F32),
        shape((64, D), F32),
        shape((LAYERS, D), F32),
        shape((LAYERS, 3, 64, D), F32),
        shape((LAYERS, 64, D), F32),
        shape((LAYERS, D), F32),
        shape((LAYERS, D, FF // 2), F32),
        shape((LAYERS, FF // 2), F32),
        shape((LAYERS, FF // 2, D), F32),
        shape((LAYERS, D), F32),
        shape((D, AC), F32),
        shape((AC,), F32),
    ]
    out_specs = [vmem] * len(outs)
    out_specs[2] = pl.BlockSpec(memory_space=pl.ANY)
    result = pl.pallas_call(
        split_kernel,
        out_shape=outs,
        in_specs=[pl.BlockSpec(memory_space=pl.ANY)] + [vmem] * 7,
        out_specs=out_specs,
        scratch_shapes=[pltpu.SemaphoreType.DMA],
        compiler_params=pltpu.CompilerParams(vmem_limit_bytes=20 * 2**20),
        name="split_results",
    )(*main)
    result = list(result)
    result[1] = result[1][0]
    result[5] = jnp.transpose(result[5])
    result[6] = jnp.transpose(result[6], (0, 2, 1))
    result[9] = jnp.transpose(result[9], (0, 1, 3, 2))
    return tuple(result)


def solution(mesh):
    radices = radices_of(mesh.shape["dp"])
    in_specs = (
        P(("dp", "mp"), None),
        P(),
        P(),
        P(None, "mp"),
        P(None, None, "mp"),
        P("mp", None),
        P(),
        P(None, None, None, "mp"),
        P(None, "mp", None),
        P(),
        P(None, None, "mp"),
        P(None, "mp"),
        P(None, "mp", None),
        P(),
        P(),
        P(),
        P(("dp", "mp")),
        P(("dp", "mp"), None),
        P(("dp", "mp"), None),
    )
    out_specs = (
        P(("dp", "mp"), None),
        P(),
        P(("dp", "mp"), None),
        P(),
        P(),
        P(None, "mp"),
        P(None, None, "mp"),
        P("mp", None),
        P(),
        P(None, None, None, "mp"),
        P(None, "mp", None),
        P(),
        P(None, None, "mp"),
        P(None, "mp"),
        P(None, "mp", None),
        P(),
        P(),
        P(),
    )
    return jax.shard_map(
        functools.partial(on_device, radices),
        mesh=mesh,
        in_specs=in_specs,
        out_specs=out_specs,
        check_vma=False,
    )
```

time: 643 us -> 54 us (0.08)
  waiting for transfers between devices: 373 us -> 0 us
  blocking collectives: 98.5 us -> 0 us
  matrix products: 58.3 us -> 0 us
  other arithmetic: 48.8 us -> 0 us
  Pallas kernels: 0 us -> 39.8 us
  local copies, waits for them, and re-layouts: 40.7 us -> 12.8 us
  between operations: 18.7 us -> 0.71 us
    psum x3 -> x0, waiting for transfers between devices: 296 us -> none  [the longest x2 234 us: on_device(): summed = lax.psum(pending, 'dp')]
    psum x2 -> x0, blocking collectives: 81.6 us -> none  [the longest x1 40.9 us: on_device(): entries = lax.psum(jnp.sum(valid_mask), ('dp', 'mp'))]
    reduce_scatter x10 -> x0, waiting for transfers between devices: 65.4 us -> none  [the longest x5 33.3 us: fold_rows(): lax.psum_scatter(values_in.astype(jnp.bfloat16), 'mp', scatter_dimension=...]
    dot_general x69 -> x0, matrix products: 58.3 us -> none  [the longest x46 41 us: low_dot(): return jnp.dot(left, right, preferred_element_type=jnp.float32)]
    pallas_call x0 -> x2, Pallas kernels: none -> 39.8 us  [the longest x1 37.8 us: on_device(): pl.pallas_call(functools.partial(main_kernel, radices), out_shape=[shape(...]
    reduce_sum x23 -> x0, other arithmetic: 21.1 us -> none  [the longest x5 8.14 us: normalize_back(): d_gain = jnp.sum(upstream * unit_rows, axis=0)]
    all_gather x9 -> x0, blocking collectives: 16.9 us -> none  [the longest x5 9.45 us: spread_grads(): return lax.all_gather(values_in, 'mp', axis=0, tiled=True)]
    reshape x21 -> x0, local copies, waits for them, and re-layouts: 15.9 us -> none  [the longest x6 6.16 us: trunk_back(): grad_part.astype(jnp.bfloat16).reshape(flat_shape)]
  transfers between devices with their start and end apart: 14 -> 0, of which waited for: 12 -> 0; matrix products, arithmetic and copies ran while one was open for 6% -> 0% of each run, Pallas kernels for 0% -> 0%
where the time goes in v1:
time: 54 us; the launch traced here: 53.3 us
  Pallas kernels  39.8 us (74%)
  local copies, waits for them, and re-layouts  12.8 us (24%)
  between operations  0.71 us (1%)
    pallas_call x1, Pallas kernels, on_device(): pl.pallas_call(functools.partial(main_kernel, radices), out_shape=[shape(...  37.8 us
    unnamed x38, local copies, waits for them, and re-layouts  12.8 us
    pallas_call x1, Pallas kernels, on_device(): pl.pallas_call(split_kernel, out_shape=outs, in_specs=[pl.BlockSpec(memor...  2.02 us

profile of v1, /device:TPU:0, one launch (start us, length us, event | category | flops | bytes accessed | tf_op | source)
XLA Modules:
  0.0 53.3 jit_solution(15902810543113823041)
XLA Ops:
  0.7 0.0 copy-start.9
  0.7 0.0 copy-start.12
  0.7 0.0 copy-start.13
  0.7 0.7 %copy-done.9 = bf16[16,128]{1,0:T(8,128)(2,1)S(1)} copy-done((bf16[16,128]{1,0:T(8,128)(2,1)S(1)}, bf16[16,128]{1,0:T(8,128)(2,1)}, u32[]{:S(2)}) %copy-start.9) | copy-done | bytes 4120
  1.4 0.0 copy-done.12
  1.4 0.0 copy-done.13
  1.4 0.0 copy-start
  1.4 1.0 %copy-done = bf16[2048,128]{1,0:T(8,128)(2,1)S(1)} copy-done((bf16[2048,128]{1,0:T(8,128)(2,1)S(1)}, bf16[2048,128]{1,0:T(8,128)(2,1)}, u32[]{:S(2)}) %copy-start) | copy-done | bytes 524312
  2.4 0.0 copy-start.1
  2.4 0.9 %copy-done.1 = bf16[2,128,256]{2,1,0:T(8,128)(2,1)S(1)} copy-done((bf16[2,128,256]{2,1,0:T(8,128)(2,1)S(1)}, bf16[2,128,256]{2,1,0:T(8,128)(2,1)}, u32[]{:S(2)}) %copy-start.1) | copy-done | bytes 131096
  3.3 0.0 copy-start.2
  3.3 0.9 %copy-done.2 = bf16[2,256,128]{2,1,0:T(8,128)(2,1)S(1)} copy-done((bf16[2,256,128]{2,1,0:T(8,128)(2,1)S(1)}, bf16[2,256,128]{2,1,0:T(8,128)(2,1)}, u32[]{:S(2)}) %copy-start.2) | copy-done | bytes 131096
  4.2 0.0 copy-start.3
  4.2 0.9 %copy-done.3 = bf16[2,3,128,64]{2,3,1,0:T(8,128)(2,1)S(1)} copy-done((bf16[2,3,128,64]{2,3,1,0:T(8,128)(2,1)S(1)}, bf16[2,3,128,64]{2,3,1,0:T(8,128)(2,1)}, u32[]{:S(2)}) %copy-start.3) | copy-done | bytes 98328
  5.1 0.0 copy-start.4
  5.1 0.8 %copy-done.4 = bf16[2,128,64]{1,2,0:T(8,128)(2,1)S(1)} copy-done((bf16[2,128,64]{1,2,0:T(8,128)(2,1)S(1)}, bf16[2,128,64]{1,2,0:T(8,128)(2,1)}, u32[]{:S(2)}) %copy-start.4) | copy-done | bytes 32792
  5.9 0.8 %copy-done.5 = bf16[2,64,128]{2,1,0:T(8,128)(2,1)S(1)} copy-done((bf16[2,64,128]{2,1,0:T(8,128)(2,1)S(1)}, bf16[2,64,128]{2,1,0:T(8,128)(2,1)}, u32[]{:S(2)}) %copy-start.5) | copy-done | bytes 32792
  6.6 0.0 copy-start.6
  6.6 0.8 %copy-done.6 = bf16[128,128]{1,0:T(8,128)(2,1)S(1)} copy-done((bf16[128,128]{1,0:T(8,128)(2,1)S(1)}, bf16[128,128]{1,0:T(8,128)(2,1)}, u32[]{:S(2)}) %copy-start.6) | copy-done | bytes 32792
  7.4 0.0 copy-start.7
  7.4 0.7 %copy-done.7 = bf16[128,64]{0,1:T(8,128)(2,1)S(1)} copy-done((bf16[128,64]{0,1:T(8,128)(2,1)S(1)}, bf16[128,64]{0,1:T(8,128)(2,1)}, u32[]{:S(2)}) %copy-start.7) | copy-done | bytes 16408
  8.1 0.0 copy-start.8
  8.1 0.7 %copy-done.8 = bf16[64,128]{1,0:T(8,128)(2,1)S(1)} copy-done((bf16[64,128]{1,0:T(8,128)(2,1)S(1)}, bf16[64,128]{1,0:T(8,128)(2,1)}, u32[]{:S(2)}) %copy-start.8) | copy-done | bytes 16408
  8.8 0.7 %copy-done.10 = s32[8,8]{1,0:T(8,128)S(1)} copy-done((s32[8,8]{1,0:T(8,128)S(1)}, s32[8,8]{1,0:T(8,128)}, u32[]{:S(2)}) %copy-start.10) | copy-done | bytes 280
  9.5 0.7 %copy-done.11 = f32[8,128]{1,0:T(8,128)S(1)} copy-done((f32[8,128]{1,0:T(8,128)S(1)}, f32[8,128]{1,0:T(8,128)}, u32[]{:S(2)}) %copy-start.11) | copy-done | bytes 4120
  10.2 0.7 %copy-done.14 = bf16[2,128]{1,0:T(2,128)(2,1)S(1)} copy-done((bf16[2,128]{1,0:T(2,128)(2,1)S(1)}, bf16[2,128]{1,0:T(2,128)(2,1)}, u32[]{:S(2)}) %copy-start.14) | copy-done | bytes 536
  10.9 0.7 %copy-done.15 = bf16[2,128]{1,0:T(2,128)(2,1)S(1)} copy-done((bf16[2,128]{1,0:T(2,128)(2,1)S(1)}, bf16[2,128]{1,0:T(2,128)(2,1)}, u32[]{:S(2)}) %copy-start.15) | copy-done | bytes 536
  11.5 0.7 %copy-done.16 = bf16[2,128]{1,0:T(2,128)(2,1)S(1)} copy-done((bf16[2,128]{1,0:T(2,128)(2,1)S(1)}, bf16[2,128]{1,0:T(2,128)(2,1)}, u32[]{:S(2)}) %copy-start.16) | copy-done | bytes 536
  12.2 0.7 %copy-done.17 = bf16[128]{0:T(256)(128)(2,1)S(1)} copy-done((bf16[128]{0:T(256)(128)(2,1)S(1)}, bf16[128]{0:T(256)(128)(2,1)}, u32[]{:S(2)}) %copy-start.17) | copy-done | bytes 280
  12.8 0.7 %copy-done.18 = s32[8]{0:T(128)S(1)} copy-done((s32[8]{0:T(128)S(1)}, s32[8]{0:T(128)}, u32[]{:S(2)}) %copy-start.18) | copy-done | bytes 56
  13.5 37.8 %stem_trunk_head.1 = (f32[2048,128]{1,0:T(8,128)S(1)}, bf16[640,128]{1,0:T(8,128)(2,1)S(1)}, bf16[256,128]{1,0:T(8,128)(2,1)S(1)}, bf16[512,128]{1,0:T(8,128)(2,...) custom-call(bf16[2048,128]{1,0:T(8,128)(2,1)S(1)} %copy-done, ...), custom_call_target="tpu_custom_call" | custom-call | tf_op jit(solution)/shard_map/stem_trunk_head/pallas_call | solution.py:754
  51.3 2.0 %split_results.1 = (f32[8,128]{1,0:T(8,128)}, f32[128]{0:T(128)}, f32[2048,128]{1,0:T(8,128)}, f32[128]{0:T(128)}, f32[16,128]{1,0:T(8,128)}, /*index=5*/f32[64,...) custom-call(f32[2048,128]{1,0:T(8,128)S(1)} %get-tuple-element.44.gr, ...), custom_call_target="tpu_custom_call" | custom-call | tf_op jit(solution)/shard_map/split_results/pallas_call | solution.py:853
  (8 shorter events, 0.0 us)
Async XLA Ops:
  0.7 0.7 %copy-start.9 = (bf16[16,128]{1,0:T(8,128)(2,1)S(1)}, bf16[16,128]{1,0:T(8,128)(2,1)}, u32[]{:S(2)}) copy-start(bf16[16,128]{1,0:T(8,128)(2,1)} %stem_latent_h.1) | copy-start | bytes 12292
  0.7 0.7 %copy-start.12 = (bf16[2,256]{1,0:T(2,128)(2,1)S(1)}, bf16[2,256]{1,0:T(2,128)(2,1)}, u32[]{:S(2)}) copy-start(bf16[2,256]{1,0:T(2,128)(2,1)} %b_up_h.1) | copy-start | bytes 3076
  0.7 0.7 %copy-start.13 = (bf16[128]{0:T(256)(128)(2,1)S(1)}, bf16[128]{0:T(256)(128)(2,1)}, u32[]{:S(2)}) copy-start(bf16[128]{0:T(256)(128)(2,1)} %stem_norm_h.1) | copy-start | bytes 772
  1.4 1.0 %copy-start = (bf16[2048,128]{1,0:T(8,128)(2,1)S(1)}, bf16[2048,128]{1,0:T(8,128)(2,1)}, u32[]{:S(2)}) copy-start(bf16[2048,128]{1,0:T(8,128)(2,1)} %tokens_h.1) | copy-start | bytes 1572868
  2.4 0.9 %copy-start.1 = (bf16[2,128,256]{2,1,0:T(8,128)(2,1)S(1)}, bf16[2,128,256]{2,1,0:T(8,128)(2,1)}, u32[]{:S(2)}) copy-start(bf16[2,128,256]{2,1,0:T(8,128)(2,1)} %w_up_h.1) | copy-start | bytes 393220
  3.3 0.9 %copy-start.2 = (bf16[2,256,128]{2,1,0:T(8,128)(2,1)S(1)}, bf16[2,256,128]{2,1,0:T(8,128)(2,1)}, u32[]{:S(2)}) copy-start(bf16[2,256,128]{2,1,0:T(8,128)(2,1)} %w_down_h.1) | copy-start | bytes 393220
  4.2 0.9 %copy-start.3 = (bf16[2,3,128,64]{2,3,1,0:T(8,128)(2,1)S(1)}, bf16[2,3,128,64]{2,3,1,0:T(8,128)(2,1)}, u32[]{:S(2)}) copy-start(bf16[2,3,128,64]{2,3,1,0:T(8,128)(2,1)} %param.26) | copy-start | bytes 294916
  5.1 0.8 %copy-start.4 = (bf16[2,128,64]{1,2,0:T(8,128)(2,1)S(1)}, bf16[2,128,64]{1,2,0:T(8,128)(2,1)}, u32[]{:S(2)}) copy-start(bf16[2,128,64]{1,2,0:T(8,128)(2,1)} %param.23) | copy-start | bytes 98308
  5.9 0.8 %copy-start.5 = (bf16[2,64,128]{2,1,0:T(8,128)(2,1)S(1)}, bf16[2,64,128]{2,1,0:T(8,128)(2,1)}, u32[]{:S(2)}) copy-start(bf16[2,64,128]{2,1,0:T(8,128)(2,1)} %w_out_h.1) | copy-start | bytes 98308
  6.6 0.8 %copy-start.6 = (bf16[128,128]{1,0:T(8,128)(2,1)S(1)}, bf16[128,128]{1,0:T(8,128)(2,1)}, u32[]{:S(2)}) copy-start(bf16[128,128]{1,0:T(8,128)(2,1)} %w_act_h.1) | copy-start | bytes 98308
  7.4 0.7 %copy-start.7 = (bf16[128,64]{0,1:T(8,128)(2,1)S(1)}, bf16[128,64]{0,1:T(8,128)(2,1)}, u32[]{:S(2)}) copy-start(bf16[128,64]{0,1:T(8,128)(2,1)} %param.22) | copy-start | bytes 49156
  8.1 0.7 %copy-start.8 = (bf16[64,128]{1,0:T(8,128)(2,1)S(1)}, bf16[64,128]{1,0:T(8,128)(2,1)}, u32[]{:S(2)}) copy-start(bf16[64,128]{1,0:T(8,128)(2,1)} %stem_wo_h.1) | copy-start | bytes 49156
  8.8 0.7 %copy-start.10 = (s32[8,8]{1,0:T(8,128)S(1)}, s32[8,8]{1,0:T(8,128)}, u32[]{:S(2)}) copy-start(s32[8,8]{1,0:T(8,128)} %joint_mask_h.1) | copy-start | bytes 772
  9.5 0.7 %copy-start.11 = (f32[8,128]{1,0:T(8,128)S(1)}, f32[8,128]{1,0:T(8,128)}, u32[]{:S(2)}) copy-start(f32[8,128]{1,0:T(8,128)} %targets_h.1) | copy-start | bytes 12292
  10.2 0.7 %copy-start.14 = (bf16[2,128]{1,0:T(2,128)(2,1)S(1)}, bf16[2,128]{1,0:T(2,128)(2,1)}, u32[]{:S(2)}) copy-start(bf16[2,128]{1,0:T(2,128)(2,1)} %norm_attn_h.1) | copy-start | bytes 1540
  10.8 0.7 %copy-start.15 = (bf16[2,128]{1,0:T(2,128)(2,1)S(1)}, bf16[2,128]{1,0:T(2,128)(2,1)}, u32[]{:S(2)}) copy-start(bf16[2,128]{1,0:T(2,128)(2,1)} %norm_mlp_h.1) | copy-start | bytes 1540
  11.5 0.7 %copy-start.16 = (bf16[2,128]{1,0:T(2,128)(2,1)S(1)}, bf16[2,128]{1,0:T(2,128)(2,1)}, u32[]{:S(2)}) copy-start(bf16[2,128]{1,0:T(2,128)(2,1)} %b_down_h.1) | copy-start | bytes 1540
  12.2 0.7 %copy-start.17 = (bf16[128]{0:T(256)(128)(2,1)S(1)}, bf16[128]{0:T(256)(128)(2,1)}, u32[]{:S(2)}) copy-start(bf16[128]{0:T(256)(128)(2,1)} %b_act_h.1) | copy-start | bytes 772
  12.8 0.7 %copy-start.18 = (s32[8]{0:T(128)S(1)}, s32[8]{0:T(128)}, u32[]{:S(2)}) copy-start(s32[8]{0:T(128)} %span_len_h.1) | copy-start | bytes 100

commit v2 on v1

--- a/solution.py
+++ b/solution.py
@@ -808,25 +808,30 @@
         ),
         name="stem_trunk_head",
     )(
-        tokens,
-        stem_norm,
-        stem_latent,
-        jnp.transpose(stem_wq),
-        jnp.transpose(stem_wkv, (0, 2, 1)),
-        stem_wo,
-        norm_attn,
-        jnp.transpose(w_qkv, (0, 1, 3, 2)),
-        w_out,
-        norm_mlp,
-        w_up,
-        b_up,
-        w_down,
-        b_down,
-        w_act,
-        b_act,
-        span_len,
-        joint_mask,
-        targets,
+        *[
+            pltpu.with_memory_space_constraint(arg, pltpu.HBM)
+            for arg in (
+                tokens,
+                stem_norm,
+                stem_latent,
+                jnp.transpose(stem_wq),
+                jnp.transpose(stem_wkv, (0, 2, 1)),
+                stem_wo,
+                norm_attn,
+                jnp.transpose(w_qkv, (0, 1, 3, 2)),
+                w_out,
+                norm_mlp,
+                w_up,
+                b_up,
+                w_down,
+                b_down,
+                w_act,
+                b_act,
+                span_len,
+                joint_mask,
+                targets,
+            )
+        ]
     )
     outs = [
         shape((own_seqs, AC), F32),

time: 54 us -> 40.7 us (0.75); the launches traced: 53.3 us -> 40.6 us
  local copies, waits for them, and re-layouts: 12.8 us -> 0 us
    unnamed x38 -> x0, local copies, waits for them, and re-layouts: 12.8 us -> none
where the time goes in v2:
time: 40.7 us; the launch traced here: 40.6 us
  Pallas kernels  39.9 us (98%)
  between operations  0.67 us (2%)
    pallas_call x1, Pallas kernels, on_device(): pl.pallas_call(functools.partial(main_kernel, radices), out_shape=[shape(...  37.9 us
    pallas_call x1, Pallas kernels, on_device(): pl.pallas_call(split_kernel, out_shape=outs, in_specs=[pl.BlockSpec(memor...  2.02 us

profile of v2, /device:TPU:0, one launch (start us, length us, event | category | flops | bytes accessed | tf_op | source)
XLA Modules:
  0.0 40.6 jit_solution(10253665828428934408)
XLA Ops:
  0.7 37.9 %stem_trunk_head.1 = (f32[2048,128]{1,0:T(8,128)S(1)}, bf16[640,128]{1,0:T(8,128)(2,1)S(1)}, bf16[256,128]{1,0:T(8,128)(2,1)S(1)}, bf16[512,128]{1,0:T(8,128)(2,...) custom-call(bf16[2048,128]{1,0:T(8,128)(2,1)} %tokens_h.1, ...), custom_call_target="tpu_custom_call" | custom-call | tf_op jit(solution)/shard_map/stem_trunk_head/pallas_call | solution.py:754
  38.6 2.0 %split_results.1 = (f32[8,128]{1,0:T(8,128)}, f32[128]{0:T(128)}, f32[2048,128]{1,0:T(8,128)}, f32[128]{0:T(128)}, f32[16,128]{1,0:T(8,128)}, /*index=5*/f32[64,...) custom-call(f32[2048,128]{1,0:T(8,128)S(1)} %get-tuple-element.44.gr, ...), custom_call_target="tpu_custom_call" | custom-call | tf_op jit(solution)/shard_map/split_results/pallas_call | solution.py:858

commit v3 on v2

--- a/solution.py
+++ b/solution.py
@@ -1,4 +1,5 @@
 import functools
+import math
 
 import jax
 import jax.numpy as jnp
@@ -24,8 +25,7 @@
 epsilon = 1e-05
 highest = lax.Precision.HIGHEST
 
-CHUNKS = (640, 256, 512, 384)
-TAIL = 112
+CHUNKS = (256, 256, 256, 256, 256, 256, 256, 128)
 
 
 def nn(left, right):
@@ -47,18 +47,22 @@
 def radices_of(count):
     found = []
     while count > 1:
-        radix = 4 if count % 4 == 0 else 2
+        radix = 8 if count % 8 == 0 else 4 if count % 4 == 0 else 2
         found.append(radix)
         count //= radix
     return found
 
 
 def flip(digit, offset):
-    if offset == 1:
-        return digit + 1 - 2 * (digit % 2)
-    if offset == 2:
-        return (digit + 2) % 4
-    return 3 - digit
+    flipped = digit
+    for bit in (1, 2, 4):
+        if offset & bit:
+            flipped = flipped + bit - 2 * bit * ((digit // bit) % 2)
+    return flipped
+
+
+def far_first(radix):
+    return sorted(range(1, radix), key=lambda offset: -bin(offset).count("1"))
 
 
 def norm_rows(values_in, gain_vec):
@@ -113,7 +117,10 @@
     fin_b,
     fin_c,
     fin_d,
-    tail_out,
+    fin_e,
+    fin_f,
+    fin_g,
+    fin_h,
     wq_out,
     head_out,
     x_v,
@@ -150,8 +157,6 @@
     rs_r,
     part,
     full_r,
-    tail_s,
-    tail_r,
     in_sem,
     send_sem,
     recv_sem,
@@ -159,18 +164,21 @@
     dp, mp = lax.axis_index("dp"), lax.axis_index("mp")
     own_seqs = targets_h.shape[0]
     rows = own_seqs * LAT
-    fins = (fin_a, fin_b, fin_c, fin_d)
+    fins = (fin_a, fin_b, fin_c, fin_d, fin_e, fin_f, fin_g, fin_h)
     core = (dp, 1 - mp)
-    strides, digits = [], []
-    stride = 1
-    for radix in radices:
-        strides.append(stride)
-        digits.append((dp // stride) % radix)
-        stride *= radix
+    digits = [(dp // math.prod(radices[:level])) % radix for level, radix in enumerate(radices)]
+
+    places = {}
 
     def partner(level, offset):
-        digit = digits[level]
-        return (dp + (flip(digit, offset) - digit) * strides[level], mp)
+        stride = math.prod(radices[:level])
+        if (level, offset) not in places:
+            digit = digits[level]
+            places[level, offset] = (dp + (flip(digit, offset) - digit) * stride, mp)
+        return places[level, offset]
+
+    def apart(step, *given):
+        pl.when(dp >= 0)(functools.partial(step, *given))
 
     barrier = pltpu.get_barrier_semaphore()
     greeted = [core]
@@ -179,21 +187,30 @@
     for device in greeted:
         pl.semaphore_signal(barrier, inc=1, device_id=device, device_id_type=MESH)
 
+    piece_of = {}
+    for size in sorted({chunk // radices[0] for chunk in CHUNKS}):
+        piece_of[size] = [
+            pl.multiple_of(flip(digits[0], offset) * size, size) for offset in range(radices[0])
+        ]
     slots = [0]
     sends = []
 
-    def remote(src, dst, device):
+    def remote(ends, device):
         slot = slots[0]
         slots[0] += 1
-        copy = pltpu.make_async_remote_copy(
-            src_ref=src,
-            dst_ref=dst,
-            send_sem=send_sem.at[slot],
-            recv_sem=recv_sem.at[slot],
-            device_id=device,
-            device_id_type=MESH,
-        )
-        copy.start()
+
+        def copy():
+            src, dst = ends()
+            return pltpu.make_async_remote_copy(
+                src_ref=src,
+                dst_ref=dst,
+                send_sem=send_sem.at[slot],
+                recv_sem=recv_sem.at[slot],
+                device_id=device,
+                device_id_type=MESH,
+            )
+
+        copy().start()
         sends.append(copy)
         return copy
 
@@ -202,16 +219,16 @@
         ("tokens", tokens_h, x_v),
         ("stem_norm", stem_norm_h, stem_norm_v),
         ("stem_latent", stem_latent_h, stem_latent_v),
-        ("wq", stem_wq_h, wq_v.at[0]),
-        ("wkv", stem_wkv_h, wkv_v.at[0]),
-        ("wo", stem_wo_h, wo_v.at[0]),
-        ("wqkv", w_qkv_h, wqkv_v.at[0]),
-        ("wout", w_out_h, wout_v.at[0]),
-        ("wup", w_up_h, wup_v.at[0]),
-        ("wdn", w_down_h, wdn_v.at[0]),
+        ("wq", stem_wq_h, wq_v),
+        ("wkv", stem_wkv_h, wkv_v),
+        ("wo", stem_wo_h, wo_v),
+        ("wqkv", w_qkv_h, wqkv_v),
+        ("wout", w_out_h, wout_v),
+        ("wup", w_up_h, wup_v),
+        ("wdn", w_down_h, wdn_v),
         ("norm_attn", norm_attn_h, norm_attn_v),
         ("norm_mlp", norm_mlp_h, norm_mlp_v),
-        ("bup", b_up_h, bup_v.at[0]),
+        ("bup", b_up_h, bup_v),
         ("b_down", b_down_h, b_down_v),
         ("w_act", w_act_h, w_act_v),
         ("b_act", b_act_h, b_act_v),
@@ -219,9 +236,15 @@
         ("joint", joint_mask_h, joint_v),
         ("targets", targets_h, targets_v),
     )
+    halves = ("wq", "wkv", "wo", "wqkv", "wout", "wup", "wdn", "bup")
+
+    def load(place, name, src, dst):
+        here = dst.at[0] if name in halves else dst
+        return pltpu.make_async_copy(src, here, in_sem.at[place])
+
     for place, (name, src, dst) in enumerate(pairs):
-        local[name] = pltpu.make_async_copy(src, dst, in_sem.at[place])
-        local[name].start()
+        local[name] = functools.partial(load, place, name, src, dst)
+        local[name]().start()
 
     head_mask = (
         (iota((HEADS, D, D), 2) // HD == iota((HEADS, D, D), 0)).astype(F32).astype(BF)
@@ -232,34 +255,11 @@
     mean_mat = jnp.full((D, D), 1.0 / D, BF)
     mean_twice = jnp.full((2 * D, D), 1.0 / D, BF)
 
-    pl.semaphore_wait(barrier, len(greeted))
     gathered = {}
-    for name, src, dst in (
-        ("wq", stem_wq_h, wq_v.at[1]),
-        ("wkv", stem_wkv_h, wkv_v.at[1]),
-        ("wo", stem_wo_h, wo_v.at[1]),
-        ("wqkv", w_qkv_h, wqkv_v.at[1]),
-        ("wout", w_out_h, wout_v.at[1]),
-        ("wup", w_up_h, wup_v.at[1]),
-        ("wdn", w_down_h, wdn_v.at[1]),
-        ("bup", b_up_h, bup_v.at[1]),
-    ):
-        gathered[name] = remote(src, dst, core)
-
-    local["span"].wait()
-    local["joint"].wait()
-    spans = jnp.zeros((own_seqs, AC), jnp.int32)
-    for seq in range(own_seqs):
-        spans = jnp.where(iota((own_seqs, AC), 0) == seq, span_s[seq], spans)
-    joints = (joint_v[...] > 0).astype(F32).astype(BF)
-    spread = (iota((JOINTS, AC), 1) % JOINTS == iota((JOINTS, AC), 0)).astype(F32).astype(BF)
-    valid = jnp.where(iota((own_seqs, AC), 1) // JOINTS < spans, nn(joints, spread), 0.0)
-    ent_v[0] = jnp.broadcast_to(jnp.sum(valid, axis=0, keepdims=True), (8, AC))
-    pending = [remote(ent_v.at[0], ent_r.at[0], core)]
 
     def entries_step(level):
         for copy in pending:
-            copy.wait_recv()
+            copy().wait_recv()
         if level == 0:
             total = ent_v[0] + ent_r[0]
         else:
@@ -272,19 +272,40 @@
         for offset in range(1, radices[level]):
             place = 1 + sum(radices[:level]) - level + offset - 1
             places.append(place)
-            pending.append(remote(ent_v.at[level + 1], ent_r.at[place], partner(level, offset)))
+            pending.append(
+                remote(
+                    lambda place=place: (ent_v.at[level + 1], ent_r.at[place]),
+                    partner(level, offset),
+                )
+            )
         ent_slots.append(places)
         return None
 
     ent_slots = []
 
     def tree(mine, others):
-        if len(others) == 1:
-            return mine + others[0]
-        return (mine + others[0]) + (others[1] + others[2])
-
-    local["tokens"].wait()
-    local["stem_norm"].wait()
+        terms = [mine] + list(others)
+        while len(terms) > 1:
+            terms = [terms[at] + terms[at + 1] for at in range(0, len(terms), 2)]
+        return terms[0]
+
+    def wait_for(*names):
+        for name in names:
+            local[name]().wait()
+
+    def wait_gathered(*names):
+        for name in names:
+            gathered[name]().wait_recv()
+
+    def meet():
+        pl.semaphore_wait(barrier, len(greeted))
+        for name, src, dst in pairs:
+            if name in halves:
+                gathered[name] = remote(lambda src=src, dst=dst: (src, dst.at[1]), core)
+
+    apart(meet)
+
+    apart(wait_for, "tokens", "stem_norm")
     stem_gain = stem_norm_v[...].astype(F32).reshape(1, D)
     half = own_seqs * SEQ_LEN // 2
     for start in (0, half):
@@ -304,19 +325,31 @@
     def both(ref, *index):
         return jnp.concatenate([ref[(0,) + index], ref[(1,) + index]], axis=0)
 
-    entries_step(0)
-    local["stem_latent"].wait()
-    for name in ("wq", "wkv"):
-        local[name].wait()
-        gathered[name].wait_recv()
+    apart(wait_for, "span", "joint")
+    spans = jnp.zeros((own_seqs, AC), jnp.int32)
+    for seq in range(own_seqs):
+        spans = jnp.where(iota((own_seqs, AC), 0) == seq, span_s[seq], spans)
+    joints = (joint_v[...] > 0).astype(F32).astype(BF)
+    spread = (iota((JOINTS, AC), 1) % JOINTS == iota((JOINTS, AC), 0)).astype(F32).astype(BF)
+    valid = jnp.where(iota((own_seqs, AC), 1) // JOINTS < spans, nn(joints, spread), 0.0)
+    ent_v[0] = jnp.broadcast_to(jnp.sum(valid, axis=0, keepdims=True), (8, AC))
+    pending = []
+
+    def entries_begin():
+        pending.append(remote(lambda: (ent_v.at[0], ent_r.at[0]), core))
+
+    apart(entries_begin)
+
+    apart(wait_for, "stem_latent", "wq", "wkv")
+    apart(wait_gathered, "wq", "wkv")
     latent = stem_latent_v[...]
     wq_t = both(wq_v)
     wk_t, wv_t = both(wkv_v, 0), both(wkv_v, 1)
-    stem_q = (nt(latent, wq_t).astype(BF).astype(F32) * HD ** (-0.5)).astype(BF)
-    q_diag = (jnp.concatenate([stem_q] * HEADS, axis=0).astype(F32) * diag_heads).astype(BF)
+    stem_q = nt(latent, wq_t).astype(BF).astype(F32) * HD ** (-0.5)
+    q_diag = (jnp.concatenate([stem_q] * HEADS, axis=0) * diag_heads).astype(BF)
     fold = nn(q_diag, wk_t)
     fold_b = fold.astype(BF)
-    mixed, shares, tops = [], [], []
+    mixed, shares = [], []
     for seq in range(own_seqs):
         at = pl.ds(seq * SEQ_LEN, SEQ_LEN)
         scores = nt(fold_b, next_v[at, 0:D])
@@ -326,22 +359,20 @@
         share = 1.0 / both_sums[:, D:]
         shares.append(share)
         mixed.append((both_sums[:, :D] * share).astype(BF))
+    apart(entries_step, 0)
     mixed_all = jnp.concatenate(mixed, axis=0)
     heads_out = nt(mixed_all, wv_t).reshape(own_seqs, D, D) * diag_heads[None]
     stem_out = jnp.sum(heads_out.reshape(own_seqs, HEADS, LAT, D), axis=1).reshape(rows, D)
     stem_out = stem_out.astype(BF)
-    local["wo"].wait()
-    gathered["wo"].wait_recv()
+    apart(wait_for, "wo")
+    apart(wait_gathered, "wo")
     stem_wo = both(wo_v)
     latent_f = latent.astype(F32)
     hidden = jnp.concatenate([latent_f] * own_seqs, axis=0) + nn(stem_out, stem_wo)
-    entries_step(1)
-
-    for name in ("norm_attn", "norm_mlp", "b_down", "w_act", "b_act", "targets"):
-        local[name].wait()
-    for name in ("wqkv", "wout", "wup", "wdn", "bup"):
-        local[name].wait()
-        gathered[name].wait_recv()
+
+    apart(wait_for, "norm_attn", "norm_mlp", "b_down", "w_act", "b_act", "targets")
+    apart(wait_for, "wqkv", "wout", "wup", "wdn", "bup")
+    apart(wait_gathered, "wqkv", "wout", "wup", "wdn", "bup")
     gain_attn = norm_attn_v[...].astype(F32)
     gain_mlp = norm_mlp_v[...].astype(F32)
     down_bias = b_down_v[...].astype(F32)
@@ -395,11 +426,7 @@
     for layer in range(LAYERS):
         hidden, saved = trunk_forward(hidden, layer)
         kept.append(saved)
-        if layer + 2 < len(radices):
-            entries_step(layer + 2)
-
-    entries = jnp.sum(entries_step(len(radices))[0:1], axis=1, keepdims=True)
-    total_seqs = own_seqs * lax.axis_size("dp") * lax.axis_size("mp")
+
     pooled = jnp.sum(hidden.reshape(own_seqs, LAT, D), axis=1)
     act_mat = w_act_v[...]
 
@@ -409,9 +436,8 @@
     pred = summed3(nn(split_rows(pooled), act_mat)) + b_act_v[...].astype(F32).reshape(1, AC)
     errors = pred - targets_v[...]
     squares = jnp.sum(valid * errors * errors, axis=0, keepdims=True)
-    d_pred = (total_seqs * AC / entries) * (valid * errors)
+    d_pred = valid * errors
     head_out[0:own_seqs] = valid * pred
-    head_out[own_seqs : own_seqs + 8] = jnp.broadcast_to(entries, (8, AC))
     d_act = lax.dot_general(
         pooled, d_pred, (((0,), (0,)), ((), ())), precision=highest, preferred_element_type=F32
     ).astype(BF)
@@ -429,11 +455,11 @@
 
     def core_send(chunk):
         at = pl.ds(first_row[chunk], CHUNKS[chunk])
-        live[chunk] = [remote(oth.at[at], rcv.at[at], core)]
+        live[chunk] = [remote(lambda: (oth.at[at], rcv.at[at]), core)]
 
     def received(chunk):
         for copy in live[chunk]:
-            copy.wait_recv()
+            copy().wait_recv()
         live[chunk] = []
 
     def scatter(chunk):
@@ -442,18 +468,21 @@
         snd[at, :] = (own[at, :].astype(F32) + rcv[at, :].astype(F32)).astype(BF)
         size = CHUNKS[chunk] // radices[0]
         here = pl.ds(first_piece[chunk], size)
-        for offset in range(1, radices[0]):
-            begin = first_row[chunk] + flip(digits[0], offset) * size
-            src = snd.at[pl.ds(pl.multiple_of(begin, 16), size)]
-            live[chunk].append(remote(src, rs_r.at[offset - 1, here], partner(0, offset)))
+        for offset in far_first(radices[0]):
+            piece = pl.ds(piece_of[size][offset], size)
+
+            def ends(piece=piece, offset=offset):
+                return snd.at[at].at[piece], rs_r.at[offset - 1, here]
+
+            live[chunk].append(remote(ends, partner(0, offset)))
 
     def share_on(chunk, level):
         received(chunk)
         size = CHUNKS[chunk] // radices[0]
         here = pl.ds(first_piece[chunk], size)
         if level == 1:
-            begin = pl.multiple_of(first_row[chunk] + digits[0] * size, 16)
-            mine = snd[pl.ds(begin, size), :].astype(F32)
+            whole = snd.at[pl.ds(first_row[chunk], CHUNKS[chunk])]
+            mine = whole[pl.ds(piece_of[size][0], size), :].astype(F32)
             got = [rs_r[at, here, :].astype(F32) for at in range(radices[0] - 1)]
         else:
             mine = part[level - 2, here, :].astype(F32)
@@ -462,14 +491,18 @@
         if level < len(radices):
             part[level - 1, here, :] = total
             for offset in range(1, radices[level]):
-                dst = full_r.at[level - 1, offset - 1, here]
-                live[chunk].append(remote(part.at[level - 1, here], dst, partner(level, offset)))
+
+                def ends(offset=offset):
+                    return part.at[level - 1, here], full_r.at[level - 1, offset - 1, here]
+
+                live[chunk].append(remote(ends, partner(level, offset)))
             return
-        mine_at = pl.ds(pl.multiple_of(digits[0] * size, 16), size)
+        mine_at = pl.ds(piece_of[size][0], size)
         fins[chunk][mine_at, :] = total
-        for offset in range(1, radices[0]):
-            piece = fins[chunk].at[mine_at]
-            live[chunk].append(remote(piece, piece, partner(0, offset)))
+        for offset in far_first(radices[0]):
+            live[chunk].append(
+                remote(lambda: (fins[chunk].at[mine_at], fins[chunk].at[mine_at]), partner(0, offset))
+            )
 
     last = len(radices)
 
@@ -494,7 +527,7 @@
         d_up = tn(kv["rows_m"], d_upper)
         put(chunk, 0, d_up[:, 0:128], d_up[:, 256:384])
         put(chunk, 128, d_up[:, 128:256], d_up[:, 384:512])
-        put(chunk, 256, d_down[0:256], d_down[256:512])
+        put(chunk + 1, 0, d_down[0:256], d_down[256:512])
         return d_middle
 
     def back_attn(d_middle, layer, chunk):
@@ -523,30 +556,34 @@
         put(chunk, 192, d_out[0:64], d_out[64:128])
         return d_input
 
-    put(0, 512, d_act, d_act)
+    put(6, 128, d_act, d_act)
     upstream = back_mlp(upstream, 1, 0)
-    core_send(0)
-    upstream = back_attn(upstream, 1, 1)
-    core_send(1)
-    scatter(0)
-    upstream = back_mlp(upstream, 0, 2)
-    core_send(2)
-    scatter(1)
-    upstream = back_attn(upstream, 0, 3)
-    share_on(0, 1)
-    scatter(2)
+    apart(core_send, 0)
+    apart(core_send, 1)
+    apart(entries_step, 1)
+    upstream = back_attn(upstream, 1, 2)
+    apart(core_send, 2)
+    apart(scatter, 0)
+    upstream = back_mlp(upstream, 0, 3)
+    apart(core_send, 3)
+    apart(core_send, 4)
+    apart(scatter, 1)
+    upstream = back_attn(upstream, 0, 5)
+    apart(core_send, 5)
+    for chunk in (2, 3, 4):
+        apart(scatter, chunk)
 
     grad_stem = upstream.astype(BF)
     d_out_t = nt(stem_wo, grad_stem).astype(BF)
     d_out = nt(grad_stem, stem_wo).astype(BF)
     d_stem_wo = tn(stem_out, grad_stem)
-    put(3, 256, d_stem_wo[0:64], d_stem_wo[64:128])
+    put(6, 0, d_stem_wo[0:64], d_stem_wo[64:128])
     mixed_heads = jnp.transpose(
         mixed_all.reshape(own_seqs, HEADS, LAT, D), (1, 0, 2, 3)
     ).reshape(HEADS * rows, D)
     d_wv = nn(heads_beside(d_out_t), mixed_heads)
-    put(3, 320, d_wv[0:64], d_wv[64:128])
-    core_send(3)
+    put(6, 64, d_wv[0:64], d_wv[64:128])
+    apart(core_send, 6)
     diag_b = diag_heads.astype(BF).reshape(1, HEADS, LAT, D)
     d_diag = (d_out.reshape(own_seqs, 1, LAT, D) * diag_b).reshape(own_seqs, D, D)
     back_v = nn(d_diag.reshape(own_seqs * D, D), wv_t).reshape(own_seqs, D, D)
@@ -568,6 +605,9 @@
         ds_v[:, lanes] = d_scores
         d_fold += nn(d_scores, next_v[at, 0:D])
 
+    apart(scatter, 5)
+    apart(scatter, 6)
+
     d_fold_b = d_fold.astype(BF)
     d_wk = nn(q_diag.astype(F32).T.astype(BF), d_fold_b)
     d_q = nt(d_fold_b, wk_t) * diag_heads
@@ -577,39 +617,29 @@
     gain_rows = jnp.sum(gain_sum + d_fold * fold, axis=0, keepdims=True)
     small_v[16:17, :] = gain_rows / stem_gain
     small_v[23:24, :] = jnp.sum(d_pred, axis=0, keepdims=True)
-    square_top = squares.astype(BF).astype(F32)
-    small_v[24:25, :] = square_top
-    small_v[25:26, :] = squares - square_top
-    tail_s[0, 0:64, :] = d_wk[0:64].astype(BF)
-    tail_s[0, 64:80, :] = d_q.astype(BF)
-    tail_s[1, 0:64, :] = d_wk[64:128].astype(BF)
-    tail_s[1, 64:80, :] = jnp.concatenate([d_q[:, 64:], d_q[:, :64]], axis=1).astype(BF)
-    for place, begin in ((0, 0), (1, 2)):
-        for layer in range(LAYERS):
-            row = 26 + 2 * layer
-            src = 32 + 4 * layer + begin
-            small_v[row : row + 2, :] = small_v[src : src + 2, :]
-        small_v[30:32, :] = jnp.zeros((2, D), F32)
-        tail_s[place, 80:112, :] = small_v[0:32, :].astype(BF)
-    tail_live = [remote(tail_s.at[1], tail_r.at[0], core)]
-
-    def tail_step(level):
-        for copy in tail_live:
-            copy.wait_recv()
-        tail_live.clear()
-        first = 1 + sum(radices[: level - 1]) - (level - 1)
-        count = 1 if level == 0 else radices[level - 1] - 1
-        begin = 0 if level == 0 else first
-        mine = tail_s[0 if level == 0 else level + 1].astype(F32)
-        total = tree(mine, [tail_r[begin + at].astype(F32) for at in range(count)])
-        if level == last:
-            return total
-        tail_s[level + 2] = total.astype(BF)
-        nxt = 1 + sum(radices[:level]) - level
-        for offset in range(1, radices[level]):
-            dst = tail_r.at[nxt + offset - 1]
-            tail_live.append(remote(tail_s.at[level + 2], dst, partner(level, offset)))
-        return None
+    small_v[24:25, :] = squares
+    for layer in range(LAYERS):
+        small_v[25 + 2 * layer : 27 + 2 * layer, :] = small_v[32 + 4 * layer : 34 + 4 * layer, :]
+    small_v[29:32, :] = jnp.zeros((3, D), F32)
+    shared = small_v[0:32, :]
+    d_q_other = jnp.concatenate([d_q[:, 64:], d_q[:, :64]], axis=1)
+    put(7, 0, d_wk[0:64], d_wk[64:128])
+    put(7, 64, d_q, d_q_other)
+    put(7, 80, shared, shared)
+    for layer in range(LAYERS):
+        small_v[25 + 2 * layer : 27 + 2 * layer, :] = small_v[34 + 4 * layer : 36 + 4 * layer, :]
+    oth[first_row[7] + 96 : first_row[7] + 112, :] = small_v[16:32, :].astype(BF)
+    own[first_row[7] + 112 : first_row[7] + 128, :] = jnp.zeros((16, D), BF)
+    oth[first_row[7] + 112 : first_row[7] + 128, :] = jnp.zeros((16, D), BF)
+    apart(core_send, 7)
+
+    for level in range(2, last):
+        apart(entries_step, level)
+    entries = jnp.sum(entries_step(last)[0:1], axis=1, keepdims=True)
+    total_seqs = own_seqs * lax.axis_size("dp") * lax.axis_size("mp")
+    factor = total_seqs * AC / entries
+    head_out[own_seqs : own_seqs + 8] = jnp.broadcast_to(entries, (8, AC))
+    head_out[own_seqs + 8 : own_seqs + 16] = jnp.broadcast_to(factor, (8, AC))
 
     fold_g = (fold * stem_gain).astype(BF)
     fold_side = jnp.concatenate([fold_g, nn(fold_g, mean_mat).astype(BF)], axis=1)
@@ -624,38 +654,43 @@
         scaled = both_grads[:, :D]
         unit = unit_v[at, :]
         slope_mean = nn((scaled * unit).astype(BF), mean_mat)
-        grad_tokens[at, :] = inv_v[at, :] * (scaled - both_grads[:, D:] - unit * slope_mean)
-
-    steps = [
-        lambda: share_on(1, 1),
-        lambda: scatter(3),
-        lambda: tail_step(0),
-        lambda: share_on(2, 1),
-        lambda: share_on(0, 2),
-        lambda: share_on(3, 1),
-        lambda: tail_step(1),
-        lambda: share_on(1, 2),
-    ]
+        grad_tokens[at, :] = (factor * inv_v[at, :]) * (scaled - both_grads[:, D:] - unit * slope_mean)
+
+    order = (
+        (1, share_on, 0, 1),
+        (2, scatter, 7),
+        (3, share_on, 1, 1),
+        (5, share_on, 2, 1),
+        (7, share_on, 3, 1),
+        (8, share_on, 4, 1),
+        (8, share_on, 5, 1),
+        (8, share_on, 0, 2),
+        (8, share_on, 6, 1),
+        (8, share_on, 1, 2),
+        (8, share_on, 7, 1),
+        (8, share_on, 2, 2),
+        (8, share_on, 3, 2),
+        (8, share_on, 4, 2),
+        (8, share_on, 5, 2),
+        (8, share_on, 6, 2),
+        (8, share_on, 7, 2),
+    )
     for seq in range(own_seqs):
+        for place, *step in order:
+            if place == seq:
+                apart(*step)
         token_grads(seq)
-        if seq < len(steps):
-            steps[seq]()
-    for step in steps[own_seqs:]:
-        step()
-    share_on(2, 2)
-    share_on(3, 2)
+    for place, *step in order:
+        if place >= own_seqs:
+            apart(*step)
     for level in range(3, last + 1):
         for chunk in range(len(CHUNKS)):
-            share_on(chunk, level)
-    for level in range(2, last):
-        tail_step(level)
-    total = tail_step(last)
-    tail_out[...] = total
-    wq_out[...] = tn(total[64:80, 0:64].astype(BF), latent)
+            apart(share_on, chunk, level)
     for chunk in range(len(CHUNKS)):
-        received(chunk)
+        apart(received, chunk)
+    wq_out[...] = tn(fin_h[64:80, 0:64], latent)
     for copy in sends:
-        copy.wait_send()
+        copy().wait_send()
 
 
 def split_kernel(
@@ -664,7 +699,10 @@
     fin_b,
     fin_c,
     fin_d,
-    tail,
+    fin_e,
+    fin_f,
+    fin_g,
+    fin_h,
     wq_in,
     head,
     actions,
@@ -690,28 +728,31 @@
     copy = pltpu.make_async_copy(grad_tokens, d_tokens, sem)
     copy.start()
     own_seqs = actions.shape[0]
-    for layer, mlp, attn in ((1, fin_a, fin_b), (0, fin_c, fin_d)):
-        d_up[layer, :, 0:128] = mlp[0:128, :].astype(F32)
-        d_up[layer, :, 128:256] = mlp[128:256, :].astype(F32)
-        d_down[layer] = mlp[256:512, :].astype(F32)
+    factor = head[own_seqs + 8 : own_seqs + 9, :]
+    for layer, up, down, attn in ((1, fin_a, fin_b, fin_c), (0, fin_d, fin_e, fin_f)):
+        d_up[layer, :, 0:128] = up[0:128, :].astype(F32) * factor
+        d_up[layer, :, 128:256] = up[128:256, :].astype(F32) * factor
+        d_down[layer] = down[...].astype(F32) * factor
         for place in range(3):
-            d_qkv[layer, place] = attn[64 * place : 64 * place + 64, :].astype(F32)
-        d_out[layer] = attn[192:256, :].astype(F32)
-        d_b_up[layer : layer + 1, 0:128] = tail[106 + 2 * layer : 107 + 2 * layer, :]
-        d_b_up[layer : layer + 1, 128:256] = tail[107 + 2 * layer : 108 + 2 * layer, :]
-    d_act[...] = fin_a[512:640, :].astype(F32)
-    d_stem_wo[...] = fin_d[256:320, :].astype(F32)
-    d_stem_wkv[1] = fin_d[320:384, :].astype(F32)
-    d_stem_wkv[0] = tail[0:64, :]
-    d_stem_wq[...] = wq_in[...]
-    d_latent[...] = tail[80:96, :]
-    d_stem_norm[...] = tail[96:97, :].reshape(D)
-    d_norm_attn[...] = tail[97:99, :]
-    d_norm_mlp[...] = tail[99:101, :]
-    d_b_down[...] = tail[101:103, :]
-    d_b_act[...] = tail[103:104, :].reshape(D)
+            d_qkv[layer, place] = attn[64 * place : 64 * place + 64, :].astype(F32) * factor
+        d_out[layer] = attn[192:256, :].astype(F32) * factor
+    d_act[...] = fin_g[128:256, :].astype(F32) * factor
+    d_stem_wo[...] = fin_g[0:64, :].astype(F32) * factor
+    d_stem_wkv[1] = fin_g[64:128, :].astype(F32) * factor
+    d_stem_wkv[0] = fin_h[0:64, :].astype(F32) * factor
+    tail = fin_h[64:128, :].astype(F32) * factor
+    for layer in range(LAYERS):
+        d_b_up[layer : layer + 1, 0:128] = tail[41 + 2 * layer : 42 + 2 * layer, :]
+        d_b_up[layer : layer + 1, 128:256] = tail[42 + 2 * layer : 43 + 2 * layer, :]
+    d_stem_wq[...] = factor * wq_in[...]
+    d_latent[...] = tail[16:32, :]
+    d_stem_norm[...] = tail[32:33, :].reshape(D)
+    d_norm_attn[...] = tail[33:35, :]
+    d_norm_mlp[...] = tail[35:37, :]
+    d_b_down[...] = tail[37:39, :]
+    d_b_act[...] = tail[39:40, :].reshape(D)
     actions[...] = head[0:own_seqs, :]
-    squares = jnp.sum(tail[104:105, :] + tail[105:106, :], axis=1, keepdims=True)
+    squares = jnp.sum(fin_h[64:128, :].astype(F32)[40:41, :], axis=1, keepdims=True)
     loss = squares / head[own_seqs : own_seqs + 1, :]
     masked_loss[...] = loss.reshape(D)
     copy.wait()
@@ -747,21 +788,29 @@
     vmem = pl.BlockSpec(memory_space=pltpu.VMEM)
     hbm = pl.BlockSpec(memory_space=pltpu.HBM)
     total_rows = sum(CHUNKS)
-    pieces = total_rows // radices[0]
     wide = max(radices) - 1
-    n_remote = 8 + 1 + spread + len(CHUNKS) * (1 + spread + radices[0] - 1) + 1 + spread
+
+    def summing(count_rows, dtype):
+        pieces = count_rows // radices[0]
+        return [
+            *[pltpu.VMEM((count_rows, D), dtype)] * 4,
+            pltpu.VMEM((wide, pieces, D), dtype),
+            pltpu.VMEM((last - 1, pieces, D), dtype),
+            pltpu.VMEM((last - 1, wide, pieces, D), dtype),
+        ]
+
+    n_remote = 8 + 1 + spread + len(CHUNKS) * (1 + spread + radices[0] - 1)
     shape = jax.ShapeDtypeStruct
     main = pl.pallas_call(
         functools.partial(main_kernel, radices),
         out_shape=[
             shape((count, D), F32),
             *[shape((size, D), BF) for size in CHUNKS],
-            shape((TAIL, D), F32),
             shape((64, D), F32),
-            shape((own_seqs + 8, AC), F32),
+            shape((own_seqs + 16, AC), F32),
         ],
         in_specs=[hbm] * len(args),
-        out_specs=[vmem] * 8,
+        out_specs=[vmem] * (3 + len(CHUNKS)),
         scratch_shapes=[
             pltpu.VMEM((count, D), BF),
             pltpu.VMEM((D,), BF),
@@ -790,15 +839,7 @@
             pltpu.VMEM((40, D), F32),
             pltpu.VMEM((1 + last, 8, AC), F32),
             pltpu.VMEM((1 + spread, 8, AC), F32),
-            pltpu.VMEM((total_rows, D), BF),
-            pltpu.VMEM((total_rows, D), BF),
-            pltpu.VMEM((total_rows, D), BF),
-            pltpu.VMEM((total_rows, D), BF),
-            pltpu.VMEM((wide, pieces, D), BF),
-            pltpu.VMEM((last - 1, pieces, D), BF),
-            pltpu.VMEM((last - 1, wide, pieces, D), BF),
-            pltpu.VMEM((2 + last, TAIL, D), BF),
-            pltpu.VMEM((1 + spread, TAIL, D), BF),
+            *summing(total_rows, BF),
             pltpu.SemaphoreType.DMA((len(args),)),
             pltpu.SemaphoreType.DMA((n_remote,)),
             pltpu.SemaphoreType.DMA((n_remote,)),
@@ -858,7 +899,7 @@
     result = pl.pallas_call(
         split_kernel,
         out_shape=outs,
-        in_specs=[pl.BlockSpec(memory_space=pl.ANY)] + [vmem] * 7,
+        in_specs=[pl.BlockSpec(memory_space=pl.ANY)] + [vmem] * (2 + len(CHUNKS)),
         out_specs=out_specs,
         scratch_shapes=[pltpu.SemaphoreType.DMA],
         compiler_params=pltpu.CompilerParams(vmem_limit_bytes=20 * 2**20),

time: 40.7 us -> 35.5 us (0.87)
  Pallas kernels: 39.9 us -> 34.7 us
    pallas_call x1, Pallas kernels: 37.9 us -> 32.7 us  [on_device(): pl.pallas_call(functools.partial(main_kernel, radices), out_shape=[shape(...]
where the time goes in v3:
time: 35.5 us; the launch traced here: 35.4 us
  Pallas kernels  34.7 us (98%)
  between operations  0.67 us (2%)
    pallas_call x1, Pallas kernels, on_device(): pl.pallas_call(functools.partial(main_kernel, radices), out_shape=[shape(...  32.7 us
    pallas_call x1, Pallas kernels, on_device(): pl.pallas_call(split_kernel, out_shape=outs, in_specs=[pl.BlockSpec(memor...  2.01 us

profile of v3, /device:TPU:0, one launch (start us, length us, event | category | flops | bytes accessed | tf_op | source)
XLA Modules:
  0.0 35.4 jit_solution(5826316018966606017)
XLA Ops:
  0.7 32.7 %stem_trunk_head.1 = (f32[2048,128]{1,0:T(8,128)S(1)}, bf16[256,128]{1,0:T(8,128)(2,1)S(1)}, bf16[256,128]{1,0:T(8,128)(2,1)S(1)}, bf16[256,128]{1,0:T(8,128)(2,...) custom-call(bf16[2048,128]{1,0:T(8,128)(2,1)} %tokens_h.1, ...), custom_call_target="tpu_custom_call" | custom-call | tf_op jit(solution)/shard_map/stem_trunk_head/pallas_call | solution.py:804
  33.4 2.0 %split_results.1 = (f32[8,128]{1,0:T(8,128)}, f32[128]{0:T(128)}, f32[2048,128]{1,0:T(8,128)}, f32[128]{0:T(128)}, f32[16,128]{1,0:T(8,128)}, /*index=5*/f32[64,...) custom-call(f32[2048,128]{1,0:T(8,128)S(1)} %get-tuple-element.47.gr, ...), custom_call_target="tpu_custom_call" | custom-call | tf_op jit(solution)/shard_map/split_results/pallas_call | solution.py:899

commit v4 on v3

v4 whole, which is shorter than its diff:
```python
import functools
import math

import jax
import jax.numpy as jnp
from jax import lax
from jax.experimental import pallas as pl
from jax.experimental.pallas import tpu as pltpu
from jax.sharding import PartitionSpec as P

HD = 16
LAT = 16
SEQ_LEN = 256
SPAN = 16
JOINTS = 8
HEADS = 8
D = 128
FF = 512
AC = 128
LAYERS = 2

F32 = jnp.float32
BF = jnp.bfloat16
MESH = pl.DeviceIdType.MESH
epsilon = 1e-05
highest = lax.Precision.HIGHEST

CHUNKS = (512, 256, 512, 256, 384)


def nn(left, right):
    return jnp.dot(left, right, preferred_element_type=F32)


def nt(left, right):
    return lax.dot_general(left, right, (((1,), (1,)), ((), ())), preferred_element_type=F32)


def tn(left, right):
    return lax.dot_general(left, right, (((0,), (0,)), ((), ())), preferred_element_type=F32)


def iota(shape, axis):
    return lax.broadcasted_iota(jnp.int32, shape, axis)


def radices_of(count):
    found = []
    while count > 1:
        radix = 8 if count % 8 == 0 else 4 if count % 4 == 0 else 2
        found.append(radix)
        count //= radix
    return found


def flip(digit, offset):
    flipped = digit
    for bit in (1, 2, 4):
        if offset & bit:
            flipped = flipped + bit - 2 * bit * ((digit // bit) % 2)
    return flipped


def far_first(radix):
    return sorted(range(1, radix), key=lambda offset: -bin(offset).count("1"))


def norm_rows(values_in, gain_vec):
    mean_rows = jnp.mean(values_in, axis=-1, keepdims=True)
    centred = values_in - mean_rows
    variance = jnp.mean(centred * centred, axis=-1, keepdims=True)
    inv_rows = lax.rsqrt(variance + epsilon)
    unit_rows = centred * inv_rows
    return unit_rows * gain_vec, unit_rows, inv_rows


def norm_back(upstream, unit_rows, inv_rows, gain_vec):
    scaled = upstream * gain_vec
    inner = (
        scaled
        - jnp.mean(scaled, axis=-1, keepdims=True)
        - unit_rows * jnp.mean(scaled * unit_rows, axis=-1, keepdims=True)
    )
    return inv_rows * inner


def split_rows(values_in):
    first = values_in.astype(BF).astype(F32)
    rest = values_in - first
    second = rest.astype(BF).astype(F32)
    return jnp.concatenate([first, second, rest - second], axis=0).astype(BF)


def main_kernel(
    radices,
    tokens_h,
    stem_norm_h,
    stem_latent_h,
    stem_wq_h,
    stem_wkv_h,
    stem_wo_h,
    norm_attn_h,
    w_qkv_h,
    w_out_h,
    norm_mlp_h,
    w_up_h,
    b_up_h,
    w_down_h,
    b_down_h,
    w_act_h,
    b_act_h,
    span_len_h,
    joint_mask_h,
    targets_h,
    *refs,
):
    count = 18
    results, staged = refs[:count], refs[count : 2 * count]
    (
        actions,
        masked_loss,
        grad_tokens,
        d_stem_norm,
        d_latent_out,
        d_stem_wq,
        d_stem_wkv,
        d_stem_wo_out,
        d_norm_attn,
        d_qkv_out,
        d_out_out,
        d_norm_mlp,
        d_up_out,
        d_b_up,
        d_down_out,
        d_b_down,
        d_act_out,
        d_b_act,
    ) = staged
    (
        fin,
        x_v,
        stem_norm_v,
        stem_latent_v,
        wq_v,
        wkv_v,
        wo_v,
        norm_attn_v,
        wqkv_v,
        wout_v,
        norm_mlp_v,
        wup_v,
        bup_v,
        wdn_v,
        b_down_v,
        w_act_v,
        b_act_v,
        span_s,
        joint_v,
        targets_v,
        next_v,
        inv_v,
        e_v,
        ds_v,
        small_v,
        ent_v,
        ent_r,
        own,
        oth,
        rcv,
        snd,
        rs_r,
        part,
        full_r,
        in_sem,
        send_sem,
        recv_sem,
    ) = refs[2 * count :]
    dp, mp = lax.axis_index("dp"), lax.axis_index("mp")
    own_seqs = targets_h.shape[0]
    rows = own_seqs * LAT
    core = (dp, 1 - mp)
    digits = [(dp // math.prod(radices[:level])) % radix for level, radix in enumerate(radices)]

    places = {}

    def partner(level, offset):
        stride = math.prod(radices[:level])
        if (level, offset) not in places:
            digit = digits[level]
            places[level, offset] = (dp + (flip(digit, offset) - digit) * stride, mp)
        return places[level, offset]

    def apart(step, *given):
        pl.when(dp >= 0)(functools.partial(step, *given))

    barrier = pltpu.get_barrier_semaphore()
    greeted = [core]
    for level, radix in enumerate(radices):
        greeted += [partner(level, offset) for offset in range(1, radix)]
    for device in greeted:
        pl.semaphore_signal(barrier, inc=1, device_id=device, device_id_type=MESH)

    piece_of = {}
    for size in sorted({chunk // radices[0] for chunk in CHUNKS}):
        piece_of[size] = [
            pl.multiple_of(flip(digits[0], offset) * size, size) for offset in range(radices[0])
        ]
    recv_slots = [0]
    leaving = {}

    def left(send_slot):
        if send_slot in leaving:
            leaving.pop(send_slot)()

    def group(copies, extent, send_slot):
        left(send_slot)
        recv_slot = recv_slots[0]
        recv_slots[0] += 1

        def copy(src, dst, device):
            return pltpu.make_async_remote_copy(
                src_ref=src,
                dst_ref=dst,
                send_sem=send_sem.at[send_slot],
                recv_sem=recv_sem.at[recv_slot],
                device_id=device,
                device_id_type=MESH,
            )

        for src, dst, device in copies:
            copy(src, dst, device).start()
        leaving[send_slot] = lambda: copy(extent(), extent(), core).wait_send()
        return lambda: copy(extent(), extent(), core).wait_recv()

    local = {}
    pairs = (
        ("tokens", tokens_h, x_v),
        ("stem_norm", stem_norm_h, stem_norm_v),
        ("stem_latent", stem_latent_h, stem_latent_v),
        ("wq", stem_wq_h, wq_v),
        ("wkv", stem_wkv_h, wkv_v),
        ("wo", stem_wo_h, wo_v),
        ("wqkv", w_qkv_h, wqkv_v),
        ("wout", w_out_h, wout_v),
        ("wup", w_up_h, wup_v),
        ("wdn", w_down_h, wdn_v),
        ("norm_attn", norm_attn_h, norm_attn_v),
        ("norm_mlp", norm_mlp_h, norm_mlp_v),
        ("bup", b_up_h, bup_v),
        ("b_down", b_down_h, b_down_v),
        ("w_act", w_act_h, w_act_v),
        ("b_act", b_act_h, b_act_v),
        ("span", span_len_h, span_s),
        ("joint", joint_mask_h, joint_v),
        ("targets", targets_h, targets_v),
    )
    halves = ("wq", "wkv", "wo", "wqkv", "wout", "wup", "wdn", "bup")

    def load(place, name, src, dst):
        here = dst.at[0] if name in halves else dst
        return pltpu.make_async_copy(src, here, in_sem.at[place])

    for place, (name, src, dst) in enumerate(pairs):
        local[name] = functools.partial(load, place, name, src, dst)
        local[name]().start()

    head_mask = (
        (iota((HEADS, D, D), 2) // HD == iota((HEADS, D, D), 0)).astype(F32).astype(BF)
    )
    row_mask = (iota((HEADS, D, D), 1) // HD == iota((HEADS, D, D), 0)).astype(F32).astype(BF)
    diag_heads = (iota((D, D), 0) // LAT == iota((D, D), 1) // HD).astype(F32)
    block_add = jnp.where(iota((rows, rows), 0) // LAT == iota((rows, rows), 1) // LAT, 0.0, -1e30)
    mean_mat = jnp.full((D, D), 1.0 / D, BF)
    mean_twice = jnp.full((2 * D, D), 1.0 / D, BF)

    gathered = {}

    ent_slot = len(halves)
    ent_first = [1 + sum(radices[:level]) - level for level in range(len(radices))]

    def entries_step(level):
        pending.pop()()
        if level == 0:
            total = ent_v[0] + ent_r[0]
        else:
            first = ent_first[level - 1]
            total = tree(ent_v[level], [ent_r[first + at] for at in range(radices[level - 1] - 1)])
        if level == len(radices):
            return total
        ent_v[level + 1] = total
        first, others = ent_first[level], radices[level] - 1
        copies = [
            (ent_v.at[level + 1], ent_r.at[first + at], partner(level, at + 1))
            for at in range(others)
        ]
        pending.append(group(copies, lambda: ent_r.at[pl.ds(first, others)], ent_slot))
        return None

    def tree(mine, others):
        terms = [mine] + list(others)
        while len(terms) > 1:
            terms = [terms[at] + terms[at + 1] for at in range(0, len(terms), 2)]
        return terms[0]

    def wait_for(*names):
        for name in names:
            local[name]().wait()

    def wait_gathered(*names):
        for name in names:
            gathered[name]()

    def meet():
        pl.semaphore_wait(barrier, len(greeted))
        for name, src, dst in pairs:
            if name in halves:
                copies = [(src, dst.at[1], core)]
                extent = functools.partial(dst.at.__getitem__, 1)
                gathered[name] = group(copies, extent, halves.index(name))

    apart(meet)

    apart(wait_for, "span", "joint")
    spans = jnp.zeros((own_seqs, AC), jnp.int32)
    for seq in range(own_seqs):
        spans = jnp.where(iota((own_seqs, AC), 0) == seq, span_s[seq], spans)
    joints = (joint_v[...] > 0).astype(F32).astype(BF)
    spread = (iota((JOINTS, AC), 1) % JOINTS == iota((JOINTS, AC), 0)).astype(F32).astype(BF)
    valid = jnp.where(iota((own_seqs, AC), 1) // JOINTS < spans, nn(joints, spread), 0.0)
    ent_v[0] = jnp.broadcast_to(jnp.sum(valid, axis=0, keepdims=True), (8, AC))
    pending = []

    def entries_begin():
        copies = [(ent_v.at[0], ent_r.at[0], core)]
        pending.append(group(copies, lambda: ent_r.at[0], ent_slot))

    apart(entries_begin)

    apart(wait_for, "tokens", "stem_norm")
    stem_gain = stem_norm_v[...].astype(F32).reshape(1, D)
    half = own_seqs * SEQ_LEN // 2
    for start in (0, half):
        at = pl.ds(start, half)
        raw = x_v[at, :]
        centred = raw.astype(F32) - nn(raw, mean_mat)
        square = centred * centred
        upper = square.astype(BF)
        lower = (square - upper.astype(F32)).astype(BF)
        inv = lax.rsqrt(nn(jnp.concatenate([upper, lower], axis=1), mean_twice) + epsilon)
        unit = centred * inv
        inv_v[at, :] = inv
        next_v[at, 0:D] = (unit * stem_gain).astype(BF)
        next_v[at, D : 2 * D] = jnp.ones((half, D), BF)

    def both(ref, *index):
        return jnp.concatenate([ref[(0,) + index], ref[(1,) + index]], axis=0)

    def heads_below(matrix):
        return (matrix[None] * head_mask).reshape(HEADS * D, D)

    def heads_beside(matrix):
        return jnp.concatenate([matrix * row_mask[head] for head in range(HEADS)], axis=1)

    def lanes_beside(cube):
        return jnp.concatenate([cube[head] for head in range(HEADS)], axis=1)

    apart(wait_for, "stem_latent", "wq", "wkv")
    apart(wait_for, "wo")
    apart(wait_gathered, "wq", "wkv", "wo")
    latent = stem_latent_v[...]
    wq_t = both(wq_v)
    wk_t, wv_t = both(wkv_v, 0), both(wkv_v, 1)
    stem_q = nt(latent, wq_t).astype(BF).astype(F32) * HD ** (-0.5)
    q_diag = (jnp.concatenate([stem_q] * HEADS, axis=0) * diag_heads).astype(BF)
    fold = nn(q_diag, wk_t)
    fold_b = fold.astype(BF)
    apart(entries_step, 0)
    seq_rows = [pl.ds(seq * SEQ_LEN, SEQ_LEN) for seq in range(own_seqs)]
    scores = [nt(fold_b, next_v[at, 0:D]) for at in seq_rows]
    apart_wo = both(wo_v)
    wv_cols = wv_t.T
    stem_mats = nn(heads_below(wv_cols), apart_wo).astype(BF)
    mixed, shares = [], []
    for seq, at in enumerate(seq_rows):
        tops = jnp.max(scores[seq], axis=1, keepdims=True)
        probs = jnp.exp(scores[seq] - tops).astype(BF)
        e_v[:, seq * SEQ_LEN : (seq + 1) * SEQ_LEN] = probs
        both_sums = nn(probs, next_v[at, :])
        share = 1.0 / both_sums[:, D:]
        shares.append(share)
        mixed.append((both_sums[:, :D] * share).astype(BF))

    def by_head(head):
        return jnp.concatenate([part[head * LAT : (head + 1) * LAT] for part in mixed], axis=0)

    mixed_heads = [by_head(head) for head in range(HEADS)]
    latent_f = latent.astype(F32)
    hidden = jnp.concatenate([latent_f] * own_seqs, axis=0) + nn(
        jnp.concatenate(mixed_heads, axis=1), stem_mats
    )
    stem_wo = apart_wo

    def stem_heads_out():
        below = nt(jnp.concatenate(mixed_heads, axis=0), wv_t).reshape(HEADS, rows, D)
        return jnp.sum(below * head_mask.astype(F32), axis=0).astype(BF)


    apart(wait_for, "norm_attn", "norm_mlp", "b_down", "w_act", "b_act", "targets")
    apart(wait_for, "wqkv", "wout", "wup", "wdn", "bup")
    apart(wait_gathered, "wqkv", "wout", "wup", "wdn", "bup")
    gain_attn = norm_attn_v[...].astype(F32)
    gain_mlp = norm_mlp_v[...].astype(F32)
    down_bias = b_down_v[...].astype(F32)
    up_bias = jnp.concatenate([bup_v[0], bup_v[1]], axis=1).astype(F32)

    def row_blocks_beside(matrix):
        return jnp.concatenate([matrix[head * D : (head + 1) * D] for head in range(HEADS)], axis=1)

    def lane_blocks_below(matrix):
        return jnp.concatenate(
            [matrix[:, head * D : (head + 1) * D] for head in range(HEADS)], axis=0
        )

    def trunk_forward(residual, layer):
        gain_a, gain_m = gain_attn[layer : layer + 1], gain_mlp[layer : layer + 1]
        qkv = jnp.concatenate([both(wqkv_v, layer, part_at) for part_at in range(3)], axis=0)
        out_mat = both(wout_v, layer)
        out_mats = nn(heads_below(out_mat.T), qkv[2 * D :]).astype(BF)
        up_mat = jnp.concatenate([wup_v[0, layer], wup_v[1, layer]], axis=1)
        down_mat = both(wdn_v, layer)
        normed, unit_a, inv_a = norm_rows(residual, gain_a)
        rows_a = normed.astype(BF)
        flat = nt(rows_a, qkv).astype(BF)
        queries = flat[:, :D] * jnp.asarray(HD ** (-0.5), BF)
        keys = flat[:, D : 2 * D]
        scores = nt(heads_below(keys), queries).reshape(HEADS, rows, rows) + block_add[None]
        moved_t = row_blocks_beside(nt(out_mats, rows_a).astype(BF))
        exped = jnp.exp(scores - jnp.max(scores, axis=1, keepdims=True))
        probs = exped / jnp.sum(exped, axis=1, keepdims=True)
        probs_b = probs.astype(BF)
        probs_flat = probs_b.reshape(HEADS * rows, rows)
        middle = residual + nn(moved_t, probs_flat).T
        keys_t = nt(qkv[D : 2 * D], rows_a).astype(BF) * jnp.asarray(HD ** (-0.5), BF)
        values_t = nt(qkv[2 * D :], rows_a).astype(BF)
        normed_m, unit_m, inv_m = norm_rows(middle, gain_m)
        rows_m = normed_m.astype(BF)
        up_rows = nn(rows_m, up_mat) + up_bias[layer : layer + 1]
        attended_t = nn(heads_beside(values_t), probs_flat).astype(BF)
        moved = lane_blocks_below(nt(rows_a, out_mats).astype(BF))
        cdf = 0.5 + 0.5 * lax.erf(up_rows * (0.5**0.5))
        slope = cdf + up_rows * (jnp.exp(-0.5 * up_rows * up_rows) * 0.3989422804014327)
        hidden_act = (up_rows * cdf).astype(BF)
        output = middle + nn(hidden_act, down_mat) + down_bias[layer : layer + 1]
        saved = dict(
            gain_a=gain_a, gain_m=gain_m, qkv=qkv, out_mat=out_mat, up_mat=up_mat,
            down_mat=down_mat, unit_a=unit_a, inv_a=inv_a, rows_a=rows_a, queries=queries,
            keys_t=keys_t, moved=moved, probs=probs, probs_b=probs_b, attended_t=attended_t,
            unit_m=unit_m, inv_m=inv_m, rows_m=rows_m, slope=slope, hidden_act=hidden_act,
        )
        return output, saved

    kept = []
    for layer in range(LAYERS):
        hidden, saved = trunk_forward(hidden, layer)
        kept.append(saved)
        if layer == 0:
            stem_out = stem_heads_out()

    pooled = jnp.sum(hidden.reshape(own_seqs, LAT, D), axis=1)
    act_mat = w_act_v[...]

    def summed3(stacked):
        return stacked[0:own_seqs] + stacked[own_seqs : 2 * own_seqs] + stacked[2 * own_seqs :]

    pred = summed3(nn(split_rows(pooled), act_mat)) + b_act_v[...].astype(F32).reshape(1, AC)
    errors = pred - targets_v[...]
    squares = jnp.sum(valid * errors * errors, axis=0, keepdims=True)
    d_pred = valid * errors
    actions[...] = valid * pred

    def act_grad():
        top, rest = pooled.astype(BF), d_pred.astype(BF)
        left = jnp.concatenate([top.astype(F32), pooled - top.astype(F32), top.astype(F32)], axis=0)
        right = jnp.concatenate(
            [rest.astype(F32), rest.astype(F32), d_pred - rest.astype(F32)], axis=0
        )
        return tn(left.astype(BF), right.astype(BF))

    d_pooled = summed3(nt(split_rows(d_pred), act_mat))
    upstream = jnp.broadcast_to(d_pooled[:, None, :], (own_seqs, LAT, D)).reshape(rows, D)

    first_row = [sum(CHUNKS[:chunk]) for chunk in range(len(CHUNKS))]
    first_piece = [begin // radices[0] for begin in first_row]
    live = {}

    def put(chunk, offset, mine, others):
        at = pl.ds(first_row[chunk] + offset, mine.shape[0])
        own[at, :] = mine.astype(BF)
        oth[at, :] = others.astype(BF)

    def core_send(chunk):
        at = pl.ds(first_row[chunk], CHUNKS[chunk])
        live[chunk] = group([(oth.at[at], rcv.at[at], core)], lambda: rcv.at[at], chunk)

    def received(chunk):
        live.pop(chunk)()

    def scatter(chunk):
        received(chunk)
        at = pl.ds(first_row[chunk], CHUNKS[chunk])
        snd[at, :] = (own[at, :].astype(F32) + rcv[at, :].astype(F32)).astype(BF)
        size = CHUNKS[chunk] // radices[0]
        here = pl.ds(first_piece[chunk], size)
        copies = [
            (
                snd.at[at].at[pl.ds(piece_of[size][offset], size)],
                rs_r.at[offset - 1, here],
                partner(0, offset),
            )
            for offset in far_first(radices[0])
        ]
        live[chunk] = group(copies, lambda: rs_r.at[pl.ds(0, radices[0] - 1), here], chunk)

    def share_on(chunk, level):
        received(chunk)
        size = CHUNKS[chunk] // radices[0]
        here = pl.ds(first_piece[chunk], size)
        if level == 1:
            whole = snd.at[pl.ds(first_row[chunk], CHUNKS[chunk])]
            mine = whole[pl.ds(piece_of[size][0], size), :].astype(F32)
            got = [rs_r[at, here, :].astype(F32) for at in range(radices[0] - 1)]
        else:
            mine = part[level - 2, here, :].astype(F32)
            got = [full_r[level - 2, at, here, :].astype(F32) for at in range(radices[level - 1] - 1)]
        total = tree(mine, got).astype(BF)
        if level < len(radices):
            part[level - 1, here, :] = total
            others = radices[level] - 1
            copies = [
                (part.at[level - 1, here], full_r.at[level - 1, at, here], partner(level, at + 1))
                for at in range(others)
            ]
            live[chunk] = group(
                copies, lambda: full_r.at[level - 1, pl.ds(0, others), here], chunk
            )
            return
        mine_at = pl.ds(piece_of[size][0], size)
        done = fin.at[pl.ds(first_row[chunk], CHUNKS[chunk])]
        done[mine_at, :] = total
        copies = [
            (done.at[mine_at], done.at[mine_at], partner(0, offset))
            for offset in far_first(radices[0])
        ]
        rest = pl.ds(first_row[chunk], (radices[0] - 1) * size)
        live[chunk] = group(copies, lambda: fin.at[rest], chunk)

    last = len(radices)

    def back_mlp(upstream, layer, chunk):
        kv = kept[layer]
        grad_top = upstream.astype(BF)
        small_v[16 + 5 + layer : 16 + 6 + layer, :] = jnp.sum(
            grad_top.astype(F32), axis=0, keepdims=True
        )
        d_hidden = nt(grad_top, kv["down_mat"])
        d_upper = (kv["slope"] * d_hidden).astype(BF)
        d_rows = nt(d_upper, kv["up_mat"])
        d_middle = upstream + norm_back(d_rows, kv["unit_m"], kv["inv_m"], kv["gain_m"])
        small_v[16 + 3 + layer : 16 + 4 + layer, :] = jnp.sum(
            d_rows * kv["unit_m"], axis=0, keepdims=True
        )
        d_bias = jnp.sum(d_upper.astype(F32), axis=0, keepdims=True)
        for block in range(4):
            row = 32 + 4 * layer + block
            small_v[row : row + 1, :] = d_bias[:, block * D : (block + 1) * D]
        d_down = tn(kv["hidden_act"], grad_top)
        d_up = tn(kv["rows_m"], d_upper)
        put(chunk, 0, d_up[:, 0:128], d_up[:, 256:384])
        put(chunk, 128, d_up[:, 128:256], d_up[:, 384:512])
        put(chunk, 256, d_down[0:256], d_down[256:512])
        return d_middle

    def back_attn(d_middle, layer, chunk):
        kv = kept[layer]
        grad_attn = d_middle.astype(BF)
        d_probs = nt(kv["moved"], grad_attn).reshape(HEADS, rows, rows)
        d_mixed = nt(grad_attn, kv["out_mat"]).astype(BF)
        probs = kv["probs"]
        weighted = probs * d_probs
        inner = jnp.sum(weighted, axis=1, keepdims=True)
        d_scores = (weighted - probs * inner).astype(BF)
        d_values = nn(lanes_beside(kv["probs_b"]), heads_below(d_mixed)).astype(BF)
        d_q_t = nn(heads_beside(kv["keys_t"]), d_scores.reshape(HEADS * rows, rows))
        d_keys = nn(lanes_beside(d_scores), heads_below(kv["queries"])).astype(BF)
        grads = jnp.concatenate([d_q_t.T.astype(BF), d_keys, d_values], axis=1)
        d_rows = nn(grads, kv["qkv"])
        small_v[16 + 1 + layer : 16 + 2 + layer, :] = jnp.sum(
            d_rows * kv["unit_a"], axis=0, keepdims=True
        )
        d_input = d_middle + norm_back(d_rows, kv["unit_a"], kv["inv_a"], kv["gain_a"])
        d_out = nn(kv["attended_t"], grad_attn)
        d_qkv = tn(grads, kv["rows_a"])
        for place in range(3):
            begin = place * D
            put(chunk, place * 64, d_qkv[begin : begin + 64], d_qkv[begin + 64 : begin + 128])
        put(chunk, 192, d_out[0:64], d_out[64:128])
        return d_input

    upstream = back_mlp(upstream, 1, 0)
    apart(core_send, 0)
    apart(entries_step, 1)
    upstream = back_attn(upstream, 1, 1)
    apart(core_send, 1)
    upstream = back_mlp(upstream, 0, 2)
    apart(core_send, 2)
    apart(scatter, 0)
    upstream = back_attn(upstream, 0, 3)
    apart(core_send, 3)
    apart(scatter, 1)
    apart(scatter, 2)

    grad_stem = upstream.astype(BF)
    back_flat = nt(grad_stem, stem_mats)
    back_v = [
        jnp.concatenate(
            [
                back_flat[seq * LAT : (seq + 1) * LAT, head * D : (head + 1) * D]
                for head in range(HEADS)
            ],
            axis=0,
        )
        for seq in range(own_seqs)
    ]
    gain_sum = jnp.zeros((D, D), F32)
    folds_v, d_all = [], []
    for seq, at in enumerate(seq_rows):
        gain_sum += back_v[seq] * mixed[seq].astype(F32)
        folds_v.append((back_v[seq] * shares[seq]).astype(BF))
        d_all.append(nt(folds_v[seq], next_v[at, 0:D]))
    for seq in range(own_seqs):
        lanes = slice(seq * SEQ_LEN, (seq + 1) * SEQ_LEN)
        probs = e_v[:, lanes].astype(F32)
        weighted = probs * d_all[seq]
        inner = jnp.sum(weighted, axis=1, keepdims=True) * shares[seq][:, 0:1]
        ds_v[:, lanes] = (weighted - probs * inner).astype(BF)
    d_out_t = nt(stem_wo, grad_stem).astype(BF)
    d_stem_wo = tn(stem_out, grad_stem)
    put(4, 0, d_stem_wo[0:64], d_stem_wo[64:128])
    d_wv = nn(heads_beside(d_out_t), jnp.concatenate(mixed_heads, axis=0))
    put(4, 64, d_wv[0:64], d_wv[64:128])
    d_act = act_grad()
    put(4, 128, d_act, d_act)
    d_fold = nn(ds_v[...], next_v[:, 0:D])
    apart(scatter, 3)

    d_fold_b = d_fold.astype(BF)
    d_wk = nn(q_diag.astype(F32).T.astype(BF), d_fold_b)
    d_q = nt(d_fold_b, wk_t) * diag_heads
    d_q = jnp.sum(d_q.reshape(HEADS, LAT, D), axis=0) * HD ** (-0.5)
    d_latent = jnp.sum(upstream.reshape(own_seqs, LAT, D), axis=0) + nn(d_q.astype(BF), wq_t)
    small_v[0:16, :] = d_latent
    gain_rows = jnp.sum(gain_sum + d_fold * fold, axis=0, keepdims=True)
    small_v[16:17, :] = gain_rows / stem_gain
    small_v[23:24, :] = jnp.sum(d_pred, axis=0, keepdims=True)
    small_v[24:25, :] = squares
    for layer in range(LAYERS):
        small_v[25 + 2 * layer : 27 + 2 * layer, :] = small_v[32 + 4 * layer : 34 + 4 * layer, :]
    small_v[29:32, :] = jnp.zeros((3, D), F32)
    shared = small_v[0:32, :]
    d_q_other = jnp.concatenate([d_q[:, 64:], d_q[:, :64]], axis=1)
    put(4, 256, d_wk[0:64], d_wk[64:128])
    put(4, 320, d_q, d_q_other)
    put(4, 336, shared, shared)
    for layer in range(LAYERS):
        small_v[25 + 2 * layer : 27 + 2 * layer, :] = small_v[34 + 4 * layer : 36 + 4 * layer, :]
    oth[first_row[4] + 352 : first_row[4] + 368, :] = small_v[16:32, :].astype(BF)
    own[first_row[4] + 368 : first_row[4] + 384, :] = jnp.zeros((16, D), BF)
    oth[first_row[4] + 368 : first_row[4] + 384, :] = jnp.zeros((16, D), BF)
    apart(core_send, 4)

    def hand_over(*places):
        for place in places:
            pltpu.make_async_copy(staged[place], results[place], in_sem.at[place]).start()

    fold_g = (fold * stem_gain).astype(BF)
    fold_side = jnp.concatenate([fold_g, nn(fold_g, mean_mat).astype(BF)], axis=1)

    def token_grads(seq):
        at = pl.ds(seq * SEQ_LEN, SEQ_LEN)
        lanes = slice(seq * SEQ_LEN, (seq + 1) * SEQ_LEN)
        left = jnp.concatenate([ds_v[:, lanes], e_v[:, lanes]], axis=0)
        value_g = (folds_v[seq].astype(F32) * stem_gain).astype(BF)
        value_side = jnp.concatenate([value_g, nn(value_g, mean_mat).astype(BF)], axis=1)
        both_grads = tn(left, jnp.concatenate([fold_side, value_side], axis=0))
        scaled = both_grads[:, :D]
        raw = x_v[at, :]
        unit = (raw.astype(F32) - nn(raw, mean_mat)) * inv_v[at, :]
        slope_mean = nn((scaled * unit).astype(BF), mean_mat)
        grad_tokens[at, :] = inv_v[at, :] * (scaled - both_grads[:, D:] - unit * slope_mean)

    order = (
        (2, scatter, 4),
        (3, share_on, 0, 1),
        (5, share_on, 1, 1),
        (8, share_on, 2, 1),
        (8, share_on, 3, 1),
        (8, share_on, 4, 1),
        (8, share_on, 0, 2),
    )
    for seq in range(own_seqs):
        for place, *step in order:
            if place == seq:
                apart(*step)
        token_grads(seq)
    for place, *step in order:
        if place >= own_seqs:
            apart(*step)

    for level in range(2, last):
        apart(entries_step, level)
    entries = jnp.sum(entries_step(last)[0:1], axis=1, keepdims=True)
    total_seqs = own_seqs * lax.axis_size("dp") * lax.axis_size("mp")
    factor = total_seqs * AC / entries
    grad_tokens[...] = grad_tokens[...] * factor

    apart(hand_over, 0, 2)
    for chunk, level in ((1, 2), (2, 2), (3, 2), (4, 2)):
        apart(share_on, chunk, level)
    for level in range(3, last + 1):
        for chunk in range(len(CHUNKS)):
            apart(share_on, chunk, level)

    def whole(chunk, begin, count):
        at = first_row[chunk] + begin
        return fin[at : at + count, :].astype(F32) * factor

    def finish(chunk):
        received(chunk)
        if chunk in (0, 2):
            layer = 1 if chunk == 0 else 0
            d_up_out[layer, :, 0:128] = whole(chunk, 0, 128)
            d_up_out[layer, :, 128:256] = whole(chunk, 128, 128)
            d_down_out[layer] = whole(chunk, 256, 256)
            if chunk == 2:
                hand_over(12, 14)
        if chunk in (1, 3):
            layer = 1 if chunk == 1 else 0
            for place in range(3):
                d_qkv_out[layer, place] = whole(chunk, 64 * place, 64)
            d_out_out[layer] = whole(chunk, 192, 64)
            if chunk == 3:
                hand_over(9, 10)
        if chunk == 4:
            d_stem_wo_out[...] = whole(4, 0, 64)
            d_stem_wkv[1] = whole(4, 64, 64)
            d_act_out[...] = whole(4, 128, 128)
            d_stem_wkv[0] = whole(4, 256, 64)
            d_latent_out[...] = whole(4, 336, 16)
            at = first_row[4]
            d_stem_wq[...] = tn(fin[at + 320 : at + 336, 0:64], latent) * factor
            rest = whole(4, 352, 16)
            d_stem_norm[...] = rest[0:1].reshape(D)
            d_norm_attn[...] = rest[1:3]
            d_norm_mlp[...] = rest[3:5]
            d_b_down[...] = rest[5:7]
            d_b_act[...] = rest[7:8].reshape(D)
            for layer in range(LAYERS):
                d_b_up[layer : layer + 1, 0:128] = rest[9 + 2 * layer : 10 + 2 * layer]
                d_b_up[layer : layer + 1, 128:256] = rest[10 + 2 * layer : 11 + 2 * layer]
            summed = jnp.sum(fin[at + 352 : at + 368, :].astype(F32)[8:9], axis=1, keepdims=True)
            masked_loss[...] = jnp.broadcast_to(summed / entries, (1, D)).reshape(D)
            hand_over(1, 3, 4, 5, 6, 7, 8, 11, 13, 15, 16, 17)

    def all_left(*slots):
        for send_slot in slots:
            left(send_slot)

    apart(all_left, *range(len(CHUNKS), len(halves) + 1))
    for chunk in range(len(CHUNKS)):
        apart(finish, chunk)
        apart(all_left, chunk)
    for place in range(count):
        pltpu.make_async_copy(staged[place], results[place], in_sem.at[place]).wait()


def copy_kernel(*refs):
    count = len(refs) // 2
    sem = refs[-1]
    copies = [
        pltpu.make_async_copy(refs[at], refs[count + at], sem.at[at]) for at in range(count)
    ]
    for copy in copies:
        copy.start()
    for copy in copies:
        copy.wait()


def on_device(radices, *args):
    (
        tokens,
        stem_norm,
        stem_latent,
        stem_wq,
        stem_wkv,
        stem_wo,
        norm_attn,
        w_qkv,
        w_out,
        norm_mlp,
        w_up,
        b_up,
        w_down,
        b_down,
        w_act,
        b_act,
        span_len,
        joint_mask,
        targets,
    ) = args
    own_seqs = targets.shape[0]
    count = own_seqs * SEQ_LEN
    rows = own_seqs * LAT
    last = len(radices)
    spread = sum(radices) - last
    vmem = pl.BlockSpec(memory_space=pltpu.VMEM)
    hbm = pl.BlockSpec(memory_space=pltpu.HBM)
    total_rows = sum(CHUNKS)
    wide = max(radices) - 1

    def summing(count_rows, dtype):
        pieces = count_rows // radices[0]
        return [
            *[pltpu.VMEM((count_rows, D), dtype)] * 4,
            pltpu.VMEM((wide, pieces, D), dtype),
            pltpu.VMEM((last - 1, pieces, D), dtype),
            pltpu.VMEM((last - 1, wide, pieces, D), dtype),
        ]

    n_recv = 8 + (1 + last) + len(CHUNKS) * (2 + last)
    shape = jax.ShapeDtypeStruct
    outs = [
        shape((own_seqs, AC), F32),
        shape((D,), F32),
        shape((count, D), F32),
        shape((D,), F32),
        shape((LAT, D), F32),
        shape((64, D), F32),
        shape((2, 64, D), F32),
        shape((64, D), F32),
        shape((LAYERS, D), F32),
        shape((LAYERS, 3, 64, D), F32),
        shape((LAYERS, 64, D), F32),
        shape((LAYERS, D), F32),
        shape((LAYERS, D, FF // 2), F32),
        shape((LAYERS, FF // 2), F32),
        shape((LAYERS, FF // 2, D), F32),
        shape((LAYERS, D), F32),
        shape((D, AC), F32),
        shape((AC,), F32),
    ]
    main = pl.pallas_call(
        functools.partial(main_kernel, radices),
        out_shape=outs,
        in_specs=[hbm] * len(args),
        out_specs=[pl.BlockSpec(memory_space=pl.ANY)] * len(outs),
        scratch_shapes=[
            *[pltpu.VMEM(out.shape, out.dtype) for out in outs],
            pltpu.VMEM((sum(CHUNKS), D), BF),
            pltpu.VMEM((count, D), BF),
            pltpu.VMEM((D,), BF),
            pltpu.VMEM((LAT, D), BF),
            pltpu.VMEM((2, 64, D), BF),
            pltpu.VMEM((2, 2, 64, D), BF),
            pltpu.VMEM((2, 64, D), BF),
            pltpu.VMEM((LAYERS, D), BF),
            pltpu.VMEM((2, LAYERS, 3, 64, D), BF),
            pltpu.VMEM((2, LAYERS, 64, D), BF),
            pltpu.VMEM((LAYERS, D), BF),
            pltpu.VMEM((2, LAYERS, D, FF // 2), BF),
            pltpu.VMEM((2, LAYERS, FF // 2), BF),
            pltpu.VMEM((2, LAYERS, FF // 2, D), BF),
            pltpu.VMEM((LAYERS, D), BF),
            pltpu.VMEM((D, AC), BF),
            pltpu.VMEM((AC,), BF),
            pltpu.SMEM((own_seqs,), jnp.int32),
            pltpu.VMEM((own_seqs, JOINTS), jnp.int32),
            pltpu.VMEM((own_seqs, AC), F32),
            pltpu.VMEM((count, 2 * D), BF),
            pltpu.VMEM((count, D), F32),
            pltpu.VMEM((D, count), BF),
            pltpu.VMEM((D, count), BF),
            pltpu.VMEM((40, D), F32),
            pltpu.VMEM((1 + last, 8, AC), F32),
            pltpu.VMEM((1 + spread, 8, AC), F32),
            *summing(total_rows, BF),
            pltpu.SemaphoreType.DMA((len(args),)),
            pltpu.SemaphoreType.DMA((9,)),
            pltpu.SemaphoreType.DMA((n_recv,)),
        ],
        compiler_params=pltpu.CompilerParams(
            collective_id=0, has_side_effects=True, vmem_limit_bytes=40 * 2**20
        ),
        name="stem_trunk_head",
    )(
        *[
            pltpu.with_memory_space_constraint(arg, pltpu.HBM)
            for arg in (
                tokens,
                stem_norm,
                stem_latent,
                jnp.transpose(stem_wq),
                jnp.transpose(stem_wkv, (0, 2, 1)),
                stem_wo,
                norm_attn,
                jnp.transpose(w_qkv, (0, 1, 3, 2)),
                w_out,
                norm_mlp,
                w_up,
                b_up,
                w_down,
                b_down,
                w_act,
                b_act,
                span_len,
                joint_mask,
                targets,
            )
        ]
    )
    result = pl.pallas_call(
        copy_kernel,
        out_shape=[pltpu.HBM(out.shape, out.dtype) for out in outs],
        in_specs=[vmem] * len(outs),
        out_specs=[hbm] * len(outs),
        scratch_shapes=[pltpu.SemaphoreType.DMA((len(outs),))],
        compiler_params=pltpu.CompilerParams(vmem_limit_bytes=8 * 2**20),
        name="copy_results",
    )(*main)
    result = list(result)
    result[1] = result[1][0]
    result[5] = jnp.transpose(result[5])
    result[6] = jnp.transpose(result[6], (0, 2, 1))
    result[9] = jnp.transpose(result[9], (0, 1, 3, 2))
    return tuple(result)


def solution(mesh):
    radices = radices_of(mesh.shape["dp"])
    in_specs = (
        P(("dp", "mp"), None),
        P(),
        P(),
        P(None, "mp"),
        P(None, None, "mp"),
        P("mp", None),
        P(),
        P(None, None, None, "mp"),
        P(None, "mp", None),
        P(),
        P(None, None, "mp"),
        P(None, "mp"),
        P(None, "mp", None),
        P(),
        P(),
        P(),
        P(("dp", "mp")),
        P(("dp", "mp"), None),
        P(("dp", "mp"), None),
    )
    out_specs = (
        P(("dp", "mp"), None),
        P(),
        P(("dp", "mp"), None),
        P(),
        P(),
        P(None, "mp"),
        P(None, None, "mp"),
        P("mp", None),
        P(),
        P(None, None, None, "mp"),
        P(None, "mp", None),
        P(),
        P(None, None, "mp"),
        P(None, "mp"),
        P(None, "mp", None),
        P(),
        P(),
        P(),
    )
    return jax.shard_map(
        functools.partial(on_device, radices),
        mesh=mesh,
        in_specs=in_specs,
        out_specs=out_specs,
        check_vma=False,
    )
```

time: 35.5 us -> 31.9 us (0.90)
  Pallas kernels: 34.7 us -> 31 us
    pallas_call x2, Pallas kernels: 34.7 us -> 31 us  [the longest x1 29.5 us: on_device(): pl.pallas_call(functools.partial(main_kernel, radices), out_shape=outs, i...]
where the time goes in v4:
time: 31.9 us; the launch traced here: 31.7 us
  Pallas kernels  31 us (97%)
  between operations  0.67 us (2%)
    pallas_call x1, Pallas kernels, on_device(): pl.pallas_call(functools.partial(main_kernel, radices), out_shape=outs, i...  29.5 us
    pallas_call x1, Pallas kernels, on_device(): pl.pallas_call(copy_kernel, out_shape=[pltpu.HBM(out.shape, out.dtype) fo...  1.49 us

profile of v4, /device:TPU:0, one launch (start us, length us, event | category | flops | bytes accessed | tf_op | source)
XLA Modules:
  0.0 31.7 jit_solution(8651582397150869889)
XLA Ops:
  0.7 29.5 %stem_trunk_head.1 = (f32[8,128]{1,0:T(8,128)S(1)}, f32[128]{0:T(128)S(1)}, f32[2048,128]{1,0:T(8,128)S(1)}, f32[128]{0:T(128)S(1)}, f32[16,128]{1,0:T(8,128)S(1...) custom-call(bf16[2048,128]{1,0:T(8,128)(2,1)} %tokens_h.1, ...), custom_call_target="tpu_custom_call" | custom-call | tf_op jit(solution)/shard_map/stem_trunk_head/pallas_call | solution.py:861
  30.2 1.5 %copy_results.1 = (f32[8,128]{1,0:T(8,128)}, f32[128]{0:T(128)}, f32[2048,128]{1,0:T(8,128)}, f32[128]{0:T(128)}, f32[16,128]{1,0:T(8,128)}, /*index=5*/f32[64,1...) custom-call(f32[8,128]{1,0:T(8,128)S(1)} %get-tuple-element.54.refs_, ...), custom_call_target="tpu_custom_call" | custom-call | tf_op jit(solution)/shard_map/copy_results/pallas_call | solution.py:930

commit v5 on v4

--- a/solution.py
+++ b/solution.py
@@ -25,7 +25,8 @@
 epsilon = 1e-05
 highest = lax.Precision.HIGHEST
 
-CHUNKS = (512, 256, 512, 256, 384)
+CHUNKS = (256, 256, 384, 512, 384, 128)
+DIRECT = (0, 5)
 
 
 def nn(left, right):
@@ -115,7 +116,6 @@
     *refs,
 ):
     count = 18
-    results, staged = refs[:count], refs[count : 2 * count]
     (
         actions,
         masked_loss,
@@ -135,7 +135,7 @@
         d_b_down,
         d_act_out,
         d_b_act,
-    ) = staged
+    ) = refs[:count]
     (
         fin,
         x_v,
@@ -169,12 +169,13 @@
         rcv,
         snd,
         rs_r,
+        direct_r,
         part,
         full_r,
         in_sem,
         send_sem,
         recv_sem,
-    ) = refs[2 * count :]
+    ) = refs[count:]
     dp, mp = lax.axis_index("dp"), lax.axis_index("mp")
     own_seqs = targets_h.shape[0]
     rows = own_seqs * LAT
@@ -195,6 +196,8 @@
 
     barrier = pltpu.get_barrier_semaphore()
     greeted = [core]
+    for offset in range(1, radices[0]):
+        greeted.append((partner(0, offset)[0], 1 - mp))
     for level, radix in enumerate(radices):
         greeted += [partner(level, offset) for offset in range(1, radix)]
     for device in greeted:
@@ -492,6 +495,10 @@
     first_row = [sum(CHUNKS[:chunk]) for chunk in range(len(CHUNKS))]
     first_piece = [begin // radices[0] for begin in first_row]
     live = {}
+    first_direct = {
+        chunk: sum(CHUNKS[before] for before in DIRECT[:at]) // radices[0]
+        for at, chunk in enumerate(DIRECT)
+    }
 
     def put(chunk, offset, mine, others):
         at = pl.ds(first_row[chunk] + offset, mine.shape[0])
@@ -501,6 +508,22 @@
     def core_send(chunk):
         at = pl.ds(first_row[chunk], CHUNKS[chunk])
         live[chunk] = group([(oth.at[at], rcv.at[at], core)], lambda: rcv.at[at], chunk)
+
+    def scatter_both(chunk):
+        size = CHUNKS[chunk] // radices[0]
+        at = pl.ds(first_row[chunk], CHUNKS[chunk])
+        here = pl.ds(first_direct[chunk], size)
+        copies = []
+        for offset in far_first(radices[0]) + [0]:
+            piece = pl.ds(piece_of[size][offset], size)
+            if offset:
+                device, across = partner(0, offset), (partner(0, offset)[0], 1 - mp)
+                copies.append((own.at[at].at[piece], direct_r.at[offset - 1, here], device))
+            else:
+                across = core
+            dst = direct_r.at[radices[0] - 1 + offset, here]
+            copies.append((oth.at[at].at[piece], dst, across))
+        live[chunk] = group(copies, lambda: direct_r.at[:, here], chunk)
 
     def received(chunk):
         live.pop(chunk)()
@@ -525,7 +548,12 @@
         received(chunk)
         size = CHUNKS[chunk] // radices[0]
         here = pl.ds(first_piece[chunk], size)
-        if level == 1:
+        if level == 1 and chunk in DIRECT:
+            whole = own.at[pl.ds(first_row[chunk], CHUNKS[chunk])]
+            mine = whole[pl.ds(piece_of[size][0], size), :].astype(F32)
+            there = pl.ds(first_direct[chunk], size)
+            got = [direct_r[at, there, :].astype(F32) for at in range(2 * radices[0] - 1)]
+        elif level == 1:
             whole = snd.at[pl.ds(first_row[chunk], CHUNKS[chunk])]
             mine = whole[pl.ds(piece_of[size][0], size), :].astype(F32)
             got = [rs_r[at, here, :].astype(F32) for at in range(radices[0] - 1)]
@@ -577,7 +605,10 @@
         d_up = tn(kv["rows_m"], d_upper)
         put(chunk, 0, d_up[:, 0:128], d_up[:, 256:384])
         put(chunk, 128, d_up[:, 128:256], d_up[:, 384:512])
-        put(chunk, 256, d_down[0:256], d_down[256:512])
+        if layer == 1:
+            put(chunk + 1, 0, d_down[0:256], d_down[256:512])
+        else:
+            put(chunk, 256, d_down[0:256], d_down[256:512])
         return d_middle
 
     def back_attn(d_middle, layer, chunk):
@@ -607,17 +638,19 @@
         return d_input
 
     upstream = back_mlp(upstream, 1, 0)
-    apart(core_send, 0)
+    apart(scatter_both, 0)
+    apart(core_send, 1)
     apart(entries_step, 1)
-    upstream = back_attn(upstream, 1, 1)
-    apart(core_send, 1)
-    upstream = back_mlp(upstream, 0, 2)
+    upstream = back_attn(upstream, 1, 2)
+    d_act = act_grad()
+    put(2, 256, d_act, d_act)
     apart(core_send, 2)
-    apart(scatter, 0)
-    upstream = back_attn(upstream, 0, 3)
+    upstream = back_mlp(upstream, 0, 3)
     apart(core_send, 3)
     apart(scatter, 1)
+    upstream = back_attn(upstream, 0, 4)
     apart(scatter, 2)
+    apart(scatter, 3)
 
     grad_stem = upstream.astype(BF)
     back_flat = nt(grad_stem, stem_mats)
@@ -631,6 +664,13 @@
         )
         for seq in range(own_seqs)
     ]
+    d_out_t = nt(stem_wo, grad_stem).astype(BF)
+    d_stem_wo = tn(stem_out, grad_stem)
+    put(4, 256, d_stem_wo[0:64], d_stem_wo[64:128])
+    d_wv = nn(heads_beside(d_out_t), jnp.concatenate(mixed_heads, axis=0))
+    put(4, 320, d_wv[0:64], d_wv[64:128])
+    apart(core_send, 4)
+
     gain_sum = jnp.zeros((D, D), F32)
     folds_v, d_all = [], []
     for seq, at in enumerate(seq_rows):
@@ -643,15 +683,8 @@
         weighted = probs * d_all[seq]
         inner = jnp.sum(weighted, axis=1, keepdims=True) * shares[seq][:, 0:1]
         ds_v[:, lanes] = (weighted - probs * inner).astype(BF)
-    d_out_t = nt(stem_wo, grad_stem).astype(BF)
-    d_stem_wo = tn(stem_out, grad_stem)
-    put(4, 0, d_stem_wo[0:64], d_stem_wo[64:128])
-    d_wv = nn(heads_beside(d_out_t), jnp.concatenate(mixed_heads, axis=0))
-    put(4, 64, d_wv[0:64], d_wv[64:128])
-    d_act = act_grad()
-    put(4, 128, d_act, d_act)
     d_fold = nn(ds_v[...], next_v[:, 0:D])
-    apart(scatter, 3)
+    apart(scatter, 4)
 
     d_fold_b = d_fold.astype(BF)
     d_wk = nn(q_diag.astype(F32).T.astype(BF), d_fold_b)
@@ -668,19 +701,15 @@
     small_v[29:32, :] = jnp.zeros((3, D), F32)
     shared = small_v[0:32, :]
     d_q_other = jnp.concatenate([d_q[:, 64:], d_q[:, :64]], axis=1)
-    put(4, 256, d_wk[0:64], d_wk[64:128])
-    put(4, 320, d_q, d_q_other)
-    put(4, 336, shared, shared)
+    put(5, 0, d_wk[0:64], d_wk[64:128])
+    put(5, 64, d_q, d_q_other)
+    put(5, 80, shared, shared)
     for layer in range(LAYERS):
         small_v[25 + 2 * layer : 27 + 2 * layer, :] = small_v[34 + 4 * layer : 36 + 4 * layer, :]
-    oth[first_row[4] + 352 : first_row[4] + 368, :] = small_v[16:32, :].astype(BF)
-    own[first_row[4] + 368 : first_row[4] + 384, :] = jnp.zeros((16, D), BF)
-    oth[first_row[4] + 368 : first_row[4] + 384, :] = jnp.zeros((16, D), BF)
-    apart(core_send, 4)
-
-    def hand_over(*places):
-        for place in places:
-            pltpu.make_async_copy(staged[place], results[place], in_sem.at[place]).start()
+    oth[first_row[5] + 96 : first_row[5] + 112, :] = small_v[16:32, :].astype(BF)
+    own[first_row[5] + 112 : first_row[5] + 128, :] = jnp.zeros((16, D), BF)
+    oth[first_row[5] + 112 : first_row[5] + 128, :] = jnp.zeros((16, D), BF)
+    apart(scatter_both, 5)
 
     fold_g = (fold * stem_gain).astype(BF)
     fold_side = jnp.concatenate([fold_g, nn(fold_g, mean_mat).astype(BF)], axis=1)
@@ -699,13 +728,14 @@
         grad_tokens[at, :] = inv_v[at, :] * (scaled - both_grads[:, D:] - unit * slope_mean)
 
     order = (
-        (2, scatter, 4),
-        (3, share_on, 0, 1),
-        (5, share_on, 1, 1),
-        (8, share_on, 2, 1),
+        (1, share_on, 0, 1),
+        (3, share_on, 1, 1),
+        (5, share_on, 2, 1),
         (8, share_on, 3, 1),
         (8, share_on, 4, 1),
         (8, share_on, 0, 2),
+        (8, share_on, 5, 1),
+        (8, share_on, 1, 2),
     )
     for seq in range(own_seqs):
         for place, *step in order:
@@ -723,8 +753,7 @@
     factor = total_seqs * AC / entries
     grad_tokens[...] = grad_tokens[...] * factor
 
-    apart(hand_over, 0, 2)
-    for chunk, level in ((1, 2), (2, 2), (3, 2), (4, 2)):
+    for chunk, level in ((2, 2), (3, 2), (4, 2), (5, 2)):
         apart(share_on, chunk, level)
     for level in range(3, last + 1):
         for chunk in range(len(CHUNKS)):
@@ -736,29 +765,30 @@
 
     def finish(chunk):
         received(chunk)
-        if chunk in (0, 2):
+        if chunk in (0, 3):
             layer = 1 if chunk == 0 else 0
             d_up_out[layer, :, 0:128] = whole(chunk, 0, 128)
             d_up_out[layer, :, 128:256] = whole(chunk, 128, 128)
-            d_down_out[layer] = whole(chunk, 256, 256)
-            if chunk == 2:
-                hand_over(12, 14)
-        if chunk in (1, 3):
-            layer = 1 if chunk == 1 else 0
+        if chunk == 1:
+            d_down_out[1] = whole(1, 0, 256)
+        if chunk == 3:
+            d_down_out[0] = whole(3, 256, 256)
+        if chunk in (2, 4):
+            layer = 1 if chunk == 2 else 0
             for place in range(3):
                 d_qkv_out[layer, place] = whole(chunk, 64 * place, 64)
             d_out_out[layer] = whole(chunk, 192, 64)
-            if chunk == 3:
-                hand_over(9, 10)
+        if chunk == 2:
+            d_act_out[...] = whole(2, 256, 128)
         if chunk == 4:
-            d_stem_wo_out[...] = whole(4, 0, 64)
-            d_stem_wkv[1] = whole(4, 64, 64)
-            d_act_out[...] = whole(4, 128, 128)
-            d_stem_wkv[0] = whole(4, 256, 64)
-            d_latent_out[...] = whole(4, 336, 16)
-            at = first_row[4]
-            d_stem_wq[...] = tn(fin[at + 320 : at + 336, 0:64], latent) * factor
-            rest = whole(4, 352, 16)
+            d_stem_wo_out[...] = whole(4, 256, 64)
+            d_stem_wkv[1] = whole(4, 320, 64)
+        if chunk == 5:
+            d_stem_wkv[0] = whole(5, 0, 64)
+            d_latent_out[...] = whole(5, 80, 16)
+            at = first_row[5]
+            d_stem_wq[...] = tn(fin[at + 64 : at + 80, 0:64], latent) * factor
+            rest = whole(5, 96, 16)
             d_stem_norm[...] = rest[0:1].reshape(D)
             d_norm_attn[...] = rest[1:3]
             d_norm_mlp[...] = rest[3:5]
@@ -767,9 +797,8 @@
             for layer in range(LAYERS):
                 d_b_up[layer : layer + 1, 0:128] = rest[9 + 2 * layer : 10 + 2 * layer]
                 d_b_up[layer : layer + 1, 128:256] = rest[10 + 2 * layer : 11 + 2 * layer]
-            summed = jnp.sum(fin[at + 352 : at + 368, :].astype(F32)[8:9], axis=1, keepdims=True)
+            summed = jnp.sum(fin[at + 96 : at + 112, :].astype(F32)[8:9], axis=1, keepdims=True)
             masked_loss[...] = jnp.broadcast_to(summed / entries, (1, D)).reshape(D)
-            hand_over(1, 3, 4, 5, 6, 7, 8, 11, 13, 15, 16, 17)
 
     def all_left(*slots):
         for send_slot in slots:
@@ -779,8 +808,6 @@
     for chunk in range(len(CHUNKS)):
         apart(finish, chunk)
         apart(all_left, chunk)
-    for place in range(count):
-        pltpu.make_async_copy(staged[place], results[place], in_sem.at[place]).wait()
 
 
 def copy_kernel(*refs):
@@ -829,9 +856,11 @@
 
     def summing(count_rows, dtype):
         pieces = count_rows // radices[0]
+        direct_pieces = sum(CHUNKS[chunk] for chunk in DIRECT) // radices[0]
         return [
             *[pltpu.VMEM((count_rows, D), dtype)] * 4,
             pltpu.VMEM((wide, pieces, D), dtype),
+            pltpu.VMEM((2 * radices[0] - 1, direct_pieces, D), dtype),
             pltpu.VMEM((last - 1, pieces, D), dtype),
             pltpu.VMEM((last - 1, wide, pieces, D), dtype),
         ]
@@ -862,9 +891,8 @@
         functools.partial(main_kernel, radices),
         out_shape=outs,
         in_specs=[hbm] * len(args),
-        out_specs=[pl.BlockSpec(memory_space=pl.ANY)] * len(outs),
+        out_specs=[vmem] * len(outs),
         scratch_shapes=[
-            *[pltpu.VMEM(out.shape, out.dtype) for out in outs],
             pltpu.VMEM((sum(CHUNKS), D), BF),
             pltpu.VMEM((count, D), BF),
             pltpu.VMEM((D,), BF),

time: 31.9 us -> 31.3 us (0.981)
  Pallas kernels: 31 us -> 30.5 us
    pallas_call x1, Pallas kernels: 29.5 us -> 29 us  [on_device(): pl.pallas_call(functools.partial(main_kernel, radices), out_shape=outs, i...]
where the time goes in v5:
time: 31.3 us; the launch traced here: 31.2 us
  Pallas kernels  30.5 us (97%)
  between operations  0.67 us (2%)
    pallas_call x1, Pallas kernels, on_device(): pl.pallas_call(functools.partial(main_kernel, radices), out_shape=outs, i...  29 us
    pallas_call x1, Pallas kernels, on_device(): pl.pallas_call(copy_kernel, out_shape=[pltpu.HBM(out.shape, out.dtype) fo...  1.49 us

profile of v5, /device:TPU:0, one launch (start us, length us, event | category | flops | bytes accessed | tf_op | source)
XLA Modules:
  0.0 31.2 jit_solution(14789518298912176532)
XLA Ops:
  0.7 29.0 %stem_trunk_head.1 = (f32[8,128]{1,0:T(8,128)S(1)}, f32[128]{0:T(128)S(1)}, f32[2048,128]{1,0:T(8,128)S(1)}, f32[128]{0:T(128)S(1)}, f32[16,128]{1,0:T(8,128)S(1...) custom-call(bf16[2048,128]{1,0:T(8,128)(2,1)} %tokens_h.1, ...), custom_call_target="tpu_custom_call" | custom-call | tf_op jit(solution)/shard_map/stem_trunk_head/pallas_call | solution.py:890
  29.7 1.5 %copy_results.1 = (f32[8,128]{1,0:T(8,128)}, f32[128]{0:T(128)}, f32[2048,128]{1,0:T(8,128)}, f32[128]{0:T(128)}, f32[16,128]{1,0:T(8,128)}, /*index=5*/f32[64,1...) custom-call(f32[8,128]{1,0:T(8,128)S(1)} %get-tuple-element.54.refs_, ...), custom_call_target="tpu_custom_call" | custom-call | tf_op jit(solution)/shard_map/copy_results/pallas_call | solution.py:958

commit v6 on v5

--- a/solution.py
+++ b/solution.py
@@ -175,6 +175,7 @@
         in_sem,
         send_sem,
         recv_sem,
+        meet_sem,
     ) = refs[count:]
     dp, mp = lax.axis_index("dp"), lax.axis_index("mp")
     own_seqs = targets_h.shape[0]
@@ -195,11 +196,14 @@
         pl.when(dp >= 0)(functools.partial(step, *given))
 
     barrier = pltpu.get_barrier_semaphore()
-    greeted = [core]
-    for offset in range(1, radices[0]):
-        greeted.append((partner(0, offset)[0], 1 - mp))
+    bits = [
+        (level, bit) for level, radix in enumerate(radices) for bit in (1, 2, 4) if bit < radix
+    ]
+    greeted = [core] + [partner(level, bit) for level, bit in bits]
+    passing = [core] + [partner(level, bit) for level, bit in bits if radices[level] > 2]
     for level, radix in enumerate(radices):
-        greeted += [partner(level, offset) for offset in range(1, radix)]
+        for offset in range(1, radix):
+            partner(level, offset)
     for device in greeted:
         pl.semaphore_signal(barrier, inc=1, device_id=device, device_id_type=MESH)
 
@@ -265,6 +269,8 @@
 
     for place, (name, src, dst) in enumerate(pairs):
         local[name] = functools.partial(load, place, name, src, dst)
+    at_once = ("tokens", "span", "joint", "stem_norm", "stem_latent", "wq", "wkv", "wo")
+    for name in at_once:
         local[name]().start()
 
     head_mask = (
@@ -313,13 +319,30 @@
         for name in names:
             gathered[name]()
 
+    def gather(*names):
+        for name, _, dst in pairs:
+            if name in names:
+                local[name]().wait()
+                copies = [(dst.at[0], dst.at[1], core)]
+                extent = functools.partial(dst.at.__getitem__, 1)
+                gathered[name] = group(copies, extent, halves.index(name))
+
+    def pass_on(turn):
+        if turn:
+            pl.semaphore_wait(meet_sem.at[turn - 1], len(passing))
+        if turn < 3:
+            for device in passing:
+                pl.semaphore_signal(
+                    meet_sem.at[turn], inc=1, device_id=device, device_id_type=MESH
+                )
+
     def meet():
         pl.semaphore_wait(barrier, len(greeted))
-        for name, src, dst in pairs:
-            if name in halves:
-                copies = [(src, dst.at[1], core)]
-                extent = functools.partial(dst.at.__getitem__, 1)
-                gathered[name] = group(copies, extent, halves.index(name))
+        pass_on(0)
+        gather("wq", "wkv", "wo")
+        for name in local:
+            if name not in at_once:
+                local[name]().start()
 
     apart(meet)
 
@@ -367,8 +390,8 @@
     def lanes_beside(cube):
         return jnp.concatenate([cube[head] for head in range(HEADS)], axis=1)
 
-    apart(wait_for, "stem_latent", "wq", "wkv")
-    apart(wait_for, "wo")
+    apart(gather, "wqkv", "wout")
+    apart(wait_for, "stem_latent")
     apart(wait_gathered, "wq", "wkv", "wo")
     latent = stem_latent_v[...]
     wq_t = both(wq_v)
@@ -377,13 +400,13 @@
     q_diag = (jnp.concatenate([stem_q] * HEADS, axis=0) * diag_heads).astype(BF)
     fold = nn(q_diag, wk_t)
     fold_b = fold.astype(BF)
-    apart(entries_step, 0)
+    apart(gather, "wup", "wdn", "bup")
     seq_rows = [pl.ds(seq * SEQ_LEN, SEQ_LEN) for seq in range(own_seqs)]
     scores = [nt(fold_b, next_v[at, 0:D]) for at in seq_rows]
     apart_wo = both(wo_v)
     wv_cols = wv_t.T
     stem_mats = nn(heads_below(wv_cols), apart_wo).astype(BF)
-    mixed, shares = [], []
+    mixed, shares, sums = [], [], []
     for seq, at in enumerate(seq_rows):
         tops = jnp.max(scores[seq], axis=1, keepdims=True)
         probs = jnp.exp(scores[seq] - tops).astype(BF)
@@ -391,6 +414,7 @@
         both_sums = nn(probs, next_v[at, :])
         share = 1.0 / both_sums[:, D:]
         shares.append(share)
+        sums.append(both_sums[:, :D])
         mixed.append((both_sums[:, :D] * share).astype(BF))
 
     def by_head(head):
@@ -409,12 +433,11 @@
 
 
     apart(wait_for, "norm_attn", "norm_mlp", "b_down", "w_act", "b_act", "targets")
-    apart(wait_for, "wqkv", "wout", "wup", "wdn", "bup")
-    apart(wait_gathered, "wqkv", "wout", "wup", "wdn", "bup")
+    apart(wait_gathered, "wqkv", "wout")
+    apart(pass_on, 1)
     gain_attn = norm_attn_v[...].astype(F32)
     gain_mlp = norm_mlp_v[...].astype(F32)
     down_bias = b_down_v[...].astype(F32)
-    up_bias = jnp.concatenate([bup_v[0], bup_v[1]], axis=1).astype(F32)
 
     def row_blocks_beside(matrix):
         return jnp.concatenate([matrix[head * D : (head + 1) * D] for head in range(HEADS)], axis=1)
@@ -429,8 +452,6 @@
         qkv = jnp.concatenate([both(wqkv_v, layer, part_at) for part_at in range(3)], axis=0)
         out_mat = both(wout_v, layer)
         out_mats = nn(heads_below(out_mat.T), qkv[2 * D :]).astype(BF)
-        up_mat = jnp.concatenate([wup_v[0, layer], wup_v[1, layer]], axis=1)
-        down_mat = both(wdn_v, layer)
         normed, unit_a, inv_a = norm_rows(residual, gain_a)
         rows_a = normed.astype(BF)
         flat = nt(rows_a, qkv).astype(BF)
@@ -445,6 +466,11 @@
         middle = residual + nn(moved_t, probs_flat).T
         keys_t = nt(qkv[D : 2 * D], rows_a).astype(BF) * jnp.asarray(HD ** (-0.5), BF)
         values_t = nt(qkv[2 * D :], rows_a).astype(BF)
+        if layer == 0:
+            apart(wait_gathered, "wup", "wdn", "bup")
+        up_mat = jnp.concatenate([wup_v[0, layer], wup_v[1, layer]], axis=1)
+        down_mat = both(wdn_v, layer)
+        up_bias = jnp.concatenate([bup_v[0], bup_v[1]], axis=1).astype(F32)
         normed_m, unit_m, inv_m = norm_rows(middle, gain_m)
         rows_m = normed_m.astype(BF)
         up_rows = nn(rows_m, up_mat) + up_bias[layer : layer + 1]
@@ -466,6 +492,8 @@
     for layer in range(LAYERS):
         hidden, saved = trunk_forward(hidden, layer)
         kept.append(saved)
+        if layer == 0:
+            apart(pass_on, 2)
         if layer == 0:
             stem_out = stem_heads_out()
 
@@ -637,10 +665,11 @@
         put(chunk, 192, d_out[0:64], d_out[64:128])
         return d_input
 
+    apart(pass_on, 3)
+    apart(entries_step, 0)
     upstream = back_mlp(upstream, 1, 0)
     apart(scatter_both, 0)
     apart(core_send, 1)
-    apart(entries_step, 1)
     upstream = back_attn(upstream, 1, 2)
     d_act = act_grad()
     put(2, 256, d_act, d_act)
@@ -650,7 +679,6 @@
     apart(scatter, 1)
     upstream = back_attn(upstream, 0, 4)
     apart(scatter, 2)
-    apart(scatter, 3)
 
     grad_stem = upstream.astype(BF)
     back_flat = nt(grad_stem, stem_mats)
@@ -670,19 +698,20 @@
     d_wv = nn(heads_beside(d_out_t), jnp.concatenate(mixed_heads, axis=0))
     put(4, 320, d_wv[0:64], d_wv[64:128])
     apart(core_send, 4)
+    apart(scatter, 3)
 
     gain_sum = jnp.zeros((D, D), F32)
-    folds_v, d_all = [], []
+    folds_v, inners = [], []
+    for seq in range(own_seqs):
+        gain_sum += back_v[seq] * mixed[seq].astype(F32)
+        folded = (back_v[seq] * shares[seq]).astype(BF)
+        folds_v.append(folded)
+        inner = jnp.sum(folded.astype(F32) * sums[seq], axis=1, keepdims=True)
+        inners.append(inner * shares[seq][:, 0:1])
     for seq, at in enumerate(seq_rows):
-        gain_sum += back_v[seq] * mixed[seq].astype(F32)
-        folds_v.append((back_v[seq] * shares[seq]).astype(BF))
-        d_all.append(nt(folds_v[seq], next_v[at, 0:D]))
-    for seq in range(own_seqs):
         lanes = slice(seq * SEQ_LEN, (seq + 1) * SEQ_LEN)
-        probs = e_v[:, lanes].astype(F32)
-        weighted = probs * d_all[seq]
-        inner = jnp.sum(weighted, axis=1, keepdims=True) * shares[seq][:, 0:1]
-        ds_v[:, lanes] = (weighted - probs * inner).astype(BF)
+        d_probs = nt(folds_v[seq], next_v[at, 0:D])
+        ds_v[:, lanes] = (e_v[:, lanes].astype(F32) * (d_probs - inners[seq])).astype(BF)
     d_fold = nn(ds_v[...], next_v[:, 0:D])
     apart(scatter, 4)
 
@@ -710,6 +739,7 @@
     own[first_row[5] + 112 : first_row[5] + 128, :] = jnp.zeros((16, D), BF)
     oth[first_row[5] + 112 : first_row[5] + 128, :] = jnp.zeros((16, D), BF)
     apart(scatter_both, 5)
+    apart(entries_step, 1)
 
     fold_g = (fold * stem_gain).astype(BF)
     fold_side = jnp.concatenate([fold_g, nn(fold_g, mean_mat).astype(BF)], axis=1)
@@ -732,8 +762,8 @@
         (3, share_on, 1, 1),
         (5, share_on, 2, 1),
         (8, share_on, 3, 1),
+        (8, share_on, 0, 2),
         (8, share_on, 4, 1),
-        (8, share_on, 0, 2),
         (8, share_on, 5, 1),
         (8, share_on, 1, 2),
     )
@@ -924,6 +954,7 @@
             pltpu.SemaphoreType.DMA((len(args),)),
             pltpu.SemaphoreType.DMA((9,)),
             pltpu.SemaphoreType.DMA((n_recv,)),
+            pltpu.SemaphoreType.REGULAR((3,)),
         ],
         compiler_params=pltpu.CompilerParams(
             collective_id=0, has_side_effects=True, vmem_limit_bytes=40 * 2**20

time: 31.3 us -> 31.1 us (level)
  no operation moved by 1% of the time
where the time goes in v6:
time: 31.1 us; the launch traced here: 30.9 us
  Pallas kernels  30.2 us (97%)
  between operations  0.67 us (2%)
    pallas_call x1, Pallas kernels, on_device(): pl.pallas_call(functools.partial(main_kernel, radices), out_shape=outs, i...  28.7 us
    pallas_call x1, Pallas kernels, on_device(): pl.pallas_call(copy_kernel, out_shape=[pltpu.HBM(out.shape, out.dtype) fo...  1.49 us

profile of v6, /device:TPU:0, one launch (start us, length us, event | category | flops | bytes accessed | tf_op | source)
XLA Modules:
  0.0 30.9 jit_solution(11799439547932185026)
XLA Ops:
  0.7 28.7 %stem_trunk_head.1 = (f32[8,128]{1,0:T(8,128)S(1)}, f32[128]{0:T(128)S(1)}, f32[2048,128]{1,0:T(8,128)S(1)}, f32[128]{0:T(128)S(1)}, f32[16,128]{1,0:T(8,128)S(1...) custom-call(bf16[2048,128]{1,0:T(8,128)(2,1)} %tokens_h.1, ...), custom_call_target="tpu_custom_call" | custom-call | tf_op jit(solution)/shard_map/stem_trunk_head/pallas_call | solution.py:920
  29.4 1.5 %copy_results.1 = (f32[8,128]{1,0:T(8,128)}, f32[128]{0:T(128)}, f32[2048,128]{1,0:T(8,128)}, f32[128]{0:T(128)}, f32[16,128]{1,0:T(8,128)}, /*index=5*/f32[64,1...) custom-call(f32[8,128]{1,0:T(8,128)S(1)} %get-tuple-element.54.refs_, ...), custom_call_target="tpu_custom_call" | custom-call | tf_op jit(solution)/shard_map/copy_results/pallas_call | solution.py:989

commit v7 on v6

--- a/solution.py
+++ b/solution.py
@@ -196,16 +196,33 @@
         pl.when(dp >= 0)(functools.partial(step, *given))
 
     barrier = pltpu.get_barrier_semaphore()
+    count_below = math.prod(radices[:-1])
     bits = [
         (level, bit) for level, radix in enumerate(radices) for bit in (1, 2, 4) if bit < radix
     ]
-    greeted = [core] + [partner(level, bit) for level, bit in bits]
-    passing = [core] + [partner(level, bit) for level, bit in bits if radices[level] > 2]
+    greeted = [core] + [partner(level, bit) for level, bit in bits if radices[level] > 2]
+    split = len(radices) > 1 and radices[-1] == 2
+    if split:
+        low = (dp // (count_below // 2)) % 2
+        high = dp // count_below
+        inner = (low + high) % 2
+        across = (dp + (1 - 2 * high) * count_below + (1 - 2 * low) * (count_below // 2), mp)
+    else:
+        inner = 0
+
+    def signal_all(semaphore):
+        for device in greeted:
+            pl.semaphore_signal(semaphore, inc=1, device_id=device, device_id_type=MESH)
+        if split:
+
+            @pl.when(inner == 1)
+            def _():
+                pl.semaphore_signal(semaphore, inc=1, device_id=across, device_id_type=MESH)
+
     for level, radix in enumerate(radices):
         for offset in range(1, radix):
             partner(level, offset)
-    for device in greeted:
-        pl.semaphore_signal(barrier, inc=1, device_id=device, device_id_type=MESH)
+    signal_all(barrier)
 
     piece_of = {}
     for size in sorted({chunk // radices[0] for chunk in CHUNKS}):
@@ -329,15 +346,12 @@
 
     def pass_on(turn):
         if turn:
-            pl.semaphore_wait(meet_sem.at[turn - 1], len(passing))
+            pl.semaphore_wait(meet_sem.at[turn - 1], len(greeted) + inner)
         if turn < 3:
-            for device in passing:
-                pl.semaphore_signal(
-                    meet_sem.at[turn], inc=1, device_id=device, device_id_type=MESH
-                )
+            signal_all(meet_sem.at[turn])
 
     def meet():
-        pl.semaphore_wait(barrier, len(greeted))
+        pl.semaphore_wait(barrier, len(greeted) + inner)
         pass_on(0)
         gather("wq", "wkv", "wo")
         for name in local:

time: 31.1 us -> 31 us (level)
  no operation moved by 1% of the time
where the time goes in v7:
time: 31 us; the launch traced here: 30.8 us
  Pallas kernels  30.2 us (97%)
  between operations  0.67 us (2%)
    pallas_call x1, Pallas kernels, on_device(): pl.pallas_call(functools.partial(main_kernel, radices), out_shape=outs, i...  28.7 us
    pallas_call x1, Pallas kernels, on_device(): pl.pallas_call(copy_kernel, out_shape=[pltpu.HBM(out.shape, out.dtype) fo...  1.49 us

profile of v7, /device:TPU:0, one launch (start us, length us, event | category | flops | bytes accessed | tf_op | source)
XLA Modules:
  0.0 30.8 jit_solution(5171155120194925306)
XLA Ops:
  0.7 28.7 %stem_trunk_head.1 = (f32[8,128]{1,0:T(8,128)S(1)}, f32[128]{0:T(128)S(1)}, f32[2048,128]{1,0:T(8,128)S(1)}, f32[128]{0:T(128)S(1)}, f32[16,128]{1,0:T(8,128)S(1...) custom-call(bf16[2048,128]{1,0:T(8,128)(2,1)} %tokens_h.1, ...), custom_call_target="tpu_custom_call" | custom-call | tf_op jit(solution)/shard_map/stem_trunk_head/pallas_call | solution.py:934
  29.3 1.5 %copy_results.1 = (f32[8,128]{1,0:T(8,128)}, f32[128]{0:T(128)}, f32[2048,128]{1,0:T(8,128)}, f32[128]{0:T(128)}, f32[16,128]{1,0:T(8,128)}, /*index=5*/f32[64,1...) custom-call(f32[8,128]{1,0:T(8,128)S(1)} %get-tuple-element.54.refs_, ...), custom_call_target="tpu_custom_call" | custom-call | tf_op jit(solution)/shard_map/copy_results/pallas_call | solution.py:1003
